TPU v7x, 256 devices: a whole 4x4x8 slice. The times are simulated.
256 devices in a mesh: sx: 8 (over x, z_lo), sy: 32 (over y, z_hi, core).
Axes of the slice: x: 4, y: 4, z: 8 (z_hi: 4, z_lo: 2; z = z_hi * 2 + z_lo), core: 2. Of those that a mesh axis runs over, the one named last changes fastest.
Arguments:
- coarse_vectors: bfloat16 [3, 64, 72, 288, 64], P(None, None, 'sx', 'sy'), may hold values from -0.032 to 0.032
- stiffness: float32 [40, 160, 64], P('sx', 'sy'), may hold values from 0.3 to 3
- vector_counts: int32 [8, 32], P('sx', 'sy'), may hold values from 32 to 64, as said below
Outputs:
- coarse_rows: float32 [8, 32, 9, 64, 64], P('sx')
Inputs may be any that keep to these rules, and one draw needn't show every extreme that they name: vector_counts[r, c] vectors of subdomain (r, c) are used; some subdomain uses all 64.
All inputs are finite; a program needn't handle non-finite values.
Results may differ from a plain program's by a relative error of at most 0.0003.
Values may be sent and summed in bfloat16 or wider, within the bound.
No kernel may reach another device: no remote copies, remote signals or barrier semaphores. Data moves between devices by JAX's collectives and lax.ppermute only.
A program may use at most 192 MiB of HBM per device.

v0:
```python
import jax
import jax.numpy as jnp
from jax import lax
from jax.sharding import PartitionSpec as P

MARGIN = 2
CX = 5
CY = 5


MASS = 0.5


def padded_2(x, sides, width):
    for axis, dim in sides:
        peers, length = (lax.axis_size(axis), x.shape[dim])
        up = [(i, (i + 1) % peers) for i in range(peers - 1)]
        down = [(j, i) for i, j in up]
        last = lax.slice_in_dim(x, length - width, length, axis=dim)
        initial = lax.slice_in_dim(x, 0, width, axis=dim)
        before = lax.ppermute(last, axis, up)
        after = lax.ppermute(initial, axis, down)
        x = jnp.concatenate([before, x, after], axis=dim)
    return x


def inside_line(first_cell, length, extent_all):
    places = first_cell + jnp.arange(length, dtype=jnp.int32)
    return ((places >= 0) & (places < extent_all)).astype(jnp.float32)


def edge_weights(stiff_rim, inside):
    stiff_in = stiff_rim * inside
    weight_x = 0.5 * (stiff_in[1:] + stiff_in[:-1]) * inside[1:] * inside[:-1]
    weight_y = 0.5 * (stiff_in[:, 1:] + stiff_in[:, :-1]) * inside[:, 1:] * inside[:, :-1]
    weight_z = 0.5 * (stiff_in[:, :, 1:] + stiff_in[:, :, :-1])
    return (weight_x, weight_y, weight_z)


def apply_component(padded_field, weights, component):
    weight_x, weight_y, weight_z = weights
    flux_x = weight_x * (padded_field[:, 1:] - padded_field[:, :-1])
    term_x = jnp.pad(flux_x, ((0, 0), (1, 0), (0, 0), (0, 0))) - jnp.pad(
        flux_x, ((0, 0), (0, 1), (0, 0), (0, 0))
    )
    flux_y = weight_y * (padded_field[:, :, 1:] - padded_field[:, :, :-1])
    term_y = jnp.pad(flux_y, ((0, 0), (0, 0), (1, 0), (0, 0))) - jnp.pad(
        flux_y, ((0, 0), (0, 0), (0, 1), (0, 0))
    )
    flux_z = weight_z * (padded_field[:, :, :, 1:] - padded_field[:, :, :, :-1])
    term_z = jnp.pad(flux_z, ((0, 0), (0, 0), (0, 0), (1, 0))) - jnp.pad(
        flux_z, ((0, 0), (0, 0), (0, 0), (0, 1))
    )
    factors = [1.0 + 2.0 * float(component == axis_number) for axis_number in range(3)]
    return MASS * padded_field + factors[0] * term_x + factors[1] * term_y + factors[2] * term_z


def frame_span(step, extent, strip_width):
    if step < 0:
        return (0, strip_width)
    if step == 0:
        return (1, extent + 1)
    return (extent + 2 - strip_width, extent + 2)


def halo_span(step, extent, strip_width):
    if step < 0:
        return (0, strip_width)
    if step == 0:
        return (strip_width, strip_width + extent)
    return (strip_width + extent, extent + 2 * strip_width)


def contract(applied, piece):
    return jnp.einsum(
        "kxyz,lxyz->kl",
        applied,
        piece.astype(jnp.float32),
        precision=lax.Precision.HIGHEST,
        preferred_element_type=jnp.float32,
    )


def body(coarse_vectors, stiffness, vector_counts):
    vector_total = coarse_vectors.shape[1]
    ext_x = coarse_vectors.shape[2]
    ext_y = coarse_vectors.shape[3]
    strip_width = 2 * MARGIN + 1
    row_index = lax.axis_index("sx")
    col_index = lax.axis_index("sy")
    cells_x = CX * lax.axis_size("sx")
    cells_y = CY * lax.axis_size("sy")
    keep_rows = (jnp.arange(vector_total, dtype=jnp.int32) < vector_counts[0, 0]).astype(
        jnp.float32
    )
    in_x = inside_line(row_index * CX - MARGIN, ext_x, cells_x)
    in_y = inside_line(col_index * CY - MARGIN, ext_y, cells_y)
    cell_mask = keep_rows[:, None, None] * in_x[None, :, None] * in_y[None, None, :]
    masked = coarse_vectors * cell_mask.astype(jnp.bfloat16)[None, :, :, :, None]
    stiff_rim = padded_2(stiffness, (("sx", 0), ("sy", 1)), MARGIN + 1)
    inside = (
        inside_line(row_index * CX - MARGIN - 1, ext_x + 2, cells_x)[:, None, None]
        * inside_line(col_index * CY - MARGIN - 1, ext_y + 2, cells_y)[None, :, None]
    )
    weights = edge_weights(stiff_rim, inside)
    padded = padded_2(masked, (("sx", 2), ("sy", 3)), strip_width)
    pieces = {}
    for step_x in (-1, 0, 1):
        for step_y in (-1, 0, 1):
            part_x = halo_span(step_x, ext_x, strip_width)
            part_y = halo_span(step_y, ext_y, strip_width)
            pieces[step_x, step_y] = padded[:, :, part_x[0] : part_x[1], part_y[0] : part_y[1]]
    blocks = {offset: jnp.zeros((vector_total, vector_total), jnp.float32) for offset in pieces}
    for component in range(3):
        padded_field = jnp.pad(
            masked[component].astype(jnp.float32), ((0, 0), (1, 1), (1, 1), (0, 0))
        )
        applied = apply_component(padded_field, weights, component)
        for offset in pieces:
            span_x = frame_span(offset[0], ext_x, strip_width)
            span_y = frame_span(offset[1], ext_y, strip_width)
            blocks[offset] = blocks[offset] + contract(
                applied[:, span_x[0] : span_x[1], span_y[0] : span_y[1]], pieces[offset][component]
            )
    ordered = jnp.stack([blocks[step_x, step_y] for step_x in (-1, 0, 1) for step_y in (-1, 0, 1)])
    return lax.all_gather(ordered[None, None], "sy", axis=1, tiled=True)


def solution(mesh):
    return jax.shard_map(
        body,
        mesh=mesh,
        in_specs=(P(None, None, "sx", "sy", None), P("sx", "sy", None), P("sx", "sy")),
        out_specs=P("sx", None, None, None, None),
        check_vma=False,
    )
```

profile of v0, /device:TPU:11, one launch (start us, length us, event | category | flops | bytes accessed | tf_op | source)
XLA Modules:
  0.0 413.6 jit_solution(4537436991311946608)
XLA Ops:
  7.3 3.5 collective-permute-start
  10.9 2.6 collective-permute-start.1
  14.4 2.8 broadcast_multiply_fusion
  17.1 3.4 fusion.53
  20.5 2.6 collective-permute-start.5
  23.1 2.7 collective-permute-start.4
  25.8 2.0 slice_bitcast_fusion.2
  29.7 3.7 collective-permute-start.3
  33.4 5.2 %collective-permute-start.2 = (f32[11,3,64]{2,1,0:T(4,128)S(1)}, f32[11,3,64]{2,1,0:T(4,128)S(1)}, u32[]{:S(2)}, u32[]{:S(2)}) collective-permute-start(f32[11,3,64]{2,1,0:T(4,128)S(1)} %get-tuple-element.21), channel_id=1, source_target_pairs={{0,1},{1,2},{2,3},{3,4},{4,5},{5,6},{6,7},{7,8},{8,9},{9,10},{10,1... | collective-permute-start | bytes 25352 | tf_op jit(solution)/shard_map/ppermute | solution.py:21
  39.1 78.5 %collective-permute-done.2 = f32[11,3,64]{2,1,0:T(4,128)S(1)} collective-permute-done((f32[11,3,64]{2,1,0:T(4,128)S(1)}, f32[11,3,64]{2,1,0:T(4,128)S(1)}, u32[]{:S(2)}, u32[]{:S(2)}) %collective-permute-start.2) | collective-permute-done | bytes 8480 | tf_op jit(solution)/shard_map/ppermute | solution.py:21
  117.9 5.4 %fusion.7 = (f32[64,11,10,64]{3,0,2,1:T(8,128)}, f32[64,11,10,64]{3,0,2,1:T(8,128)}, f32[64,11,10,64]{3,0,2,1:T(8,128)}) fusion(f32[64,11,11,64]{3,0,2,1:T(8,128)S(1)} %pad_convert_fusion.2, f32[11,10,64]{2,1,0:T(8,128)S(1)} %fusion.47, f32[64,11,11,64]{3,0,2,1:T(8,128)S(1)} %pad_convert_fusion.1, f32[64,11,11,64]{3,0,2,1:T(8,128)S(1)} %pad_convert_fusion), kind=kLoop, calls=%fused_computation.19 | loop fusion | flops 2703360 | bytes 16248320 | tf_op jit(solution)/shard_map/mul | solution.py:46
  123.3 4.8 %fusion.8 = (f32[64,10,11,64]{3,0,2,1:T(8,128)}, f32[64,10,11,64]{3,0,2,1:T(8,128)}, f32[64,10,11,64]{3,0,2,1:T(8,128)}) fusion(f32[64,11,11,64]{3,0,2,1:T(8,128)S(1)} %pad_convert_fusion.2, f32[10,11,64]{2,1,0:T(8,128)S(1)} %fusion.49, f32[64,11,11,64]{3,0,2,1:T(8,128)S(1)} %pad_convert_fusion.1, f32[64,11,11,64]{3,0,2,1:T(8,128)S(1)} %pad_convert_fusion), kind=kLoop, calls=%fused_computation.21 | loop fusion | flops 2703360 | bytes 16248320 | tf_op jit(solution)/shard_map/mul | solution.py:42
  128.1 6.0 %fusion.2 = (f32[64,11,11,63]{3,0,2,1:T(8,128)}, f32[64,11,11,63]{3,0,2,1:T(8,128)}, f32[64,11,11,63]{3,0,2,1:T(8,128)}) fusion(f32[64,11,11,64]{3,0,2,1:T(8,128)S(1)} %pad_convert_fusion.2, f32[11,11,63]{2,1,0:T(8,128)S(1)} %fusion.45, f32[64,11,11,64]{3,0,2,1:T(8,128)S(1)} %pad_convert_fusion.1, f32[64,11,11,64]{3,0,2,1:T(8,128)S(1)} %pad_convert_fusion), kind=kLoop, calls=%fused_computation.6 | loop fusion | flops 2927232 | bytes 17593884 | tf_op jit(solution)/shard_map/mul | solution.py:50
  134.2 6.7 %pad_maximum_fusion = bf16[3,64,19,9,64]{4,1,3,2,0:T(8,128)(2,1)} fusion(bf16[3,64,5,9,64]{4,1,3,2,0:T(8,128)(2,1)} %collective-permute-done.5, bf16[3,64,9,9,64]{4,1,3,2,0:T(8,128)(2,1)S(1)} %copy-done.3, bf16[3,64,5,9,64]{4,1,3,2,0:T(8,128)(2,1)} %collective-permute-done.4), kind=kLoop, calls=%fused_computation | loop fusion | flops 4202496 | bytes 8404992 | tf_op jit(solution)/shard_map/concatenate | solution.py:23
  140.9 9.7 %fusion.52 = (bf16[3,64,19,5,64]{4,1,3,2,0:T(8,128)(2,1)}, bf16[3,64,19,5,64]{4,1,3,2,0:T(8,128)(2,1)}) fusion(bf16[3,64,19,9,64]{4,1,3,2,0:T(8,128)(2,1)} %pad_maximum_fusion), kind=kLoop, calls=%fused_computation.143 | loop fusion | bytes 9338880 | tf_op jit(solution)/shard_map/slice | solution.py:20
  150.5 5.3 %collective-permute-start.6 = (bf16[3,64,19,5,64]{4,1,3,2,0:T(8,128)(2,1)}, bf16[3,64,19,5,64]{4,1,3,2,0:T(8,128)(2,1)}, u32[]{:S(2)}, u32[]{:S(2)}) collective-permute-start(bf16[3,64,19,5,64]{4,1,3,2,0:T(8,128)(2,1)} %get-tuple-element.6), channel_id=1, source_target_pairs={{0,1},{1,2},{2,3},{3,4},{4,5},{5,6},{6,7},{7,8},{8,9},{9,10},{10,1... | collective-permute-start | bytes 7004168 | tf_op jit(solution)/shard_map/ppermute | solution.py:21
  155.8 20.7 %multiply_add_fusion = (f32[64,11,11,64]{3,0,2,1:T(8,128)}, f32[64,11,11,64]{3,0,2,1:T(8,128)}) fusion(f32[64,11,11,63]{3,0,2,1:T(8,128)} %get-tuple-element.17, f32[64,11,10,64]{3,0,2,1:T(8,128)} %get-tuple-element.14, f32[64,10,11,64]{3,0,2,1:T(8,128)} %get-tuple-element.20, bf16[64,9,9,64]{3,0,2,1:T(8,128)(2,1)S(1)} %get-tuple-element.8, ...), kind=kLoop, calls=%fused_computation.7 | loop fusion | flops 8921088 | bytes 16403968 | tf_op jit(solution)/shard_map/add | solution.py:55
  176.5 16.8 %collective-permute-start.7 = (bf16[3,64,19,5,64]{4,1,3,2,0:T(8,128)(2,1)}, bf16[3,64,19,5,64]{4,1,3,2,0:T(8,128)(2,1)S(1)}, u32[]{:S(2)}, u32[]{:S(2)}) collective-permute-start(bf16[3,64,19,5,64]{4,1,3,2,0:T(8,128)(2,1)} %get-tuple-element.5), channel_id=1, source_target_pairs={{1,0},{2,1},{3,2},{4,3},{5,4},{6,5},{7,6},{8,7},{9,8},{10,9},{11,1... | collective-permute-start | bytes 7004168 | tf_op jit(solution)/shard_map/ppermute | solution.py:22
  193.3 3.7 convolution_bitcast_fusion.12
  196.9 2.7 convolution_bitcast_fusion.13
  199.7 6.8 %subtract_add_fusion.1 = f32[64,11,11,64]{3,0,2,1:T(8,128)S(1)} fusion(f32[64,11,11,63]{3,0,2,1:T(8,128)S(1)} %copy-done.4, f32[64,11,10,64]{3,0,2,1:T(8,128)} %get-tuple-element.12, f32[64,10,11,64]{3,0,2,1:T(8,128)} %get-tuple-element.18, bf16[64,9,9,64]{3,0,2,1:T(8,128)(2,1)S(1)} %get-tuple-element.7), kind=kLoop, calls=%fused_computation.9 | loop fusion | flops 4460544 | bytes 8201984 | tf_op jit(solution)/shard_map/add | solution.py:55
  208.5 2.0 convolution_bitcast_fusion.25
  210.4 2.0 convolution_bitcast_fusion.15
  212.4 2.0 convolution_bitcast_fusion.16
  214.4 42.8 %collective-permute-done.6 = bf16[3,64,19,5,64]{4,1,3,2,0:T(8,128)(2,1)} collective-permute-done((bf16[3,64,19,5,64]{4,1,3,2,0:T(8,128)(2,1)}, bf16[3,64,19,5,64]{4,1,3,2,0:T(8,128)(2,1)}, u32[]{:S(2)}, u32[]{:S(2)}) %collective-permute-start.6) | collective-permute-done | bytes 2334752 | tf_op jit(solution)/shard_map/ppermute | solution.py:21
  260.2 23.4 %collective-permute-done.7 = bf16[3,64,19,5,64]{4,1,3,2,0:T(8,128)(2,1)S(1)} collective-permute-done((bf16[3,64,19,5,64]{4,1,3,2,0:T(8,128)(2,1)}, bf16[3,64,19,5,64]{4,1,3,2,0:T(8,128)(2,1)S(1)}, u32[]{:S(2)}, u32[]{:S(2)}) %collective-permute-start.7) | collective-permute-done | bytes 2334752 | tf_op jit(solution)/shard_map/ppermute | solution.py:22
  290.2 2.0 fusion.32
  292.7 2.0 fusion.36
  294.6 2.7 fusion.28
  305.9 2.0 fusion.44
  309.2 88.0 %all-gather.3.cloned.1.call-done = f32[288,64,64]{2,1,0:T(8,128)} async-done(((f32[9,64,64]{2,1,0:T(8,128)}), f32[288,64,64]{2,1,0:T(8,128)}) %all-gather.3.cloned.1.call-update) | async-done | bytes 4718608 | tf_op jit(solution)/shard_map/all_gather | solution.py:126
  397.2 9.4 %copy.43 = f32[1,32,9,64,64]{4,3,2,1,0:T(8,128)} copy(f32[1,32,9,64,64]{4,3,2,1,0:T(8,128)} %bitcast.335) | data formatting | bytes 9437184
  (64 shorter events, 25.5 us)
Async XLA Ops:
  6.5 390.7 %all-gather.3.cloned.1.call-start = ((), (), s32[]{:S(2)}) async-start(), calls=%async_computation | async-start | bytes 9732096 | tf_op jit(solution)/shard_map/all_gather | solution.py:126
  7.3 22.3 %collective-permute-start = (f32[3,5,64]{2,1,0:T(8,128)S(1)}, f32[3,5,64]{2,1,0:T(8,128)S(1)}, u32[]{:S(2)}, u32[]{:S(2)}) collective-permute-start(f32[3,5,64]{2,1,0:T(8,128)S(1)} %get-tuple-element.24), channel_id=1, source_target_pairs={{0,32},{32,64},{64,96},{96,128},{128,160},{160,192},{192,224},{1,3... | collective-permute-start | bytes 11528 | tf_op jit(solution)/shard_map/ppermute | solution.py:21
  10.9 18.8 %collective-permute-start.1 = (f32[3,5,64]{2,1,0:T(8,128)S(1)}, f32[3,5,64]{2,1,0:T(8,128)S(1)}, u32[]{:S(2)}, u32[]{:S(2)}) collective-permute-start(f32[3,5,64]{2,1,0:T(8,128)S(1)} %get-tuple-element.23), channel_id=1, source_target_pairs={{32,0},{64,32},{96,64},{128,96},{160,128},{192,160},{224,192},{33,... | collective-permute-start | bytes 11528 | tf_op jit(solution)/shard_map/ppermute | solution.py:22
  17.1 8.7 %copy-start.2 = (bf16[3,64,9,9,64]{4,1,3,2,0:T(8,128)(2,1)}, bf16[3,64,9,9,64]{4,1,3,2,0:T(8,128)(2,1)S(1)}, u32[]{:S(2)}) copy-start(bf16[3,64,9,9,64]{4,1,3,2,0:T(8,128)(2,1)S(1)} %broadcast_multiply_fusion) | copy-start | bytes 5971972
  20.5 113.6 %collective-permute-start.5 = (bf16[3,64,5,9,64]{4,1,3,2,0:T(8,128)(2,1)}, bf16[3,64,5,9,64]{4,1,3,2,0:T(8,128)(2,1)}, u32[]{:S(2)}, u32[]{:S(2)}) collective-permute-start(bf16[3,64,5,9,64]{4,1,3,2,0:T(8,128)(2,1)} %get-tuple-element.11), channel_id=1, source_target_pairs={{32,0},{64,32},{96,64},{128,96},{160,128},{192,160},{224,192},{33,... | collective-permute-start | bytes 3317768 | tf_op jit(solution)/shard_map/ppermute | solution.py:22
  23.1 111.0 %collective-permute-start.4 = (bf16[3,64,5,9,64]{4,1,3,2,0:T(8,128)(2,1)}, bf16[3,64,5,9,64]{4,1,3,2,0:T(8,128)(2,1)}, u32[]{:S(2)}, u32[]{:S(2)}) collective-permute-start(bf16[3,64,5,9,64]{4,1,3,2,0:T(8,128)(2,1)} %get-tuple-element.10), channel_id=1, source_target_pairs={{0,32},{32,64},{64,96},{96,128},{128,160},{160,192},{192,224},{1,3... | collective-permute-start | bytes 3317768 | tf_op jit(solution)/shard_map/ppermute | solution.py:21
  27.8 1.3 copy-start.5
  28.5 1.1 copy-start.7
  29.7 9.4 %collective-permute-start.3 = (f32[11,3,64]{2,1,0:T(4,128)S(1)}, f32[11,3,64]{2,1,0:T(4,128)S(1)}, u32[]{:S(2)}, u32[]{:S(2)}) collective-permute-start(f32[11,3,64]{2,1,0:T(4,128)S(1)} %get-tuple-element.22), channel_id=1, source_target_pairs={{1,0},{2,1},{3,2},{4,3},{5,4},{6,5},{7,6},{8,7},{9,8},{10,9},{11,1... | collective-permute-start | bytes 25352 | tf_op jit(solution)/shard_map/ppermute | solution.py:22
  33.4 84.2 %collective-permute-start.2 = (f32[11,3,64]{2,1,0:T(4,128)S(1)}, f32[11,3,64]{2,1,0:T(4,128)S(1)}, u32[]{:S(2)}, u32[]{:S(2)}) collective-permute-start(f32[11,3,64]{2,1,0:T(4,128)S(1)} %get-tuple-element.21), channel_id=1, source_target_pairs={{0,1},{1,2},{2,3},{3,4},{4,5},{5,6},{6,7},{7,8},{8,9},{9,10},{10,1... | collective-permute-start | bytes 25352 | tf_op jit(solution)/shard_map/ppermute | solution.py:21
  128.1 6.0 %copy-start.3 = (bf16[3,64,9,9,64]{4,1,3,2,0:T(8,128)(2,1)S(1)}, bf16[3,64,9,9,64]{4,1,3,2,0:T(8,128)(2,1)}, u32[]{:S(2)}) copy-start(bf16[3,64,9,9,64]{4,1,3,2,0:T(8,128)(2,1)} %copy-done.2) | copy-start | bytes 5971972
  150.5 106.6 %collective-permute-start.6 = (bf16[3,64,19,5,64]{4,1,3,2,0:T(8,128)(2,1)}, bf16[3,64,19,5,64]{4,1,3,2,0:T(8,128)(2,1)}, u32[]{:S(2)}, u32[]{:S(2)}) collective-permute-start(bf16[3,64,19,5,64]{4,1,3,2,0:T(8,128)(2,1)} %get-tuple-element.6), channel_id=1, source_target_pairs={{0,1},{1,2},{2,3},{3,4},{4,5},{5,6},{6,7},{7,8},{8,9},{9,10},{10,1... | collective-permute-start | bytes 7004168 | tf_op jit(solution)/shard_map/ppermute | solution.py:21
  176.5 20.4 %copy-start = (f32[64,11,11,64]{3,0,2,1:T(8,128)S(1)}, f32[64,11,11,64]{3,0,2,1:T(8,128)}, u32[]{:S(2)}) copy-start(f32[64,11,11,64]{3,0,2,1:T(8,128)} %get-tuple-element.30) | copy-start | bytes 5947396
  176.5 107.1 %collective-permute-start.7 = (bf16[3,64,19,5,64]{4,1,3,2,0:T(8,128)(2,1)}, bf16[3,64,19,5,64]{4,1,3,2,0:T(8,128)(2,1)S(1)}, u32[]{:S(2)}, u32[]{:S(2)}) collective-permute-start(bf16[3,64,19,5,64]{4,1,3,2,0:T(8,128)(2,1)} %get-tuple-element.5), channel_id=1, source_target_pairs={{1,0},{2,1},{3,2},{4,3},{5,4},{6,5},{7,6},{8,7},{9,8},{10,9},{11,1... | collective-permute-start | bytes 7004168 | tf_op jit(solution)/shard_map/ppermute | solution.py:22
  193.2 6.4 %copy-start.4 = (f32[64,11,11,63]{3,0,2,1:T(8,128)S(1)}, f32[64,11,11,63]{3,0,2,1:T(8,128)}, u32[]{:S(2)}) copy-start(f32[64,11,11,63]{3,0,2,1:T(8,128)} %get-tuple-element.15) | copy-start | bytes 5854468
  199.7 6.8 %copy-start.1 = (f32[64,11,11,64]{3,0,2,1:T(8,128)S(1)}, f32[64,11,11,64]{3,0,2,1:T(8,128)}, u32[]{:S(2)}) copy-start(f32[64,11,11,64]{3,0,2,1:T(8,128)} %get-tuple-element.29) | copy-start | bytes 5947396
  308.4 0.7 copy-start.6
Sparse Core Ops, SparseCore 0:
  309.3 87.8 all-gather.2
where the time goes:
time: 419 us; the launch traced here: 414 us
  waiting for transfers between devices  233 us (56%)
  other arithmetic  55.4 us (13%)
  starting transfers between devices  42.4 us (10%)
  matrix products  42 us (10%)
  local copies, waits for them, and re-layouts  26.5 us (6%)
  between operations  14.8 us (4%)
    ppermute x4, waiting for transfers between devices, padded_2(): before = lax.ppermute(last, axis, up)  121 us
    all_gather x1, waiting for transfers between devices, body(): return lax.all_gather(ordered[None, None], 'sy', axis=1, tiled=True)  88 us
    dot_general x27, matrix products, contract(): jnp.einsum('kxyz,lxyz->kl', applied, piece.astype(jnp.float32), precision...  42 us
    add x2, other arithmetic, apply_component(): MASS * padded_field + factors[0] * term_x + factors[1] * term_y  27.5 us
    ppermute x4, starting transfers between devices, padded_2(): after = lax.ppermute(initial, axis, down)  25.7 us
    ppermute x4, waiting for transfers between devices, padded_2(): after = lax.ppermute(initial, axis, down)  23.4 us
    ppermute x4, starting transfers between devices, padded_2(): before = lax.ppermute(last, axis, up)  16.7 us
    unnamed x19, local copies, waits for them, and re-layouts  10.7 us
  transfers between devices with their start and end apart: 9, of which 4 were waited for; matrix products, arithmetic and copies ran while one was open for 17% of the time, Pallas kernels for 0%

commit v1 on v0

v1 whole, which is shorter than its diff:
```python
import functools

import jax
import jax.numpy as jnp
from jax import lax
from jax.experimental import pallas as pl
from jax.experimental.pallas import tpu as pltpu
from jax.sharding import PartitionSpec as P

MARGIN = 2
CX = 5
CY = 5
MASS = 0.5
EXT = 9
STRIP = 5
VEC = 64
NZ = 64
L = 128
ROWS = 96
CODE_MAX = 32767.0
VMEM = 56 * 1024 * 1024

NT = (((1,), (1,)), ((), ()))


def pairs(values):
    low = lax.broadcasted_iota(jnp.int32, values[0].shape, 1) < NZ
    out = []
    for at in range(0, len(values), 2):
        first = values[at]
        if at + 1 < len(values):
            second = values[at + 1]
            top = jnp.where(low, first, pltpu.roll(second, NZ, 1))
            bottom = jnp.where(low, pltpu.roll(first, NZ, 1), second)
        else:
            top = jnp.where(low, first, 0.0)
            bottom = jnp.where(low, pltpu.roll(first, NZ, 1), 0.0)
        out.append(jnp.concatenate([top, bottom], axis=0))
    return out


def split(value):
    high = value.astype(jnp.bfloat16)
    low = (value - high.astype(jnp.float32)).astype(jnp.bfloat16)
    return high, low


def pack_kernel(meta, cv, own, strip_y, strip_x, corner):
    a = pl.program_id(0)
    count, mirrored, row, col = meta[0], meta[1], meta[2], meta[3]
    x = row * CX - MARGIN + a
    in_x = (x >= 0) & (x < meta[4])
    index01 = lax.broadcasted_iota(jnp.int32, (VEC, L), 0)
    lane = lax.broadcasted_iota(jnp.int32, (VEC // 2, L), 1)
    index2 = lax.broadcasted_iota(jnp.int32, (VEC // 2, L), 0) + jnp.where(lane < NZ, 0, VEC // 2)
    for b in range(EXT):
        place = jnp.where(mirrored == 1, EXT - 1 - b, b)
        y = col * CY - MARGIN + place
        keep = jnp.where(in_x & (y >= 0) & (y < meta[5]), count, 0)
        zero, one, two = (cv[component, 0, place] for component in range(3))
        mask01 = (index01 < keep).astype(jnp.float32).astype(jnp.bfloat16)
        mask2 = (index2 < keep).astype(jnp.float32).astype(jnp.bfloat16)
        both = jnp.concatenate([zero, one], axis=1) * mask01
        last = jnp.concatenate([two[: VEC // 2], two[VEC // 2 :]], axis=1) * mask2
        cell = jnp.concatenate([both, last], axis=0)
        span = slice(b * L, (b + 1) * L)
        own[0, :, span] = cell
        if b < STRIP:
            strip_y[0, :, span] = cell
        turned = EXT - 1 - b
        span = slice(turned * L, (turned + 1) * L)
        strip_x[0, :, span] = cell
        if turned < STRIP:
            corner[0, :, span] = cell


def pack(meta, cv):
    tail = lambda a, m: (jnp.maximum(a - (EXT - STRIP), 0), 0, 0)
    plain = lambda a, m: (a, 0, 0)
    return pl.pallas_call(
        pack_kernel,
        grid_spec=pltpu.PrefetchScalarGridSpec(
            num_scalar_prefetch=1,
            grid=(EXT,),
            in_specs=[pl.BlockSpec((3, 1, EXT, VEC, NZ), lambda a, m: (0, a, 0, 0, 0))],
            out_specs=[
                pl.BlockSpec((1, ROWS, EXT * L), plain),
                pl.BlockSpec((1, ROWS, STRIP * L), plain),
                pl.BlockSpec((1, ROWS, EXT * L), tail),
                pl.BlockSpec((1, ROWS, STRIP * L), tail),
            ],
        ),
        out_shape=[
            jax.ShapeDtypeStruct((EXT, ROWS, EXT * L), jnp.bfloat16),
            jax.ShapeDtypeStruct((EXT, ROWS, STRIP * L), jnp.bfloat16),
            jax.ShapeDtypeStruct((STRIP, ROWS, EXT * L), jnp.bfloat16),
            jax.ShapeDtypeStruct((STRIP, ROWS, STRIP * L), jnp.bfloat16),
        ],
        compiler_params=pltpu.CompilerParams(vmem_limit_bytes=VMEM),
        cost_estimate=pl.CostEstimate(flops=1000000, bytes_accessed=9000000, transcendentals=0),
        name="pack",
    )(meta, cv)


FRAME = EXT + 2


def weights_into(stiff, wx, wy, up, down):
    lane = lax.broadcasted_iota(jnp.int32, (FRAME, L), 1)
    inner = (lane % NZ) < NZ - 1
    wx[...] = jnp.zeros_like(wx)
    wy[...] = jnp.zeros_like(wy)
    for a in range(FRAME):
        here = stiff[a]
        if a > 0:
            other = stiff[a - 1]
            wx[a, :FRAME] = jnp.where((here > 0) & (other > 0), 0.5 * (here + other), 0.0)
        left, right = here[:-1], here[1:]
        wy[a, 1:FRAME] = jnp.where((left > 0) & (right > 0), 0.5 * (left + right), 0.0)
        above = jnp.where(inner, 0.5 * (here + pltpu.roll(here, L - 1, 1)), 0.0)
        up[a, :FRAME] = above
        down[a, :FRAME] = pltpu.roll(above, 1, 1)


def apply_cell(field, weights, a, b, ra, lane_low):
    wx, wy, up, down = weights
    wxa, wxb = wx[a, b : b + 1], wx[a + 1, b : b + 1]
    wya, wyb = wy[a, b : b + 1], wy[a, b + 1 : b + 2]
    upw, dnw = up[a, b : b + 1], down[a, b : b + 1]
    fx = jnp.where(lane_low, 3.0, 1.0)
    fy = jnp.where(lane_low, 1.0, 3.0)

    def at(da, db, rows):
        return field[ra + da, rows, (b + db) * L : (b + db + 1) * L]

    out = []
    for rows, (cx, cy, cz) in ((slice(0, VEC), (fx, fy, 1.0)), (slice(VEC, ROWS), (1.0, 1.0, 3.0))):
        xa, xb, ya, yb, zu, zd = wxa * cx, wxb * cx, wya * cy, wyb * cy, upw * cz, dnw * cz
        diagonal = MASS + (xa + xb) + (ya + yb) + (zu + zd)
        u = at(0, 0, rows)
        total = diagonal * u - xa * at(-1, 0, rows) - xb * at(1, 0, rows)
        total = total - ya * at(0, -1, rows) - yb * at(0, 1, rows)
        total = total - zu * pltpu.roll(u, L - 1, 1) - zd * pltpu.roll(u, 1, 1)
        out.append(total)
    return out


def own_kernel(u, stiff, applied01, applied2a, applied2b, self_block, wx, wy, up, down, field, acc):
    weights_into(stiff, wx, wy, up, down)
    zero = jnp.zeros((ROWS, L), jnp.float32)
    field[0] = jnp.zeros((ROWS, (FRAME + 1) * L), jnp.float32)
    field[1] = jnp.zeros((ROWS, (FRAME + 1) * L), jnp.float32)
    field[FRAME] = jnp.zeros((ROWS, (FRAME + 1) * L), jnp.float32)

    @pl.loop(0, EXT)
    def _(a):
        field[a + 2, :, 0:L] = zero
        field[a + 2, :, L : (EXT + 1) * L] = u[a].astype(jnp.float32)
        field[a + 2, :, (EXT + 1) * L : (FRAME + 1) * L] = jnp.zeros((ROWS, 2 * L), jnp.float32)

    lane_low = lax.broadcasted_iota(jnp.int32, (1, L), 1) < NZ
    weights = (wx, wy, up, down)

    @pl.loop(0, FRAME - 1)
    def _(a):
        thirds = []
        for b in range(1, FRAME):
            first, third = apply_cell(field, weights, a, b, a + 1, lane_low)
            high, low = split(first)
            applied01[a, :VEC, (b - 1) * L : b * L] = high
            applied01[a, VEC:, (b - 1) * L : b * L] = low
            thirds.append(third)
        for target, cells in ((applied2a, thirds[:EXT]), (applied2b, thirds[STRIP:])):
            for n, value in enumerate(pairs(cells)):
                high, low = split(value)
                target[a, :VEC, n * L : (n + 1) * L] = high
                target[a, VEC:, n * L : (n + 1) * L] = low

    acc[...] = jnp.zeros_like(acc)

    @pl.loop(0, EXT)
    def _(a):
        third = u[a, VEC:].astype(jnp.float32)
        third = pairs([third[:, b * L : (b + 1) * L] for b in range(EXT)])
        third = jnp.concatenate(third, axis=1).astype(jnp.bfloat16)
        acc[...] += lax.dot_general(
            applied01[a + 1, :, : EXT * L], u[a, :VEC], NT, preferred_element_type=jnp.float32
        ) + lax.dot_general(applied2a[a + 1], third, NT, preferred_element_type=jnp.float32)

    self_block[...] = acc[:VEC] + acc[VEC:]


def own(u, stiff):
    weight = jax.ShapeDtypeStruct((FRAME, 16, L), jnp.float32)
    return pl.pallas_call(
        own_kernel,
        out_shape=[
            jax.ShapeDtypeStruct((FRAME - 1, 2 * VEC, (FRAME - 1) * L), jnp.bfloat16),
            jax.ShapeDtypeStruct((FRAME - 1, 2 * VEC, 5 * L), jnp.bfloat16),
            jax.ShapeDtypeStruct((FRAME - 1, 2 * VEC, 3 * L), jnp.bfloat16),
            jax.ShapeDtypeStruct((VEC, VEC), jnp.float32),
            weight,
            weight,
            weight,
            weight,
        ],
        scratch_shapes=[
            pltpu.VMEM((FRAME + 1, ROWS, (FRAME + 1) * L), jnp.float32),
            pltpu.VMEM((2 * VEC, VEC), jnp.float32),
        ],
        compiler_params=pltpu.CompilerParams(vmem_limit_bytes=VMEM),
        cost_estimate=pl.CostEstimate(flops=300000000, bytes_accessed=12000000, transcendentals=0),
        name="own",
    )(u, stiff)


def lane_join(left, right):
    return jnp.concatenate([left, right], axis=1)


def thirds_of(ref, a, cells):
    third = ref[a, VEC:].astype(jnp.float32)
    third = pairs([third[:, b * L : (b + 1) * L] for b in range(cells)])
    return jnp.concatenate(third, axis=1).astype(jnp.bfloat16)


def cross_kernel(
    applied01, applied2a, applied2b, self_block, wx, wy, up, down, high_y, low_x, corner,
    mine, theirs, field, acc_y, acc_x, acc_c, acc_d, ah01, ah2,
):
    dot = functools.partial(lax.dot_general, dimension_numbers=NT, preferred_element_type=jnp.float32)
    acc_y[...] = jnp.zeros_like(acc_y)
    acc_x[...] = jnp.zeros_like(acc_x)
    acc_c[...] = jnp.zeros_like(acc_c)
    acc_d[...] = jnp.zeros_like(acc_d)
    first = FRAME - 1 - STRIP

    @pl.loop(0, EXT)
    def _(a):
        acc_y[...] += dot(applied01[a + 1, :, first * L :], high_y[a, :VEC]) + dot(
            applied2b[a + 1], thirds_of(high_y, a, STRIP)
        )

    field[...] = jnp.zeros_like(field)
    for a in range(STRIP):
        field[a + 2, :, 2 * L : (2 + STRIP) * L] = high_y[a].astype(jnp.float32)
    lane_low = lax.broadcasted_iota(jnp.int32, (1, L), 1) < NZ

    class Shifted:
        def __getitem__(self, key):
            a, rows, span = key
            return field[a, rows, span.start - 4 * L : span.stop - 4 * L]

    @pl.loop(0, STRIP)
    def _(a):
        thirds = []
        for n in range(STRIP):
            both, third = apply_cell(Shifted(), (wx, wy, up, down), a, n + 5, a + 1, lane_low)
            high, low = split(both)
            ah01[:VEC, n * L : (n + 1) * L] = high
            ah01[VEC:, n * L : (n + 1) * L] = low
            thirds.append(third)
        for n, value in enumerate(pairs(thirds)):
            high, low = split(value)
            ah2[:VEC, n * L : (n + 1) * L] = high
            ah2[VEC:, n * L : (n + 1) * L] = low
        acc_x[...] += dot(applied01[a, :, : EXT * L], low_x[a, :VEC]) + dot(
            applied2a[a], thirds_of(low_x, a, EXT)
        )
        acc_c[...] += dot(applied01[a, :, first * L :], corner[a, :VEC]) + dot(
            applied2b[a], thirds_of(corner, a, STRIP)
        )
        third = low_x[a, VEC:, (EXT - STRIP) * L :].astype(jnp.float32)
        third = pairs([third[:, n * L : (n + 1) * L] for n in range(STRIP)])
        third = jnp.concatenate(third, axis=1).astype(jnp.bfloat16)
        acc_d[...] += dot(ah01[...], low_x[a, :VEC, (EXT - STRIP) * L :]) + dot(ah2[...], third)

    own_block = self_block[...]
    block_y = acc_y[:VEC] + acc_y[VEC:]
    block_x = acc_x[:VEC] + acc_x[VEC:]
    block_c = acc_c[:VEC] + acc_c[VEC:]
    block_d = acc_d[:VEC] + acc_d[VEC:]
    nothing = jnp.zeros((VEC, VEC), jnp.float32)
    tiles = [lane_join(own_block, block_y), lane_join(block_x, block_d), lane_join(block_c, nothing)]
    turned = [lane_join(block_x.T, block_d.T), lane_join(nothing, block_c.T)]
    largest = functools.reduce(jnp.maximum, [jnp.abs(tile) for tile in tiles])
    largest = jnp.max(jnp.max(largest, axis=0, keepdims=True), axis=1, keepdims=True)
    exponent = jnp.clip(jnp.ceil(jnp.log2(largest)), -100.0, 120.0)
    scale = jnp.exp2(-exponent)

    def code(tile):
        size = jnp.minimum(jnp.sqrt(jnp.abs(tile) * scale) * CODE_MAX, CODE_MAX) + 0.5
        size = size.astype(jnp.int32)
        return jnp.where(tile < 0, -size, size).astype(jnp.int16)

    for n, tile in enumerate(tiles):
        mine[n * VEC : (n + 1) * VEC] = code(tile)
    for n, tile in enumerate(turned):
        theirs[n * VEC : (n + 1) * VEC] = code(tile)
    level = jnp.broadcast_to(exponent.astype(jnp.int32), (16, L))
    low_lanes = lax.broadcasted_iota(jnp.int32, (16, L), 1) < NZ
    mine[3 * VEC : 3 * VEC + 16] = jnp.where(low_lanes, level, 0).astype(jnp.int16)
    theirs[2 * VEC : 2 * VEC + 16] = jnp.where(low_lanes, 0, level).astype(jnp.int16)


def cross(applied, strips):
    total = pltpu.VMEM((2 * VEC, VEC), jnp.float32)
    return pl.pallas_call(
        cross_kernel,
        out_shape=[
            jax.ShapeDtypeStruct((3 * VEC + 16, L), jnp.int16),
            jax.ShapeDtypeStruct((2 * VEC + 16, L), jnp.int16),
        ],
        scratch_shapes=[
            pltpu.VMEM((STRIP + 2, ROWS, (STRIP + 2) * L), jnp.float32),
            total,
            total,
            total,
            total,
            pltpu.VMEM((2 * VEC, STRIP * L), jnp.bfloat16),
            pltpu.VMEM((2 * VEC, 3 * L), jnp.bfloat16),
        ],
        compiler_params=pltpu.CompilerParams(vmem_limit_bytes=VMEM),
        cost_estimate=pl.CostEstimate(flops=500000000, bytes_accessed=9000000, transcendentals=0),
        name="cross",
    )(*applied, *strips)


PAY = 4 * VEC + 16
GROUP = 4


def decode_kernel(meta, here, there, out):
    mirrored = meta[0] == 1
    my_y, my_z, my_core = meta[1], meta[2], meta[3]
    total = 32

    def tile(c, part, rows):
        d_y = (c // 8 - my_y) & 3
        d_z = ((c % 8) // 2 - my_z) & 3
        slot = d_y * 4 + d_z
        away = (c % 2) != my_core
        one = here[slot, part : part + rows].astype(jnp.int32)
        two = there[slot, part : part + rows].astype(jnp.int32)
        return jnp.where(away, two, one).astype(jnp.float32)

    def levels(c):
        level = tile(c, 4 * VEC, 16)
        level = jnp.exp2(level) * (1.0 / (CODE_MAX * CODE_MAX))
        return level[0:1, 0:1], level[0:1, NZ : NZ + 1]

    def value(code, scale):
        return code * jnp.abs(code) * scale

    i_y = jnp.where(mirrored, 3, 5)
    i_yt = jnp.where(mirrored, 5, 3)
    i_c = jnp.where(mirrored, 0, 2)
    i_d = jnp.where(mirrored, 2, 0)
    i_dn = jnp.where(mirrored, 8, 6)
    i_cn = jnp.where(mirrored, 6, 8)
    step = jnp.where(mirrored, 1, -1)
    for n in range(GROUP):
        c = pl.program_id(0) * GROUP + n
        from_own = (c + step + total) & (total - 1)
        from_next = (c - step + total) & (total - 1)
        mine, next_row = levels(c)
        tile0 = value(tile(c, 0, VEC), mine)
        out[0, n, 4] = tile0[:, :NZ]
        out[0, n, i_y] = tile0[:, NZ:]
        tile1 = value(tile(c, VEC, VEC), mine)
        out[0, n, 1] = tile1[:, :NZ]
        tile2 = value(tile(c, 2 * VEC, VEC), next_row)
        out[0, n, 7] = tile2[:, :NZ]
        out[0, n, i_dn] = tile2[:, NZ:]
        tile3 = value(tile(c, 3 * VEC, VEC), mine)
        out[0, n, i_c] = tile3[:, :NZ]
        mine, _ = levels(from_own)
        tile0 = value(tile(from_own, 0, VEC), mine)
        out[0, n, i_yt] = tile0[:, NZ:].T
        tile1 = value(tile(from_own, VEC, VEC), mine)
        out[0, n, i_d] = tile1[:, NZ:]
        _, next_row = levels(from_next)
        tile3 = value(tile(from_next, 3 * VEC, VEC), next_row)
        out[0, n, i_cn] = tile3[:, NZ:]


def decode(meta, here, there, columns):
    whole = pl.BlockSpec((16, PAY, L), lambda g, m: (0, 0, 0))
    return pl.pallas_call(
        decode_kernel,
        grid_spec=pltpu.PrefetchScalarGridSpec(
            num_scalar_prefetch=1,
            grid=(columns // GROUP,),
            in_specs=[whole, whole],
            out_specs=pl.BlockSpec((1, GROUP, 9, VEC, VEC), lambda g, m: (0, g, 0, 0, 0)),
        ),
        out_shape=jax.ShapeDtypeStruct((1, columns, 9, VEC, VEC), jnp.float32),
        compiler_params=pltpu.CompilerParams(vmem_limit_bytes=VMEM),
        cost_estimate=pl.CostEstimate(flops=10000000, bytes_accessed=12000000, transcendentals=0),
        name="decode",
    )(meta, here, there)


def padded_2(x, sides, width):
    for axis, dim in sides:
        peers, length = (lax.axis_size(axis), x.shape[dim])
        up = [(i, (i + 1) % peers) for i in range(peers - 1)]
        down = [(j, i) for i, j in up]
        last = lax.slice_in_dim(x, length - width, length, axis=dim)
        initial = lax.slice_in_dim(x, 0, width, axis=dim)
        before = lax.ppermute(last, axis, up)
        after = lax.ppermute(initial, axis, down)
        x = jnp.concatenate([before, x, after], axis=dim)
    return x


def body(coarse_vectors, stiffness, vector_counts):
    rows, columns = lax.axis_size("sx"), lax.axis_size("sy")
    row, col = lax.axis_index("sx"), lax.axis_index("sy")
    mirrored = 1 - row % 2
    meta = jnp.stack([vector_counts[0, 0], mirrored, row, col, jnp.int32(CX * rows), jnp.int32(CY * columns)])
    cv = jnp.transpose(coarse_vectors, (0, 2, 3, 1, 4))

    rim = padded_2(stiffness, (("sx", 0), ("sy", 1)), MARGIN + 1)
    u, strip_y, strip_x, corner = pack(meta.astype(jnp.int32), cv)

    both = ("sx", "sy")
    number = lambda r, c: r * columns + c
    side, diagonal = [], []
    for r in range(rows):
        toward = 1 if r % 2 else -1
        for c in range(columns):
            if 0 <= c + toward < columns:
                side.append((number(r, c + toward), number(r, c)))
                if r > 0:
                    diagonal.append((number(r - 1, c + toward), number(r, c)))
    return_x = [(r, r + 1) for r in range(rows - 1)]
    high_y = lax.ppermute(strip_y, both, side)
    low_x = lax.ppermute(strip_x, "sx", return_x)
    far = lax.ppermute(corner, both, diagonal)

    rim = jnp.where(mirrored == 1, rim[:, ::-1], rim)
    rim = jnp.concatenate([rim, rim], axis=2)
    applied = own(u, rim)
    mine, theirs = cross(applied, (high_y, low_x, far))
    got = lax.ppermute(theirs, "sx", [(r + 1, r) for r in range(rows - 1)])
    pay = jnp.concatenate(
        [mine[: 2 * VEC], got[:VEC], mine[2 * VEC : 3 * VEC] + got[VEC : 2 * VEC], mine[3 * VEC :] + got[2 * VEC :]],
        axis=0,
    )

    def ring(d_y, d_z, d_core):
        out = []
        for target in range(columns):
            y, z, core = target // 8, target % 8 // 2, target % 2
            out.append(((y + d_y) % 4 * 8 + (z + d_z) % 4 * 2 + (core ^ d_core), target))
        return out

    def around(x, one, other):
        half = x.shape[0] // 2
        ahead = lax.ppermute(x, "sy", one)
        behind = lax.ppermute(x, "sy", other)
        far_a = lax.ppermute(ahead[:half], "sy", one)
        far_b = lax.ppermute(behind[half:], "sy", other)
        return x, ahead, (far_a, far_b), behind

    x, ahead, (far_a, far_b), behind = around(pay, ring(0, 1, 0), ring(0, -1, 0))
    line = jnp.stack([x, ahead, jnp.concatenate([far_a, far_b], axis=0), behind])
    x, ahead, (far_a, far_b), behind = around(line, ring(1, 0, 0), ring(-1, 0, 0))
    here = jnp.concatenate([x, ahead, far_a, far_b, behind], axis=0)
    there = lax.ppermute(here, "sy", ring(0, 0, 1))
    place = jnp.stack([mirrored, col // 8, col % 8 // 2, col % 2]).astype(jnp.int32)
    return decode(place, here, there, columns)


def solution(mesh):
    return jax.shard_map(
        body,
        mesh=mesh,
        in_specs=(P(None, None, "sx", "sy", None), P("sx", "sy", None), P("sx", "sy")),
        out_specs=P("sx", None, None, None, None),
        check_vma=False,
    )
```

time: 419 us -> 146 us (0.35)
  the two profiles are of different devices: /device:TPU:11 before, /device:TPU:1 now
where the time goes in v1:
time: 146 us; the launch traced here: 145 us
  waiting for transfers between devices  52.8 us (36%)
  starting transfers between devices  45.3 us (31%)
  Pallas kernels  38.7 us (27%)
  local copies, waits for them, and re-layouts  4.19 us (3%)
  other arithmetic  2.9 us (2%)
    ppermute x2, waiting for transfers between devices, padded_2(): before = lax.ppermute(last, axis, up)  27.2 us
    ppermute x2, starting transfers between devices, padded_2(): before = lax.ppermute(last, axis, up)  14.4 us
    pallas_call x1, Pallas kernels, own(): pl.pallas_call(own_kernel, out_shape=[jax.ShapeDtypeStruct((FRAME - 1, 2...  11.7 us
    pallas_call x1, Pallas kernels, cross(): pl.pallas_call(cross_kernel, out_shape=[jax.ShapeDtypeStruct((3 * VEC + 1...  9.66 us
    pallas_call x1, Pallas kernels, decode(): pl.pallas_call(decode_kernel, grid_spec=pltpu.PrefetchScalarGridSpec(num_...  8.96 us
    pallas_call x1, Pallas kernels, pack(): pl.pallas_call(pack_kernel, grid_spec=pltpu.PrefetchScalarGridSpec(num_sc...  8.4 us
    ppermute x2, waiting for transfers between devices, around(): ahead = lax.ppermute(x, 'sy', one)  8.28 us
    ppermute x2, starting transfers between devices, around(): ahead = lax.ppermute(x, 'sy', one)  6.61 us
  transfers between devices with their start and end apart: 17, of which 11 were waited for; matrix products, arithmetic and copies ran while one was open for 2% of the time, Pallas kernels for 8%

profile of v1, /device:TPU:1, one launch (start us, length us, event | category | flops | bytes accessed | tf_op | source)
XLA Modules:
  0.0 144.8 jit_solution(15522546496387693479)
XLA Ops:
  0.7 0.7 stack.47.meta
  1.3 8.4 %pack.1 = (bf16[9,96,1152]{2,1,0:T(8,128)(2,1)}, bf16[9,96,640]{2,1,0:T(8,128)(2,1)}, bf16[5,96,1152]{2,1,0:T(8,128)(2,1)}, bf16[5,96,640]{2,1,0:T(8,128)(2,1)}) custom-call(s32[6]{0:T(128)} %stack.47.meta, bf16[3,9,9,64,64]{4,3,2,1,0:T(8,128)(2,1)} %bitcast.20), custom_call_target="tpu_custom_call" | custom-call | flops 1000000 | bytes 9000000 | tf_op jit(solution)/shard_map/pack/pallas_call | solution.py:80
  9.7 6.3 %collective-permute-start.4 = (bf16[9,96,640]{2,1,0:T(8,128)(2,1)}, bf16[9,96,640]{2,1,0:T(8,128)(2,1)S(1)}, u32[]{:S(2)}, u32[]{:S(2)}) collective-permute-start(bf16[9,96,640]{2,1,0:T(8,128)(2,1)} %get-tuple-element.28), channel_id=1, source_target_pairs={{0,1},{1,2},{2,3},{3,4},{4,5},{5,6},{6,7},{7,8},{8,9},{9,10},{10,1... | collective-permute-start | bytes 3317768 | tf_op jit(solution)/shard_map/ppermute | solution.py:438
  16.0 1.4 collective-permute-start.5
  17.4 4.8 %collective-permute-start = (f32[3,5,64]{2,1,0:T(8,128)S(1)}, f32[3,5,64]{2,1,0:T(8,128)S(1)}, u32[]{:S(2)}, u32[]{:S(2)}) collective-permute-start(f32[3,5,64]{2,1,0:T(8,128)S(1)} %get-tuple-element.40), channel_id=1, source_target_pairs={{0,32},{32,64},{64,96},{96,128},{128,160},{160,192},{192,224},{1,3... | collective-permute-start | bytes 11528 | tf_op jit(solution)/shard_map/ppermute | solution.py:411
  22.3 1.3 collective-permute-start.1
  23.6 1.8 %collective-permute-start.6 = (bf16[5,96,640]{2,1,0:T(8,128)(2,1)}, bf16[5,96,640]{2,1,0:T(8,128)(2,1)S(1)}, u32[]{:S(2)}, u32[]{:S(2)}) collective-permute-start(bf16[5,96,640]{2,1,0:T(8,128)(2,1)} %get-tuple-element.30), channel_id=1, source_target_pairs={{1,32},{2,33},{3,34},{4,35},{5,36},{6,37},{7,38},{8,39},{9,40},{10... | collective-permute-start | bytes 1843208 | tf_op jit(solution)/shard_map/ppermute | solution.py:440
  25.3 27.2 %collective-permute-done = f32[3,5,64]{2,1,0:T(8,128)S(1)} collective-permute-done((f32[3,5,64]{2,1,0:T(8,128)S(1)}, f32[3,5,64]{2,1,0:T(8,128)S(1)}, u32[]{:S(2)}, u32[]{:S(2)}) %collective-permute-start) | collective-permute-done | bytes 3872 | tf_op jit(solution)/shard_map/ppermute | solution.py:411
  52.6 9.6 %collective-permute-start.2 = (f32[11,3,64]{2,1,0:T(4,128)S(1)}, f32[11,3,64]{2,1,0:T(4,128)S(1)}, u32[]{:S(2)}, u32[]{:S(2)}) collective-permute-start(f32[11,3,64]{2,1,0:T(4,128)S(1)} %get-tuple-element.35), channel_id=1, source_target_pairs={{0,1},{1,2},{2,3},{3,4},{4,5},{5,6},{6,7},{7,8},{8,9},{9,10},{10,1... | collective-permute-start | bytes 25352 | tf_op jit(solution)/shard_map/ppermute | solution.py:411
  62.2 1.9 %collective-permute-start.3 = (f32[11,3,64]{2,1,0:T(4,128)S(1)}, f32[11,3,64]{2,1,0:T(4,128)S(1)}, u32[]{:S(2)}, u32[]{:S(2)}) collective-permute-start(f32[11,3,64]{2,1,0:T(4,128)S(1)} %get-tuple-element.36), channel_id=1, source_target_pairs={{1,0},{2,1},{3,2},{4,3},{5,4},{6,5},{7,6},{8,7},{9,8},{10,9},{11,1... | collective-permute-start | bytes 25352 | tf_op jit(solution)/shard_map/ppermute | solution.py:412
  64.1 4.1 %collective-permute-done.3 = f32[11,3,64]{2,1,0:T(4,128)S(1)} collective-permute-done((f32[11,3,64]{2,1,0:T(4,128)S(1)}, f32[11,3,64]{2,1,0:T(4,128)S(1)}, u32[]{:S(2)}, u32[]{:S(2)}) %collective-permute-start.3) | collective-permute-done | bytes 8480 | tf_op jit(solution)/shard_map/ppermute | solution.py:412
  68.3 0.7 pad_maximum_fusion.1.stiff
  69.0 11.7 %own.1 = (bf16[10,128,1280]{2,1,0:T(8,128)(2,1)}, bf16[10,128,640]{2,1,0:T(8,128)(2,1)}, bf16[10,128,384]{2,1,0:T(8,128)(2,1)}, f32[64,64]{1,0:T(8,128)}, f32[11...) custom-call(bf16[9,96,1152]{2,1,0:T(8,128)(2,1)} %get-tuple-element.19.u, ...), custom_call_target="tpu_custom_call" | custom-call | flops 300000000 | bytes 12000000 | tf_op jit(solution)/shard_map/own/pallas_call | solution.py:195
  80.8 0.8 copy-done.4
  82.3 9.7 %cross.1 = (s16[208,128]{1,0:T(8,128)(2,1)}, s16[144,128]{1,0:T(8,128)(2,1)}) custom-call(bf16[10,128,1280]{2,1,0:T(8,128)(2,1)} %get-tuple-element.20.applied01, bf16[10,128,640]{2,1,0:T(8,128)(2,1)} %get-tuple-element.21.applied2a, bf16[10,128,384]{2,1,0:T(8,128)(2,1)} %get-tuple-element.22.applied2b, f32[64,64]{1,0:T(8,128)} %get-tuple-element.23.self_block, ...), custom_call_target="tpu_custom_call" | custom-call | flops 500000000 | bytes 9000000 | tf_op jit(solution)/shard_map/cross/pallas_call | solution.py:308
  91.9 1.3 collective-permute-start.7
  93.2 0.8 slice.46
  94.0 2.9 %collective-permute-done.7 = s16[144,128]{1,0:T(8,128)(2,1)S(1)} collective-permute-done((s16[144,128]{1,0:T(8,128)(2,1)}, s16[144,128]{1,0:T(8,128)(2,1)S(1)}, u32[]{:S(2)}, u32[]{:S(2)}) %collective-permute-start.7) | collective-permute-done | bytes 36896 | tf_op jit(solution)/shard_map/ppermute | solution.py:446
  97.5 0.7 fusion.2
  98.3 6.5 %collective-permute-start.8 = (s16[272,128]{1,0:T(8,128)(2,1)S(1)}, s16[272,128]{1,0:T(8,128)(2,1)S(1)}, u32[]{:S(2)}, u32[]{:S(2)}) collective-permute-start(s16[272,128]{1,0:T(8,128)(2,1)S(1)} %get-tuple-element.34), channel_id=1, source_target_pairs={{2,0},{3,1},{4,2},{5,3},{6,4},{7,5},{0,6},{1,7},{10,8},{11,9},{12,... | collective-permute-start | bytes 208904 | tf_op jit(solution)/shard_map/ppermute | solution.py:461
  104.8 1.4 collective-permute-done.8
  106.2 3.9 %collective-permute-start.9 = (s16[136,128]{1,0:T(8,128)(2,1)S(1)}, s16[136,128]{1,0:T(8,128)(2,1)S(1)}, u32[]{:S(2)}, u32[]{:S(2)}) collective-permute-start(s16[136,128]{1,0:T(8,128)(2,1)S(1)} %slice.61), channel_id=1, source_target_pairs={{2,0},{3,1},{4,2},{5,3},{6,4},{7,5},{0,6},{1,7},{10,8},{11,9},{12,... | collective-permute-start | bytes 104456 | tf_op jit(solution)/shard_map/ppermute | solution.py:463
  110.3 0.8 collective-permute-done.9
  111.1 4.1 %collective-permute-done.11 = s16[136,128]{1,0:T(8,128)(2,1)S(1)} collective-permute-done((s16[136,128]{1,0:T(8,128)(2,1)S(1)}, s16[136,128]{1,0:T(8,128)(2,1)S(1)}, u32[]{:S(2)}, u32[]{:S(2)}) %collective-permute-start.11) | collective-permute-done | bytes 34848 | tf_op jit(solution)/shard_map/ppermute | solution.py:464
  115.3 1.5 %collective-permute-start.14 = (s16[4,272,128]{2,1,0:T(8,128)(2,1)S(1)}, s16[4,272,128]{2,1,0:T(8,128)(2,1)S(1)}, u32[]{:S(2)}, u32[]{:S(2)}) collective-permute-start(s16[4,272,128]{2,1,0:T(8,128)(2,1)S(1)} %pad_add_fusion), channel_id=1, source_target_pairs={{24,0},{25,1},{26,2},{27,3},{28,4},{29,5},{30,6},{31,7},{0,8},{1,9... | collective-permute-start | bytes 835592 | tf_op jit(solution)/shard_map/ppermute | solution.py:462
  116.9 6.9 %collective-permute-done.12 = s16[4,272,128]{2,1,0:T(8,128)(2,1)S(1)} collective-permute-done((s16[4,272,128]{2,1,0:T(8,128)(2,1)S(1)}, s16[4,272,128]{2,1,0:T(8,128)(2,1)S(1)}, u32[]{:S(2)}, u32[]{:S(2)}) %collective-permute-start.12) | collective-permute-done | bytes 278560 | tf_op jit(solution)/shard_map/ppermute | solution.py:461
  123.9 1.5 %collective-permute-start.15 = (s16[2,272,128]{2,1,0:T(8,128)(2,1)S(1)}, s16[2,272,128]{2,1,0:T(8,128)(2,1)S(1)}, u32[]{:S(2)}, u32[]{:S(2)}) collective-permute-start(s16[2,272,128]{2,1,0:T(8,128)(2,1)S(1)} %slice.64), channel_id=1, source_target_pairs={{24,0},{25,1},{26,2},{27,3},{28,4},{29,5},{30,6},{31,7},{0,8},{1,9... | collective-permute-start | bytes 417800 | tf_op jit(solution)/shard_map/ppermute | solution.py:464
  125.5 3.5 %collective-permute-done.13 = s16[2,272,128]{2,1,0:T(8,128)(2,1)S(1)} collective-permute-done((s16[2,272,128]{2,1,0:T(8,128)(2,1)S(1)}, s16[2,272,128]{2,1,0:T(8,128)(2,1)S(1)}, u32[]{:S(2)}, u32[]{:S(2)}) %collective-permute-start.13) | collective-permute-done | bytes 139296 | tf_op jit(solution)/shard_map/ppermute | solution.py:463
  129.2 3.3 %collective-permute-start.16 = (s16[16,272,128]{2,1,0:T(8,128)(2,1)S(1)}, s16[16,272,128]{2,1,0:T(8,128)(2,1)S(1)}, u32[]{:S(2)}, u32[]{:S(2)}) collective-permute-start(s16[16,272,128]{2,1,0:T(8,128)(2,1)S(1)} %constant_dynamic-update-slice_fusion.3.here), channel_id=1, source_target_pairs={{1,0},{0,1},{3,2},{2,3},{5,4},{4,5},{7,6},{6,7},{9,8},{8,9},{11,10... | collective-permute-start | bytes 3342344 | tf_op jit(solution)/shard_map/ppermute | solution.py:471
  133.2 1.7 %collective-permute-done.16.there = s16[16,272,128]{2,1,0:T(8,128)(2,1)S(1)} collective-permute-done((s16[16,272,128]{2,1,0:T(8,128)(2,1)S(1)}, s16[16,272,128]{2,1,0:T(8,128)(2,1)S(1)}, u32[]{:S(2)}, u32[]{:S(2)}) %collective-permute-start.16) | collective-permute-done | bytes 1114144 | tf_op jit(solution)/shard_map/ppermute | solution.py:471
  134.9 1.0 copy-done.1
  135.9 9.0 %decode.1 = f32[1,32,9,64,64]{4,3,2,1,0:T(8,128)} custom-call(s32[4]{0:T(128)} %pad_add_fusion.2.meta, s16[16,272,128]{2,1,0:T(8,128)(2,1)} %copy-done, s16[16,272,128]{2,1,0:T(8,128)(2,1)} %copy-done.1), custom_call_target="tpu_custom_call" | custom-call | flops 10000000 | bytes 12000000 | tf_op jit(solution)/shard_map/decode/pallas_call | solution.py:389
  (47 shorter events, 2.9 us)
Async XLA Ops:
  1.3 16.1 %copy-start.5 = (f32[5,5,64]{2,1,0:T(8,128)S(1)}, f32[5,5,64]{2,1,0:T(8,128)}, u32[]{:S(2)}) copy-start(f32[5,5,64]{2,1,0:T(8,128)} %param.4) | copy-start | bytes 19204
  9.7 71.0 %collective-permute-start.4 = (bf16[9,96,640]{2,1,0:T(8,128)(2,1)}, bf16[9,96,640]{2,1,0:T(8,128)(2,1)S(1)}, u32[]{:S(2)}, u32[]{:S(2)}) collective-permute-start(bf16[9,96,640]{2,1,0:T(8,128)(2,1)} %get-tuple-element.28), channel_id=1, source_target_pairs={{0,1},{1,2},{2,3},{3,4},{4,5},{5,6},{6,7},{7,8},{8,9},{9,10},{10,1... | collective-permute-start | bytes 3317768 | tf_op jit(solution)/shard_map/ppermute | solution.py:438
  16.0 64.7 %collective-permute-start.5 = (bf16[5,96,1152]{2,1,0:T(8,128)(2,1)}, bf16[5,96,1152]{2,1,0:T(8,128)(2,1)S(1)}, u32[]{:S(2)}, u32[]{:S(2)}) collective-permute-start(bf16[5,96,1152]{2,1,0:T(8,128)(2,1)} %get-tuple-element.29), channel_id=1, source_target_pairs={{0,32},{32,64},{64,96},{96,128},{128,160},{160,192},{192,224},{1,3... | collective-permute-start | bytes 3317768 | tf_op jit(solution)/shard_map/ppermute | solution.py:439
  17.4 35.1 %collective-permute-start = (f32[3,5,64]{2,1,0:T(8,128)S(1)}, f32[3,5,64]{2,1,0:T(8,128)S(1)}, u32[]{:S(2)}, u32[]{:S(2)}) collective-permute-start(f32[3,5,64]{2,1,0:T(8,128)S(1)} %get-tuple-element.40), channel_id=1, source_target_pairs={{0,32},{32,64},{64,96},{96,128},{128,160},{160,192},{192,224},{1,3... | collective-permute-start | bytes 11528 | tf_op jit(solution)/shard_map/ppermute | solution.py:411
  22.3 30.3 %collective-permute-start.1 = (f32[3,5,64]{2,1,0:T(8,128)S(1)}, f32[3,5,64]{2,1,0:T(8,128)S(1)}, u32[]{:S(2)}, u32[]{:S(2)}) collective-permute-start(f32[3,5,64]{2,1,0:T(8,128)S(1)} %get-tuple-element.39), channel_id=1, source_target_pairs={{32,0},{64,32},{96,64},{128,96},{160,128},{192,160},{224,192},{33,... | collective-permute-start | bytes 11528 | tf_op jit(solution)/shard_map/ppermute | solution.py:412
  23.6 57.2 %collective-permute-start.6 = (bf16[5,96,640]{2,1,0:T(8,128)(2,1)}, bf16[5,96,640]{2,1,0:T(8,128)(2,1)S(1)}, u32[]{:S(2)}, u32[]{:S(2)}) collective-permute-start(bf16[5,96,640]{2,1,0:T(8,128)(2,1)} %get-tuple-element.30), channel_id=1, source_target_pairs={{1,32},{2,33},{3,34},{4,35},{5,36},{6,37},{7,38},{8,39},{9,40},{10... | collective-permute-start | bytes 1843208 | tf_op jit(solution)/shard_map/ppermute | solution.py:440
  52.6 11.5 %collective-permute-start.2 = (f32[11,3,64]{2,1,0:T(4,128)S(1)}, f32[11,3,64]{2,1,0:T(4,128)S(1)}, u32[]{:S(2)}, u32[]{:S(2)}) collective-permute-start(f32[11,3,64]{2,1,0:T(4,128)S(1)} %get-tuple-element.35), channel_id=1, source_target_pairs={{0,1},{1,2},{2,3},{3,4},{4,5},{5,6},{6,7},{7,8},{8,9},{9,10},{10,1... | collective-permute-start | bytes 25352 | tf_op jit(solution)/shard_map/ppermute | solution.py:411
  62.2 6.0 %collective-permute-start.3 = (f32[11,3,64]{2,1,0:T(4,128)S(1)}, f32[11,3,64]{2,1,0:T(4,128)S(1)}, u32[]{:S(2)}, u32[]{:S(2)}) collective-permute-start(f32[11,3,64]{2,1,0:T(4,128)S(1)} %get-tuple-element.36), channel_id=1, source_target_pairs={{1,0},{2,1},{3,2},{4,3},{5,4},{6,5},{7,6},{8,7},{9,8},{10,9},{11,1... | collective-permute-start | bytes 25352 | tf_op jit(solution)/shard_map/ppermute | solution.py:412
  80.7 0.8 copy-start.4
  80.7 1.2 copy-start.2
  80.8 1.5 %copy-start.3 = (bf16[5,96,1152]{2,1,0:T(8,128)(2,1)}, bf16[5,96,1152]{2,1,0:T(8,128)(2,1)S(1)}, u32[]{:S(2)}) copy-start(bf16[5,96,1152]{2,1,0:T(8,128)(2,1)S(1)} %collective-permute-done.5.low_x) | copy-start | bytes 3317764
  91.9 4.9 %collective-permute-start.7 = (s16[144,128]{1,0:T(8,128)(2,1)}, s16[144,128]{1,0:T(8,128)(2,1)S(1)}, u32[]{:S(2)}, u32[]{:S(2)}) collective-permute-start(s16[144,128]{1,0:T(8,128)(2,1)} %get-tuple-element.32), channel_id=1, source_target_pairs={{32,0},{64,32},{96,64},{128,96},{160,128},{192,160},{224,192},{33,... | collective-permute-start | bytes 110600 | tf_op jit(solution)/shard_map/ppermute | solution.py:446
  98.3 7.9 %collective-permute-start.8 = (s16[272,128]{1,0:T(8,128)(2,1)S(1)}, s16[272,128]{1,0:T(8,128)(2,1)S(1)}, u32[]{:S(2)}, u32[]{:S(2)}) collective-permute-start(s16[272,128]{1,0:T(8,128)(2,1)S(1)} %get-tuple-element.34), channel_id=1, source_target_pairs={{2,0},{3,1},{4,2},{5,3},{6,4},{7,5},{0,6},{1,7},{10,8},{11,9},{12,... | collective-permute-start | bytes 208904 | tf_op jit(solution)/shard_map/ppermute | solution.py:461
  104.8 5.5 %collective-permute-start.10 = (s16[272,128]{1,0:T(8,128)(2,1)S(1)}, s16[272,128]{1,0:T(8,128)(2,1)S(1)}, u32[]{:S(2)}, u32[]{:S(2)}) collective-permute-start(s16[272,128]{1,0:T(8,128)(2,1)S(1)} %get-tuple-element.34), channel_id=1, source_target_pairs={{6,0},{7,1},{0,2},{1,3},{2,4},{3,5},{4,6},{5,7},{14,8},{15,9},{8,1... | collective-permute-start | bytes 208904 | tf_op jit(solution)/shard_map/ppermute | solution.py:462
  106.2 5.0 %collective-permute-start.9 = (s16[136,128]{1,0:T(8,128)(2,1)S(1)}, s16[136,128]{1,0:T(8,128)(2,1)S(1)}, u32[]{:S(2)}, u32[]{:S(2)}) collective-permute-start(s16[136,128]{1,0:T(8,128)(2,1)S(1)} %slice.61), channel_id=1, source_target_pairs={{2,0},{3,1},{4,2},{5,3},{6,4},{7,5},{0,6},{1,7},{10,8},{11,9},{12,... | collective-permute-start | bytes 104456 | tf_op jit(solution)/shard_map/ppermute | solution.py:463
  110.3 4.9 %collective-permute-start.11 = (s16[136,128]{1,0:T(8,128)(2,1)S(1)}, s16[136,128]{1,0:T(8,128)(2,1)S(1)}, u32[]{:S(2)}, u32[]{:S(2)}) collective-permute-start(s16[136,128]{1,0:T(8,128)(2,1)S(1)} %slice.62), channel_id=1, source_target_pairs={{6,0},{7,1},{0,2},{1,3},{2,4},{3,5},{4,6},{5,7},{14,8},{15,9},{8,1... | collective-permute-start | bytes 104456 | tf_op jit(solution)/shard_map/ppermute | solution.py:464
  115.2 8.6 %collective-permute-start.12 = (s16[4,272,128]{2,1,0:T(8,128)(2,1)S(1)}, s16[4,272,128]{2,1,0:T(8,128)(2,1)S(1)}, u32[]{:S(2)}, u32[]{:S(2)}) collective-permute-start(s16[4,272,128]{2,1,0:T(8,128)(2,1)S(1)} %pad_add_fusion), channel_id=1, source_target_pairs={{8,0},{9,1},{10,2},{11,3},{12,4},{13,5},{14,6},{15,7},{16,8},{17,9... | collective-permute-start | bytes 835592 | tf_op jit(solution)/shard_map/ppermute | solution.py:461
  115.3 8.6 %collective-permute-start.14 = (s16[4,272,128]{2,1,0:T(8,128)(2,1)S(1)}, s16[4,272,128]{2,1,0:T(8,128)(2,1)S(1)}, u32[]{:S(2)}, u32[]{:S(2)}) collective-permute-start(s16[4,272,128]{2,1,0:T(8,128)(2,1)S(1)} %pad_add_fusion), channel_id=1, source_target_pairs={{24,0},{25,1},{26,2},{27,3},{28,4},{29,5},{30,6},{31,7},{0,8},{1,9... | collective-permute-start | bytes 835592 | tf_op jit(solution)/shard_map/ppermute | solution.py:462
  123.8 5.2 %collective-permute-start.13 = (s16[2,272,128]{2,1,0:T(8,128)(2,1)S(1)}, s16[2,272,128]{2,1,0:T(8,128)(2,1)S(1)}, u32[]{:S(2)}, u32[]{:S(2)}) collective-permute-start(s16[2,272,128]{2,1,0:T(8,128)(2,1)S(1)} %slice.63), channel_id=1, source_target_pairs={{8,0},{9,1},{10,2},{11,3},{12,4},{13,5},{14,6},{15,7},{16,8},{17,9... | collective-permute-start | bytes 417800 | tf_op jit(solution)/shard_map/ppermute | solution.py:463
  123.9 5.2 %collective-permute-start.15 = (s16[2,272,128]{2,1,0:T(8,128)(2,1)S(1)}, s16[2,272,128]{2,1,0:T(8,128)(2,1)S(1)}, u32[]{:S(2)}, u32[]{:S(2)}) collective-permute-start(s16[2,272,128]{2,1,0:T(8,128)(2,1)S(1)} %slice.64), channel_id=1, source_target_pairs={{24,0},{25,1},{26,2},{27,3},{28,4},{29,5},{30,6},{31,7},{0,8},{1,9... | collective-permute-start | bytes 417800 | tf_op jit(solution)/shard_map/ppermute | solution.py:464
  129.2 5.7 %copy-start = (s16[16,272,128]{2,1,0:T(8,128)(2,1)}, s16[16,272,128]{2,1,0:T(8,128)(2,1)S(1)}, u32[]{:S(2)}) copy-start(s16[16,272,128]{2,1,0:T(8,128)(2,1)S(1)} %constant_dynamic-update-slice_fusion.3.here) | copy-start | bytes 3342340
  129.2 5.7 %collective-permute-start.16 = (s16[16,272,128]{2,1,0:T(8,128)(2,1)S(1)}, s16[16,272,128]{2,1,0:T(8,128)(2,1)S(1)}, u32[]{:S(2)}, u32[]{:S(2)}) collective-permute-start(s16[16,272,128]{2,1,0:T(8,128)(2,1)S(1)} %constant_dynamic-update-slice_fusion.3.here), channel_id=1, source_target_pairs={{1,0},{0,1},{3,2},{2,3},{5,4},{4,5},{7,6},{6,7},{9,8},{8,9},{11,10... | collective-permute-start | bytes 3342344 | tf_op jit(solution)/shard_map/ppermute | solution.py:471
  134.9 1.0 copy-start.1

commit v2 on v0

v2 whole, which is shorter than its diff:
```python
import functools

import jax
import jax.numpy as jnp
from jax import lax
from jax.experimental import pallas as pl
from jax.experimental.pallas import tpu as pltpu
from jax.sharding import PartitionSpec as P

MARGIN = 2
CX = 5
CY = 5
MASS = 0.5
EXT = 9
STRIP = 5
ABOVE = EXT - STRIP
VEC = 64
NZ = 64
L = 128
ROWS = 96
CODE_MAX = 32767.0
MIB = 1024 * 1024
VMEM = 56 * MIB

NT = (((1,), (1,)), ((), ()))


def pairs(values):
    low = lax.broadcasted_iota(jnp.int32, values[0].shape, 1) < NZ
    out = []
    for at in range(0, len(values), 2):
        first = values[at]
        if at + 1 < len(values):
            second = values[at + 1]
            top = jnp.where(low, first, pltpu.roll(second, NZ, 1))
            bottom = jnp.where(low, pltpu.roll(first, NZ, 1), second)
        else:
            top = jnp.where(low, first, 0.0)
            bottom = jnp.where(low, pltpu.roll(first, NZ, 1), 0.0)
        out.append(jnp.concatenate([top, bottom], axis=0))
    return out


def split(value):
    high = value.astype(jnp.bfloat16)
    low = (value - high.astype(jnp.float32)).astype(jnp.bfloat16)
    return high, low


def pack_kernel(counts, cv, *refs):
    outs, stages, (rows, mask, sems, out_sems) = refs[:4], refs[4:8], refs[8:]
    own, strip, below_a, below_b = stages
    row, col = lax.axis_index("sx"), lax.axis_index("sy")
    count, mirrored = counts[0, 0], 1 - lax.rem(row, 2)
    cells_x, cells_y = CX * lax.axis_size("sx"), CY * lax.axis_size("sy")

    def fetch(a):
        return pltpu.make_async_copy(cv.at[:, a], rows.at[a], sems.at[a])

    def leave(n, a):
        return pltpu.make_async_copy(stages[n].at[a], outs[n].at[a], out_sems.at[n, a])

    @pl.loop(0, EXT)
    def _(a):
        fetch(a).start()

    index01 = lax.broadcasted_iota(jnp.int32, (VEC, L), 0)
    lane = lax.broadcasted_iota(jnp.int32, (VEC // 2, L), 1)
    index2 = lax.broadcasted_iota(jnp.int32, (VEC // 2, L), 0) + jnp.where(lane < NZ, 0, VEC // 2)
    index = jnp.concatenate([index01, index2], axis=0)
    mask[0] = jnp.zeros((ROWS, L), jnp.bfloat16)
    mask[1] = (index < count).astype(jnp.float32).astype(jnp.bfloat16)

    def cells(a):
        fetch(a).wait()
        x = row * CX - MARGIN + a
        in_x = (x >= 0) & (x < cells_x)
        for b in range(EXT):
            place = jnp.where(mirrored == 1, EXT - 1 - b, b)
            y = col * CY - MARGIN + place
            keep = jnp.where(in_x & (y >= 0) & (y < cells_y), 1, 0)
            zero, one, two = (rows[a, component, place] for component in range(3))
            both = jnp.concatenate([zero, one], axis=1)
            last = jnp.concatenate([two[: VEC // 2], two[VEC // 2 :]], axis=1)
            cell = jnp.concatenate([both, last], axis=0) * mask[keep]
            own[a, :, b * L : (b + 1) * L] = cell
            if b < STRIP:
                strip[a, :, b * L : (b + 1) * L] = cell
            yield EXT - 1 - b, cell
        leave(1, a).start()
        leave(0, a).start()

    @pl.loop(0, ABOVE)
    def _(a):
        for _ in cells(a):
            pass

    @pl.loop(ABOVE, EXT)
    def _(a):
        at = a - ABOVE
        for b, cell in cells(a):
            if b < STRIP:
                below_a[at, :, b * L : (b + 1) * L] = cell
            else:
                below_b[at, :, (b - STRIP) * L : (b - STRIP + 1) * L] = cell
        for n in (2, 3):
            leave(n, at).start()

    for n, stage in enumerate(stages):
        @pl.loop(0, stage.shape[0])
        def _(a):
            leave(n, a).wait()


def pack(meta, cv):
    shapes = [
        (EXT, ROWS, EXT * L),
        (EXT, ROWS, STRIP * L),
        (STRIP, ROWS, STRIP * L),
        (STRIP, ROWS, ABOVE * L),
    ]
    anywhere = pl.BlockSpec(memory_space=pl.ANY)
    return pl.pallas_call(
        pack_kernel,
        in_specs=[pl.BlockSpec(memory_space=pltpu.SMEM), anywhere],
        out_specs=[anywhere] * 4,
        out_shape=[jax.ShapeDtypeStruct(shape, jnp.bfloat16) for shape in shapes],
        scratch_shapes=[pltpu.VMEM(shape, jnp.bfloat16) for shape in shapes]
        + [
            pltpu.VMEM((EXT, 3, EXT, VEC, NZ), jnp.bfloat16),
            pltpu.VMEM((2, ROWS, L), jnp.bfloat16),
            pltpu.SemaphoreType.DMA((EXT,)),
            pltpu.SemaphoreType.DMA((4, EXT)),
        ],
        compiler_params=pltpu.CompilerParams(vmem_limit_bytes=VMEM),
        cost_estimate=pl.CostEstimate(flops=4000000000, bytes_accessed=9000000, transcendentals=0),
        name="pack",
    )(meta, cv)


FRAME = EXT + 2


def weights_into(stiff, wx, wy, up, down):
    lane = lax.broadcasted_iota(jnp.int32, (FRAME, L), 1)
    inner = (lane % NZ) < NZ - 1
    wx[...] = jnp.zeros_like(wx)
    wy[...] = jnp.zeros_like(wy)
    for a in range(FRAME):
        here = stiff[a]
        if a > 0:
            other = stiff[a - 1]
            wx[a, :FRAME] = jnp.where((here > 0) & (other > 0), 0.5 * (here + other), 0.0)
        left, right = here[:-1], here[1:]
        wy[a, 1:FRAME] = jnp.where((left > 0) & (right > 0), 0.5 * (left + right), 0.0)
        above = jnp.where(inner, 0.5 * (here + pltpu.roll(here, L - 1, 1)), 0.0)
        up[a, :FRAME] = above
        down[a, :FRAME] = pltpu.roll(above, 1, 1)


def apply_cell(field, weights, a, b, ra, lane_low):
    wx, wy, up, down = weights
    wxa, wxb = wx[a, b : b + 1], wx[a + 1, b : b + 1]
    wya, wyb = wy[a, b : b + 1], wy[a, b + 1 : b + 2]
    upw, dnw = up[a, b : b + 1], down[a, b : b + 1]
    fx = jnp.where(lane_low, 3.0, 1.0)
    fy = jnp.where(lane_low, 1.0, 3.0)

    def at(da, db, rows):
        return field[ra + da, rows, (b + db) * L : (b + db + 1) * L]

    out = []
    for rows, (cx, cy, cz) in ((slice(0, VEC), (fx, fy, 1.0)), (slice(VEC, ROWS), (1.0, 1.0, 3.0))):
        xa, xb, ya, yb, zu, zd = wxa * cx, wxb * cx, wya * cy, wyb * cy, upw * cz, dnw * cz
        diagonal = MASS + (xa + xb) + (ya + yb) + (zu + zd)
        u = at(0, 0, rows)
        total = diagonal * u - xa * at(-1, 0, rows) - xb * at(1, 0, rows)
        total = total - ya * at(0, -1, rows) - yb * at(0, 1, rows)
        total = total - zu * pltpu.roll(u, L - 1, 1) - zd * pltpu.roll(u, 1, 1)
        out.append(total)
    return out


FIRST = FRAME - 1 - STRIP

dot = functools.partial(lax.dot_general, dimension_numbers=NT, preferred_element_type=jnp.float32)


def total(acc):
    return acc[:VEC] + acc[VEC:]


def store_split(target, a, n, value):
    high, low = split(value)
    target[a, :VEC, n * L : (n + 1) * L] = high
    target[a, VEC:, n * L : (n + 1) * L] = low


def own_kernel(
    u, high_y, far, stiff, applied01, applied2a, applied2b, side01, side2, first_tile, first_level, far_block,
    wx, wy, up, down, field, row01, row2a, row2b, acc, acc_y, acc_c,
):
    weights_into(stiff, wx, wy, up, down)
    weights = (wx, wy, up, down)
    lane_low = lax.broadcasted_iota(jnp.int32, (1, L), 1) < NZ
    field[0] = jnp.zeros((ROWS, (FRAME + 1) * L), jnp.float32)
    field[1] = jnp.zeros((ROWS, (FRAME + 1) * L), jnp.float32)
    field[FRAME] = jnp.zeros((ROWS, (FRAME + 1) * L), jnp.float32)

    @pl.loop(0, EXT)
    def _(a):
        field[a + 2, :, 0:L] = jnp.zeros((ROWS, L), jnp.float32)
        field[a + 2, :, L : (EXT + 1) * L] = u[a].astype(jnp.float32)
        field[a + 2, :, (EXT + 1) * L : (FRAME + 1) * L] = jnp.zeros((ROWS, 2 * L), jnp.float32)

    acc[...] = jnp.zeros_like(acc)
    acc_y[...] = jnp.zeros_like(acc_y)

    def applied_row(a, to01, to2a, to2b, at):
        thirds = []
        for b in range(1, FRAME):
            first, third = apply_cell(field, weights, a, b, a + 1, lane_low)
            store_split(to01, at, b - 1, first)
            thirds.append(third)
        for target, cells in ((to2a, thirds[:EXT]), (to2b, thirds[STRIP:])):
            for n, value in enumerate(pairs(cells)):
                store_split(target, at, n, value)

    def contract_row(a, from01, from2a, from2b, at):
        acc[...] += dot(from01[at, :, : EXT * L], u[a - 1, :VEC]) + dot(from2a[at], thirds_of(u, a - 1, EXT))
        acc_y[...] += dot(from01[at, :, FIRST * L :], high_y[a - 1, :VEC]) + dot(
            from2b[at], thirds_of(high_y, a - 1, STRIP)
        )

    def contract_corner(a):
        acc_c[...] += dot(applied01[a, :, FIRST * L :], far[a, :VEC]) + dot(applied2b[a], thirds_of(far, a, STRIP))

    acc_c[...] = jnp.zeros_like(acc_c)
    applied_row(0, applied01, applied2a, applied2b, 0)
    contract_corner(0)

    @pl.loop(1, STRIP)
    def _(a):
        applied_row(a, applied01, applied2a, applied2b, a)
        contract_row(a, applied01, applied2a, applied2b, a)
        contract_corner(a)

    @pl.loop(STRIP, FRAME - 1)
    def _(a):
        applied_row(a, row01, row2a, row2b, a % 2)
        contract_row(a, row01, row2a, row2b, a % 2)

    own_block, block_y = total(acc), total(acc_y)
    level = scale_of(own_block, block_y)
    first_tile[...] = code(lane_join(own_block, block_y), level)
    first_level[...] = jnp.broadcast_to(level, (8, L))
    far_block[...] = total(acc_c)

    wide = slice(4 * L, FRAME * L)
    field[0, :, wide] = jnp.zeros((ROWS, (STRIP + 2) * L), jnp.float32)
    field[1, :, wide] = jnp.zeros((ROWS, (STRIP + 2) * L), jnp.float32)
    for a in range(STRIP):
        field[a + 2, :, 4 * L : 6 * L] = jnp.zeros((ROWS, 2 * L), jnp.float32)
        field[a + 2, :, 6 * L : FRAME * L] = high_y[a].astype(jnp.float32)

    @pl.loop(0, STRIP)
    def _(a):
        thirds = []
        for n in range(STRIP):
            both, third = apply_cell(field, weights, a, n + 5, a + 1, lane_low)
            store_split(side01, a, n, both)
            thirds.append(third)
        for n, value in enumerate(pairs(thirds)):
            store_split(side2, a, n, value)


def own(u, high_y, far, stiff):
    weight = pltpu.VMEM((FRAME, 16, L), jnp.float32)
    half = lambda width, rows=STRIP: (rows, 2 * VEC, width * L)
    acc = pltpu.VMEM((2 * VEC, VEC), jnp.float32)
    return pl.pallas_call(
        own_kernel,
        out_shape=[jax.ShapeDtypeStruct(half(width), jnp.bfloat16) for width in (FRAME - 1, 5, 3, 5, 3)]
        + coded_shapes(1)
        + [jax.ShapeDtypeStruct((VEC, VEC), jnp.float32)],
        scratch_shapes=[weight] * 4
        + [pltpu.VMEM((FRAME + 1, ROWS, (FRAME + 1) * L), jnp.float32)]
        + [pltpu.VMEM(half(width, 2), jnp.bfloat16) for width in (FRAME - 1, 5, 3)]
        + [acc, acc, acc],
        compiler_params=pltpu.CompilerParams(vmem_limit_bytes=26 * MIB),
        cost_estimate=pl.CostEstimate(flops=14000000000, bytes_accessed=30000000, transcendentals=0),
        name="own",
    )(u, high_y, far, stiff)


def coded_shapes(tiles):
    return [jax.ShapeDtypeStruct((VEC, L), jnp.int16)] * tiles + [jax.ShapeDtypeStruct((8, L), jnp.float32)]


def lane_join(left, right):
    return jnp.concatenate([left, right], axis=1)


def scale_of(*blocks):
    largest = functools.reduce(jnp.maximum, [jnp.abs(block) for block in blocks])
    largest = jnp.max(jnp.max(largest, axis=0, keepdims=True), axis=1, keepdims=True)
    return jnp.clip(jnp.ceil(jnp.log2(largest)), -100.0, 120.0)


def code(tile, exponent):
    size = jnp.minimum(jnp.sqrt(jnp.abs(tile) * jnp.exp2(-exponent)) * CODE_MAX, CODE_MAX) + 0.5
    size = size.astype(jnp.int32)
    return jnp.where(tile < 0, -size, size).astype(jnp.int16)


def thirds_of(ref, a, cells):
    third = ref[a, VEC:].astype(jnp.float32)
    third = pairs([third[:, b * L : (b + 1) * L] for b in range(cells)])
    return jnp.concatenate(third, axis=1).astype(jnp.bfloat16)


def bring(sources, slots, sems):
    def copy(n, a):
        return pltpu.make_async_copy(sources[n].at[a], slots[n].at[a], sems.at[n, a])

    def start(which=None):
        for a in range(STRIP):
            for n in range(len(sources)):
                if which is None or n in which:
                    copy(n, a).start()

    def wait(a, which=None):
        for n in range(len(sources)):
            if which is None or n in which:
                copy(n, a).wait()

    return start, wait


def row_shapes(widths):
    return [pltpu.VMEM((STRIP, rows, width * L), jnp.bfloat16) for rows, width in widths]


BELOW = ((2 * VEC, FRAME - 1), (2 * VEC, 5), (2 * VEC, 5), (2 * VEC, 3), (ROWS, STRIP), (ROWS, ABOVE))


def below_kernel(*refs):
    sources, (tile, turned, level), slots, (sems,) = refs[:6], refs[6:9], refs[9:15], refs[15:]
    start, wait = bring(sources, slots, sems)
    start()
    applied01, applied2a, side01, side2, low_a, low_b = slots
    sum_x, sum_d = [], []
    for a in range(STRIP):
        wait(a)
        thirds = [low_a[a, VEC:, b * L : (b + 1) * L].astype(jnp.float32) for b in range(STRIP)]
        thirds += [low_b[a, VEC:, b * L : (b + 1) * L].astype(jnp.float32) for b in range(ABOVE)]
        row = jnp.concatenate(pairs(thirds), axis=1).astype(jnp.bfloat16)
        sum_x += [
            dot(applied01[a, :, : STRIP * L], low_a[a, :VEC]),
            dot(applied01[a, :, STRIP * L : EXT * L], low_b[a, :VEC]),
            dot(applied2a[a], row),
        ]
        row = jnp.concatenate(pairs(thirds[ABOVE:]), axis=1).astype(jnp.bfloat16)
        sum_d += [
            dot(side01[a, :, :L], low_a[a, :VEC, ABOVE * L :]),
            dot(side01[a, :, L:], low_b[a, :VEC]),
            dot(side2[a], row),
        ]
    block_x, block_d = total(sum(sum_x)), total(sum(sum_d))
    exponent = scale_of(block_x, block_d)
    tile[...] = code(lane_join(block_x, block_d), exponent)
    turned[...] = code(lane_join(block_x.T, block_d.T), exponent)
    level[...] = jnp.broadcast_to(exponent, (8, L))


def below(applied01, applied2a, side01, side2, low_a, low_b):
    return pl.pallas_call(
        below_kernel,
        in_specs=[pl.BlockSpec(memory_space=pl.ANY)] * 6,
        out_shape=coded_shapes(2),
        scratch_shapes=row_shapes(BELOW) + [pltpu.SemaphoreType.DMA((6, STRIP))],
        compiler_params=pltpu.CompilerParams(vmem_limit_bytes=VMEM),
        cost_estimate=pl.CostEstimate(flops=2000000000, bytes_accessed=6000000, transcendentals=0),
        name="below",
    )(applied01, applied2a, side01, side2, low_a, low_b)


CORNER = ((2 * VEC, FRAME - 1), (2 * VEC, 3), (ROWS, STRIP))


def corner_kernel(meta, *refs):
    sources, coded, (mine, theirs), slots, (sems, block) = refs[:3], refs[3:9], refs[9:11], refs[11:14], refs[14:]
    far_block, first_tile, first_level, second_tile, second_turned, second_level = coded
    start, wait = bring(sources, slots, sems)
    applied01, applied2b, partner = slots

    @pl.when(meta[0] == 1)
    def _():
        start()
        parts = []
        for a in range(STRIP):
            wait(a)
            parts.append(dot(applied01[a, :, FIRST * L :], partner[a, :VEC]))
            parts.append(dot(applied2b[a], thirds_of(partner, a, STRIP)))
        block[...] = total(sum(parts))

    @pl.when(meta[0] != 1)
    def _():
        block[...] = far_block[...]

    block = block[...]
    exponent = scale_of(block)
    nothing = jnp.zeros((VEC, VEC), jnp.float32)
    mine[:VEC] = first_tile[...]
    mine[VEC : 2 * VEC] = second_tile[...]
    mine[2 * VEC : 3 * VEC] = jnp.zeros((VEC, L), jnp.int16)
    mine[3 * VEC : 4 * VEC] = code(lane_join(block, nothing), exponent)
    theirs[:VEC] = second_turned[...]
    theirs[VEC : 2 * VEC] = code(lane_join(nothing, block.T), exponent)
    row = lax.broadcasted_iota(jnp.int32, (16, L), 0)
    low = lax.broadcasted_iota(jnp.int32, (16, L), 1) < NZ
    first, second = first_level[0:1, 0:1].astype(jnp.int32), second_level[0:1, 0:1].astype(jnp.int32)
    third = exponent.astype(jnp.int32)
    own_levels = jnp.where(row == 0, first, jnp.where(row == 1, second, jnp.where((row == 3) & low, third, 0)))
    their_levels = jnp.where(row == 2, second, jnp.where((row == 3) & ~low, third, 0))
    mine[4 * VEC : 4 * VEC + 16] = own_levels.astype(jnp.int16)
    theirs[2 * VEC : 2 * VEC + 16] = their_levels.astype(jnp.int16)


def corner_and_code(meta, applied01, applied2b, partner_x, coded):
    vmem = pl.BlockSpec(memory_space=pltpu.VMEM)
    anywhere = pl.BlockSpec(memory_space=pl.ANY)
    return pl.pallas_call(
        corner_kernel,
        in_specs=[pl.BlockSpec(memory_space=pltpu.SMEM)] + [anywhere] * 3 + [vmem] * 6,
        out_shape=[
            jax.ShapeDtypeStruct((4 * VEC + 16, L), jnp.int16),
            jax.ShapeDtypeStruct((2 * VEC + 16, L), jnp.int16),
        ],
        scratch_shapes=row_shapes(CORNER)
        + [pltpu.SemaphoreType.DMA((3, STRIP)), pltpu.VMEM((VEC, VEC), jnp.float32)],
        compiler_params=pltpu.CompilerParams(vmem_limit_bytes=VMEM),
        cost_estimate=pl.CostEstimate(flops=1500000000, bytes_accessed=5000000, transcendentals=0),
        name="corner",
    )(meta, applied01, applied2b, partner_x, *coded)


def decode_kernel(meta, here, there, out, blocks, sems, columns):
    mirrored = meta[0] == 1
    my_y, my_z, my_core = meta[1], meta[2], meta[3]
    i_y = jnp.where(mirrored, 3, 5)
    i_yt = jnp.where(mirrored, 5, 3)
    i_c = jnp.where(mirrored, 0, 2)
    i_d = jnp.where(mirrored, 2, 0)
    i_dn = jnp.where(mirrored, 8, 6)
    i_cn = jnp.where(mirrored, 6, 8)
    step = jnp.where(mirrored, -1, 1)

    def spread(ref, c):
        slot = ((c // 8 - my_y) & 3) * 4 + (((c % 8) // 2 - my_z) & 3)
        to_own = (c + step + columns) & (columns - 1)
        to_next = (c - step + columns) & (columns - 1)
        level = jnp.exp2(ref[slot, 4 * VEC : 4 * VEC + 16].astype(jnp.float32)) * (1.0 / (CODE_MAX * CODE_MAX))
        def value(part):
            code = ref[slot, part * VEC : (part + 1) * VEC].astype(jnp.float32)
            return code * jnp.abs(code) * level[part : part + 1]

        tile = value(0)
        blocks[c, 4] = tile[:, :NZ]
        other = tile[:, NZ:]
        blocks[c, i_y] = other
        blocks[to_own, i_yt] = other.T
        tile = value(1)
        blocks[c, 1] = tile[:, :NZ]
        blocks[to_own, i_d] = tile[:, NZ:]
        tile = value(2)
        blocks[c, 7] = tile[:, :NZ]
        blocks[c, i_dn] = tile[:, NZ:]
        tile = value(3)
        blocks[c, i_c] = tile[:, :NZ]
        blocks[to_next, i_cn] = tile[:, NZ:]

    def both(even, odd):
        @pl.loop(0, columns // 2)
        def _(j):
            spread(even, 2 * j)
            spread(odd, 2 * j + 1)

            @pl.when(j >= 2)
            def _():
                copy(j - 1).start()

        copy(0).start()
        copy(columns // 2 - 1).start()

    def copy(j):
        return pltpu.make_async_copy(blocks.at[pl.ds(2 * j, 2)], out.at[0, pl.ds(2 * j, 2)], sems.at[j])

    @pl.when(my_core == 0)
    def _():
        both(here, there)

    @pl.when(my_core != 0)
    def _():
        both(there, here)

    @pl.loop(0, columns // 2)
    def _(j):
        copy(j).wait()


def decode(meta, here, there, columns):
    return pl.pallas_call(
        functools.partial(decode_kernel, columns=columns),
        in_specs=[pl.BlockSpec(memory_space=pltpu.SMEM)] + [pl.BlockSpec(memory_space=pltpu.VMEM)] * 2,
        out_specs=pl.BlockSpec(memory_space=pl.ANY),
        out_shape=jax.ShapeDtypeStruct((1, columns, 9, VEC, VEC), jnp.float32),
        scratch_shapes=[
            pltpu.VMEM((columns, 9, VEC, VEC), jnp.float32),
            pltpu.SemaphoreType.DMA((columns // 2,)),
        ],
        compiler_params=pltpu.CompilerParams(vmem_limit_bytes=20 * MIB),
        cost_estimate=pl.CostEstimate(flops=10000000, bytes_accessed=12000000, transcendentals=0),
        name="decode",
    )(meta, here, there)


def body(coarse_vectors, stiffness, vector_counts):
    rows, columns = lax.axis_size("sx"), lax.axis_size("sy")
    row, col = lax.axis_index("sx"), lax.axis_index("sy")
    mirrored = 1 - row % 2
    cv = jnp.transpose(coarse_vectors, (0, 2, 3, 1, 4))

    def halo(x, axis, dim):
        peers, length, width = lax.axis_size(axis), x.shape[dim], MARGIN + 1
        up = [(i, i + 1) for i in range(peers - 1)]
        down = [(j, i) for i, j in up]
        before = lax.ppermute(lax.slice_in_dim(x, length - width, length, axis=dim), axis, up)
        after = lax.ppermute(lax.slice_in_dim(x, 0, width, axis=dim), axis, down)
        return before, after

    before, after = halo(stiffness, "sx", 0)
    counts, before, after = lax.optimization_barrier((vector_counts, before, after))
    u, strip, down_a, down_b = pack(counts, cv)

    both = ("sx", "sy")
    number = lambda r, c: r * columns + c
    sides, diagonal, partner = [], [], []
    for r in range(rows):
        toward = 1 if r % 2 else -1
        for c in range(columns):
            if 0 <= c + toward < columns:
                sides.append((number(r, c + toward), number(r, c)))
                if c + toward == c ^ 1:
                    partner.append((number(r, c + toward), number(r, c)))
                elif r > 0:
                    diagonal.append((number(r - 1, c + toward), number(r, c)))
    high_y = lax.ppermute(strip, both, sides)
    far = lax.ppermute(down_a, both, diagonal)
    lines, down_a, down_b = lax.optimization_barrier(
        (jnp.concatenate([before, stiffness, after], axis=0), down_a, down_b)
    )
    before, after = halo(lines, "sy", 1)
    next_row = [(r, r + 1) for r in range(rows - 1)]
    low_a = lax.ppermute(down_a, "sx", next_row)
    low_b = lax.ppermute(down_b, "sx", next_row)

    rim = jnp.concatenate([before, lines, after], axis=1)
    rim = jnp.where(mirrored == 1, rim[:, ::-1], rim)
    rim = jnp.concatenate([rim, rim], axis=2)
    applied01, applied2a, applied2b, side01, side2, *first, far_block = own(u, high_y, far, rim)
    low_a, low_b, far_block = lax.optimization_barrier((low_a, low_b, far_block))
    partner_x = lax.ppermute(low_a, both, partner)
    second = below(applied01, applied2a, side01, side2, low_a, low_b)
    near = (col % 2 == 1 - row % 2).astype(jnp.int32)[None]
    mine, theirs = corner_and_code(near, applied01, applied2b, partner_x, (far_block, *first, *second))
    got = lax.ppermute(theirs, "sx", [(r + 1, r) for r in range(rows - 1)])
    pay = mine + jnp.pad(got, ((2 * VEC, 0), (0, 0)))

    def ring(d_y, d_z, d_core):
        out = []
        for target in range(columns):
            y, z, core = target // 8, target % 8 // 2, target % 2
            out.append(((y + d_y) % 4 * 8 + (z + d_z) % 4 * 2 + (core ^ d_core), target))
        return out

    def everyone(x, d_y, d_z):
        return [x] + [lax.ppermute(x, "sy", ring(n * d_y, n * d_z, 0)) for n in (1, 2, 3)]

    line = jnp.stack(everyone(pay, 0, 1))
    here = jnp.concatenate(everyone(line, 1, 0), axis=0)
    there = lax.ppermute(here, "sy", ring(0, 0, 1))
    place = jnp.stack([mirrored, col // 8, col % 8 // 2, col % 2]).astype(jnp.int32)
    return decode(place, here, there, columns)


def solution(mesh):
    return jax.shard_map(
        body,
        mesh=mesh,
        in_specs=(P(None, None, "sx", "sy", None), P("sx", "sy", None), P("sx", "sy")),
        out_specs=P("sx", None, None, None, None),
        check_vma=False,
    )
```

time: 419 us -> 118 us (0.28); the launches traced: 414 us -> 117 us
  waiting for transfers between devices: 233 us -> 36.5 us
  other arithmetic: 55.4 us -> 1.15 us
  matrix products: 42 us -> 0 us
  Pallas kernels: 0 us -> 26.7 us
  local copies, waits for them, and re-layouts: 26.5 us -> 8.95 us
  between operations: 14.8 us -> 0.98 us
    ppermute x8 -> x17, waiting for transfers between devices: 145 us -> 36.5 us  [the longest x6 20.9 us: everyone(): lax.ppermute(x, 'sy', ring(n * d_y, n * d_z, 0))]
    all_gather x1 -> x0, waiting for transfers between devices: 88 us -> none  [body(): return lax.all_gather(ordered[None, None], 'sy', axis=1, tiled=True)]
    dot_general x27 -> x0, matrix products: 42 us -> none  [contract(): jnp.einsum('kxyz,lxyz->kl', applied, piece.astype(jnp.float32), precision...]
    add x2 -> x0, other arithmetic: 27.5 us -> none  [apply_component(): MASS * padded_field + factors[0] * term_x + factors[1] * term_y]
    pallas_call x0 -> x5, Pallas kernels: none -> 26.7 us  [the longest x1 9.29 us: own(): pl.pallas_call(own_kernel, out_shape=[jax.ShapeDtypeStruct(half(width), j...]
    mul x13 -> x0, other arithmetic: 19.6 us -> none  [the longest x1 6 us: apply_component(): flux_z = weight_z * (padded_field[:, :, :, 1:] - padded_field[:, :, :, :-1])]
    slice x4 -> x2, local copies, waits for them, and re-layouts: 13.8 us -> 0.01 us  [the longest x1 0.01 us: halo(): lax.slice_in_dim(x, length - width, length, axis=dim)]
    concatenate x1 -> x3, other arithmetic: 6.7 us -> 0.12 us  [the longest x1 0.09 us: body(): rim = jnp.concatenate([rim, rim], axis=2)]
  transfers between devices with their start and end apart: 9 -> 17, of which waited for: 4 -> 10; matrix products, arithmetic and copies ran while one was open for 17% -> 0% of each run, Pallas kernels for 0% -> 11%
where the time goes in v2:
time: 118 us; the launch traced here: 117 us
  starting transfers between devices  43 us (36%)
  waiting for transfers between devices  36.5 us (31%)
  Pallas kernels  26.7 us (23%)
  local copies, waits for them, and re-layouts  8.95 us (8%)
    ppermute x6, waiting for transfers between devices, everyone(): lax.ppermute(x, 'sy', ring(n * d_y, n * d_z, 0))  20.9 us
    ppermute x6, starting transfers between devices, everyone(): lax.ppermute(x, 'sy', ring(n * d_y, n * d_z, 0))  11.8 us
    pallas_call x1, Pallas kernels, own(): pl.pallas_call(own_kernel, out_shape=[jax.ShapeDtypeStruct(half(width), j...  9.29 us
    unnamed x31, local copies, waits for them, and re-layouts  8.87 us
    ppermute x2, starting transfers between devices, halo(): lax.ppermute(lax.slice_in_dim(x, length - width, length, axis=dim), axis,...  8.17 us
    ppermute x2, waiting for transfers between devices, halo(): after = lax.ppermute(lax.slice_in_dim(x, 0, width, axis=dim), axis, down)  6.96 us
    ppermute x2, starting transfers between devices, halo(): after = lax.ppermute(lax.slice_in_dim(x, 0, width, axis=dim), axis, down)  5.83 us
    pallas_call x1, Pallas kernels, decode(): pl.pallas_call(functools.partial(decode_kernel, columns=columns), in_spec...  5.47 us
  transfers between devices with their start and end apart: 17, of which 10 were waited for; matrix products, arithmetic and copies ran while one was open for 0% of the time, Pallas kernels for 11%

profile of v2, /device:TPU:11, one launch (start us, length us, event | category | flops | bytes accessed | tf_op | source)
XLA Modules:
  0.0 117.2 jit_solution(3685032571045404575)
XLA Ops:
  0.7 3.6 %pack.1 = (bf16[9,96,1152]{2,1,0:T(8,128)(2,1)}, bf16[9,96,640]{2,1,0:T(8,128)(2,1)}, bf16[5,96,640]{2,1,0:T(8,128)(2,1)}, bf16[5,96,512]{2,1,0:T(8,128)(2,1)}) custom-call(s32[1,1]{1,0:T(1,128)S(6)} %copy.10.counts, bf16[3,9,9,64,64]{4,3,2,1,0:T(8,128)(2,1)} %bitcast.18), custom_call_target="tpu_custom_call" | custom-call | flops 4000000000 | bytes 9000000 | tf_op jit(solution)/shard_map/pack/pallas_call | solution.py:123
  4.3 5.5 %collective-permute-start.2 = (bf16[9,96,640]{2,1,0:T(8,128)(2,1)}, bf16[9,96,640]{2,1,0:T(8,128)(2,1)S(1)}, u32[]{:S(2)}, u32[]{:S(2)}) collective-permute-start(bf16[9,96,640]{2,1,0:T(8,128)(2,1)} %get-tuple-element.33), channel_id=1, source_target_pairs={{0,1},{1,2},{2,3},{3,4},{4,5},{5,6},{6,7},{7,8},{8,9},{9,10},{10,1... | collective-permute-start | bytes 3317768 | tf_op jit(solution)/shard_map/ppermute | solution.py:558
  9.8 1.9 %collective-permute-start.1 = (f32[3,5,64]{2,1,0:T(8,128)S(1)}, f32[3,5,64]{2,1,0:T(8,128)S(1)}, u32[]{:S(2)}, u32[]{:S(2)}) collective-permute-start(f32[3,5,64]{2,1,0:T(8,128)S(1)} %get-tuple-element.61), channel_id=1, source_target_pairs={{32,0},{64,32},{96,64},{128,96},{160,128},{192,160},{224,192},{33,... | collective-permute-start | bytes 11528 | tf_op jit(solution)/shard_map/ppermute | solution.py:539
  11.7 3.4 %collective-permute-start = (f32[3,5,64]{2,1,0:T(8,128)S(1)}, f32[3,5,64]{2,1,0:T(8,128)S(1)}, u32[]{:S(2)}, u32[]{:S(2)}) collective-permute-start(f32[3,5,64]{2,1,0:T(8,128)S(1)} %get-tuple-element.62), channel_id=1, source_target_pairs={{0,32},{32,64},{64,96},{96,128},{128,160},{160,192},{192,224},{1,3... | collective-permute-start | bytes 11528 | tf_op jit(solution)/shard_map/ppermute | solution.py:538
  15.8 7.0 %collective-permute-done.1 = f32[3,5,64]{2,1,0:T(8,128)S(1)} collective-permute-done((f32[3,5,64]{2,1,0:T(8,128)S(1)}, f32[3,5,64]{2,1,0:T(8,128)S(1)}, u32[]{:S(2)}, u32[]{:S(2)}) %collective-permute-start.1) | collective-permute-done | bytes 3872 | tf_op jit(solution)/shard_map/ppermute | solution.py:539
  22.9 4.8 %collective-permute-start.4 = (f32[11,3,64]{2,1,0:T(4,128)S(1)}, f32[11,3,64]{2,1,0:T(4,128)S(1)}, u32[]{:S(2)}, u32[]{:S(2)}) collective-permute-start(f32[11,3,64]{2,1,0:T(4,128)S(1)} %get-tuple-element.59), channel_id=1, source_target_pairs={{0,1},{1,2},{2,3},{3,4},{4,5},{5,6},{6,7},{7,8},{8,9},{9,10},{10,1... | collective-permute-start | bytes 25352 | tf_op jit(solution)/shard_map/ppermute | solution.py:538
  27.7 3.9 %collective-permute-start.5 = (f32[11,3,64]{2,1,0:T(4,128)S(1)}, f32[11,3,64]{2,1,0:T(4,128)S(1)}, u32[]{:S(2)}, u32[]{:S(2)}) collective-permute-start(f32[11,3,64]{2,1,0:T(4,128)S(1)} %get-tuple-element.60), channel_id=1, source_target_pairs={{1,0},{2,1},{3,2},{4,3},{5,4},{6,5},{7,6},{8,7},{9,8},{10,9},{11,1... | collective-permute-start | bytes 25352 | tf_op jit(solution)/shard_map/ppermute | solution.py:539
  31.6 1.9 %collective-permute-start.7 = (bf16[5,96,512]{2,1,0:T(8,128)(2,1)}, bf16[5,96,512]{2,1,0:T(8,128)(2,1)S(1)}, u32[]{:S(2)}, u32[]{:S(2)}) collective-permute-start(bf16[5,96,512]{2,1,0:T(8,128)(2,1)} %get-tuple-element.42), channel_id=1, source_target_pairs={{0,32},{32,64},{64,96},{96,128},{128,160},{160,192},{192,224},{1,3... | collective-permute-start | bytes 1474568 | tf_op jit(solution)/shard_map/ppermute | solution.py:566
  33.6 4.2 %collective-permute-start.6 = (bf16[5,96,640]{2,1,0:T(8,128)(2,1)}, bf16[5,96,640]{2,1,0:T(8,128)(2,1)S(1)}, u32[]{:S(2)}, u32[]{:S(2)}) collective-permute-start(bf16[5,96,640]{2,1,0:T(8,128)(2,1)} %get-tuple-element.41), channel_id=1, source_target_pairs={{0,32},{32,64},{64,96},{96,128},{128,160},{160,192},{192,224},{1,3... | collective-permute-start | bytes 1843208 | tf_op jit(solution)/shard_map/ppermute | solution.py:565
  38.0 1.5 %copy-done.5 = bf16[9,96,1152]{2,1,0:T(8,128)(2,1)S(1)} copy-done((bf16[9,96,1152]{2,1,0:T(8,128)(2,1)S(1)}, bf16[9,96,1152]{2,1,0:T(8,128)(2,1)}, u32[]{:S(2)}) %copy-start.5) | copy-done | bytes 1990680
  39.6 9.3 %own.1 = (bf16[5,128,1280]{2,1,0:T(8,128)(2,1)S(1)}, bf16[5,128,640]{2,1,0:T(8,128)(2,1)S(1)}, bf16[5,128,384]{2,1,0:T(8,128)(2,1)S(1)}, bf16[5,128,640]{2,1,0:T...) custom-call(bf16[9,96,1152]{2,1,0:T(8,128)(2,1)S(1)} %copy-done.5, ...), custom_call_target="tpu_custom_call" | custom-call | flops 14000000000 | bytes 30000000 | tf_op jit(solution)/shard_map/own/pallas_call | solution.py:281
  48.9 1.2 copy-done
  50.0 0.9 copy-done.1
  50.9 0.9 copy-done.2
  55.8 1.3 %collective-permute-start.8 = (bf16[5,96,640]{2,1,0:T(8,128)(2,1)S(1)}, bf16[5,96,640]{2,1,0:T(8,128)(2,1)S(1)}, u32[]{:S(2)}, u32[]{:S(2)}) collective-permute-start(bf16[5,96,640]{2,1,0:T(8,128)(2,1)S(1)} %collective-permute-done.6.refs_4_), channel_id=1, source_target_pairs={{0,1},{2,3},{4,5},{6,7},{8,9},{10,11},{12,13},{14,15},{16,17},{18,... | collective-permute-start | bytes 1843208 | tf_op jit(solution)/shard_map/ppermute | solution.py:573
  57.1 4.2 %below.1 = (s16[64,128]{1,0:T(8,128)(2,1)}, s16[64,128]{1,0:T(8,128)(2,1)}, f32[8,128]{1,0:T(8,128)}) custom-call(bf16[5,128,1280]{2,1,0:T(8,128)(2,1)} %copy-done, bf16[5,128,640]{2,1,0:T(8,128)(2,1)} %copy-done.1, bf16[5,128,640]{2,1,0:T(8,128)(2,1)} %copy-done.2, bf16[5,128,384]{2,1,0:T(8,128)(2,1)} %copy-done.3, bf16[5,96,640]{2,1,0:T(8,128)(2,1)} %copy-done.10, ...), custom_call_target="tpu_custom_call" | custom-call | flops 2000000000 | bytes 6000000 | tf_op jit(solution)/shard_map/below/pallas_call | solution.py:377
  61.3 3.0 %collective-permute-done.8.refs_2_ = bf16[5,96,640]{2,1,0:T(8,128)(2,1)S(1)} collective-permute-done((bf16[5,96,640]{2,1,0:T(8,128)(2,1)S(1)}, bf16[5,96,640]{2,1,0:T(8,128)(2,1)S(1)}, u32[]{:S(2)}, u32[]{:S(2)}) %collective-permute-start.8) | collective-permute-done | bytes 614432 | tf_op jit(solution)/shard_map/ppermute | solution.py:573
  64.2 0.8 copy-done.11
  65.1 4.1 %corner.1 = (s16[272,128]{1,0:T(8,128)(2,1)}, s16[144,128]{1,0:T(8,128)(2,1)}) custom-call(s32[1]{0:T(128)} %bitcast.4.meta, bf16[5,128,1280]{2,1,0:T(8,128)(2,1)} %copy-done, bf16[5,128,384]{2,1,0:T(8,128)(2,1)} %copy-done.4, bf16[5,96,640]{2,1,0:T(8,128)(2,1)} %copy-done.11, f32[64,64]{1,0:T(8,128)} %copy-done.6, s16[64,128]{1,0:T(8,128)(2,1)} %copy-done.7, ...), custom_call_target="tpu_custom_call" | custom-call | flops 1500000000 | bytes 5000000 | tf_op jit(solution)/shard_map/corner/pallas_call | solution.py:433
  69.2 2.2 %collective-permute-start.9 = (s16[144,128]{1,0:T(8,128)(2,1)}, s16[144,128]{1,0:T(8,128)(2,1)S(1)}, u32[]{:S(2)}, u32[]{:S(2)}) collective-permute-start(s16[144,128]{1,0:T(8,128)(2,1)} %get-tuple-element.56), channel_id=1, source_target_pairs={{32,0},{64,32},{96,64},{128,96},{160,128},{192,160},{224,192},{33,... | collective-permute-start | bytes 110600 | tf_op jit(solution)/shard_map/ppermute | solution.py:577
  71.4 2.7 %collective-permute-done.9 = s16[144,128]{1,0:T(8,128)(2,1)S(1)} collective-permute-done((s16[144,128]{1,0:T(8,128)(2,1)}, s16[144,128]{1,0:T(8,128)(2,1)S(1)}, u32[]{:S(2)}, u32[]{:S(2)}) %collective-permute-start.9) | collective-permute-done | bytes 36896 | tf_op jit(solution)/shard_map/ppermute | solution.py:577
  74.1 0.9 constant_dynamic-update-slice_fusion.6
  75.0 3.5 %collective-permute-start.12 = (s16[272,128]{1,0:T(8,128)(2,1)S(1)}, s16[272,128]{1,0:T(8,128)(2,1)S(1)}, u32[]{:S(2)}, u32[]{:S(2)}) collective-permute-start(s16[272,128]{1,0:T(8,128)(2,1)S(1)} %get-tuple-element.58), channel_id=1, source_target_pairs={{6,0},{7,1},{0,2},{1,3},{2,4},{3,5},{4,6},{5,7},{14,8},{15,9},{8,1... | collective-permute-start | bytes 208904 | tf_op jit(solution)/shard_map/ppermute | solution.py:588
  78.5 5.0 %collective-permute-start.11 = (s16[272,128]{1,0:T(8,128)(2,1)S(1)}, s16[272,128]{1,0:T(8,128)(2,1)S(1)}, u32[]{:S(2)}, u32[]{:S(2)}) collective-permute-start(s16[272,128]{1,0:T(8,128)(2,1)S(1)} %get-tuple-element.58), channel_id=1, source_target_pairs={{4,0},{5,1},{6,2},{7,3},{0,4},{1,5},{2,6},{3,7},{12,8},{13,9},{14,... | collective-permute-start | bytes 208904 | tf_op jit(solution)/shard_map/ppermute | solution.py:588
  84.1 5.6 %collective-permute-done.11 = s16[272,128]{1,0:T(8,128)(2,1)S(1)} collective-permute-done((s16[272,128]{1,0:T(8,128)(2,1)S(1)}, s16[272,128]{1,0:T(8,128)(2,1)S(1)}, u32[]{:S(2)}, u32[]{:S(2)}) %collective-permute-start.11) | collective-permute-done | bytes 69664 | tf_op jit(solution)/shard_map/ppermute | solution.py:588
  89.8 2.3 %collective-permute-done.10 = s16[272,128]{1,0:T(8,128)(2,1)S(1)} collective-permute-done((s16[272,128]{1,0:T(8,128)(2,1)S(1)}, s16[272,128]{1,0:T(8,128)(2,1)S(1)}, u32[]{:S(2)}, u32[]{:S(2)}) %collective-permute-start.10) | collective-permute-done | bytes 69664 | tf_op jit(solution)/shard_map/ppermute | solution.py:588
  92.1 1.4 %collective-permute-start.15 = (s16[4,272,128]{2,1,0:T(8,128)(2,1)S(1)}, s16[4,272,128]{2,1,0:T(8,128)(2,1)S(1)}, u32[]{:S(2)}, u32[]{:S(2)}) collective-permute-start(s16[4,272,128]{2,1,0:T(8,128)(2,1)S(1)} %pad_add_fusion), channel_id=1, source_target_pairs={{24,0},{25,1},{26,2},{27,3},{28,4},{29,5},{30,6},{31,7},{0,8},{1,9... | collective-permute-start | bytes 835592 | tf_op jit(solution)/shard_map/ppermute | solution.py:588
  94.1 1.2 %collective-permute-start.13 = (s16[4,272,128]{2,1,0:T(8,128)(2,1)S(1)}, s16[4,272,128]{2,1,0:T(8,128)(2,1)S(1)}, u32[]{:S(2)}, u32[]{:S(2)}) collective-permute-start(s16[4,272,128]{2,1,0:T(8,128)(2,1)S(1)} %pad_add_fusion), channel_id=1, source_target_pairs={{8,0},{9,1},{10,2},{11,3},{12,4},{13,5},{14,6},{15,7},{16,8},{17,9... | collective-permute-start | bytes 835592 | tf_op jit(solution)/shard_map/ppermute | solution.py:588
  95.3 12.4 %collective-permute-done.13 = s16[4,272,128]{2,1,0:T(8,128)(2,1)S(1)} collective-permute-done((s16[4,272,128]{2,1,0:T(8,128)(2,1)S(1)}, s16[4,272,128]{2,1,0:T(8,128)(2,1)S(1)}, u32[]{:S(2)}, u32[]{:S(2)}) %collective-permute-start.13) | collective-permute-done | bytes 278560 | tf_op jit(solution)/shard_map/ppermute | solution.py:588
  107.9 1.5 %collective-permute-start.16 = (s16[16,272,128]{2,1,0:T(8,128)(2,1)S(1)}, s16[16,272,128]{2,1,0:T(8,128)(2,1)S(1)}, u32[]{:S(2)}, u32[]{:S(2)}) collective-permute-start(s16[16,272,128]{2,1,0:T(8,128)(2,1)S(1)} %constant_dynamic-update-slice_fusion.here), channel_id=1, source_target_pairs={{1,0},{0,1},{3,2},{2,3},{5,4},{4,5},{7,6},{6,7},{9,8},{8,9},{11,10... | collective-permute-start | bytes 3342344 | tf_op jit(solution)/shard_map/ppermute | solution.py:592
  109.4 2.3 %collective-permute-done.16.there = s16[16,272,128]{2,1,0:T(8,128)(2,1)S(1)} collective-permute-done((s16[16,272,128]{2,1,0:T(8,128)(2,1)S(1)}, s16[16,272,128]{2,1,0:T(8,128)(2,1)S(1)}, u32[]{:S(2)}, u32[]{:S(2)}) %collective-permute-start.16) | collective-permute-done | bytes 1114144 | tf_op jit(solution)/shard_map/ppermute | solution.py:592
  111.8 5.5 %decode.1 = f32[1,32,9,64,64]{4,3,2,1,0:T(8,128)} custom-call(s32[4]{0:T(128)S(1)} %pad_add_fusion.2.meta, s16[16,272,128]{2,1,0:T(8,128)(2,1)S(1)} %constant_dynamic-update-slice_fusion.here, s16[16,272,128]{2,1,0:T(8,128)(2,1)S(1)} %collective-permute-done.16.there), custom_call_target="tpu_custom_call" | custom-call | flops 10000000 | bytes 12000000 | tf_op jit(solution)/shard_map/decode/pallas_call | solution.py:513
  (49 shorter events, 6.5 us)
Async XLA Ops:
  0.7 9.1 %copy-start.9 = (f32[5,5,64]{2,1,0:T(8,128)S(1)}, f32[5,5,64]{2,1,0:T(8,128)}, u32[]{:S(2)}) copy-start(f32[5,5,64]{2,1,0:T(8,128)} %param.4) | copy-start | bytes 19204
  4.3 33.7 %collective-permute-start.2 = (bf16[9,96,640]{2,1,0:T(8,128)(2,1)}, bf16[9,96,640]{2,1,0:T(8,128)(2,1)S(1)}, u32[]{:S(2)}, u32[]{:S(2)}) collective-permute-start(bf16[9,96,640]{2,1,0:T(8,128)(2,1)} %get-tuple-element.33), channel_id=1, source_target_pairs={{0,1},{1,2},{2,3},{3,4},{4,5},{5,6},{6,7},{7,8},{8,9},{9,10},{10,1... | collective-permute-start | bytes 3317768 | tf_op jit(solution)/shard_map/ppermute | solution.py:558
  9.8 13.0 %collective-permute-start.1 = (f32[3,5,64]{2,1,0:T(8,128)S(1)}, f32[3,5,64]{2,1,0:T(8,128)S(1)}, u32[]{:S(2)}, u32[]{:S(2)}) collective-permute-start(f32[3,5,64]{2,1,0:T(8,128)S(1)} %get-tuple-element.61), channel_id=1, source_target_pairs={{32,0},{64,32},{96,64},{128,96},{160,128},{192,160},{224,192},{33,... | collective-permute-start | bytes 11528 | tf_op jit(solution)/shard_map/ppermute | solution.py:539
  11.7 11.2 %collective-permute-start = (f32[3,5,64]{2,1,0:T(8,128)S(1)}, f32[3,5,64]{2,1,0:T(8,128)S(1)}, u32[]{:S(2)}, u32[]{:S(2)}) collective-permute-start(f32[3,5,64]{2,1,0:T(8,128)S(1)} %get-tuple-element.62), channel_id=1, source_target_pairs={{0,32},{32,64},{64,96},{96,128},{128,160},{160,192},{192,224},{1,3... | collective-permute-start | bytes 11528 | tf_op jit(solution)/shard_map/ppermute | solution.py:538
  15.1 22.9 %collective-permute-start.3 = (bf16[5,96,640]{2,1,0:T(8,128)(2,1)}, bf16[5,96,640]{2,1,0:T(8,128)(2,1)S(1)}, u32[]{:S(2)}, u32[]{:S(2)}) collective-permute-start(bf16[5,96,640]{2,1,0:T(8,128)(2,1)} %get-tuple-element.41), channel_id=1, source_target_pairs={{2,33},{4,35},{6,37},{8,39},{10,41},{12,43},{14,45},{16,47},{18,49... | collective-permute-start | bytes 1843208 | tf_op jit(solution)/shard_map/ppermute | solution.py:559
  22.9 10.7 %collective-permute-start.4 = (f32[11,3,64]{2,1,0:T(4,128)S(1)}, f32[11,3,64]{2,1,0:T(4,128)S(1)}, u32[]{:S(2)}, u32[]{:S(2)}) collective-permute-start(f32[11,3,64]{2,1,0:T(4,128)S(1)} %get-tuple-element.59), channel_id=1, source_target_pairs={{0,1},{1,2},{2,3},{3,4},{4,5},{5,6},{6,7},{7,8},{8,9},{9,10},{10,1... | collective-permute-start | bytes 25352 | tf_op jit(solution)/shard_map/ppermute | solution.py:538
  27.7 10.1 %collective-permute-start.5 = (f32[11,3,64]{2,1,0:T(4,128)S(1)}, f32[11,3,64]{2,1,0:T(4,128)S(1)}, u32[]{:S(2)}, u32[]{:S(2)}) collective-permute-start(f32[11,3,64]{2,1,0:T(4,128)S(1)} %get-tuple-element.60), channel_id=1, source_target_pairs={{1,0},{2,1},{3,2},{4,3},{5,4},{6,5},{7,6},{8,7},{9,8},{10,9},{11,1... | collective-permute-start | bytes 25352 | tf_op jit(solution)/shard_map/ppermute | solution.py:539
  31.6 23.6 %collective-permute-start.7 = (bf16[5,96,512]{2,1,0:T(8,128)(2,1)}, bf16[5,96,512]{2,1,0:T(8,128)(2,1)S(1)}, u32[]{:S(2)}, u32[]{:S(2)}) collective-permute-start(bf16[5,96,512]{2,1,0:T(8,128)(2,1)} %get-tuple-element.42), channel_id=1, source_target_pairs={{0,32},{32,64},{64,96},{96,128},{128,160},{160,192},{192,224},{1,3... | collective-permute-start | bytes 1474568 | tf_op jit(solution)/shard_map/ppermute | solution.py:566
  33.6 22.2 %collective-permute-start.6 = (bf16[5,96,640]{2,1,0:T(8,128)(2,1)}, bf16[5,96,640]{2,1,0:T(8,128)(2,1)S(1)}, u32[]{:S(2)}, u32[]{:S(2)}) collective-permute-start(bf16[5,96,640]{2,1,0:T(8,128)(2,1)} %get-tuple-element.41), channel_id=1, source_target_pairs={{0,32},{32,64},{64,96},{96,128},{128,160},{160,192},{192,224},{1,3... | collective-permute-start | bytes 1843208 | tf_op jit(solution)/shard_map/ppermute | solution.py:565
  38.0 1.6 %copy-start.5 = (bf16[9,96,1152]{2,1,0:T(8,128)(2,1)S(1)}, bf16[9,96,1152]{2,1,0:T(8,128)(2,1)}, u32[]{:S(2)}) copy-start(bf16[9,96,1152]{2,1,0:T(8,128)(2,1)} %get-tuple-element.32.u) | copy-start | bytes 5971972
  48.9 1.2 copy-start
  50.0 0.9 copy-start.1
  50.9 0.9 copy-start.2
  51.8 0.8 copy-start.3
  52.6 0.8 copy-start.4
  53.4 0.6 copy-start.6
  54.0 0.6 copy-start.7
  54.6 0.6 copy-start.8
  55.2 1.9 %copy-start.12 = (bf16[5,96,512]{2,1,0:T(8,128)(2,1)}, bf16[5,96,512]{2,1,0:T(8,128)(2,1)S(1)}, u32[]{:S(2)}) copy-start(bf16[5,96,512]{2,1,0:T(8,128)(2,1)S(1)} %collective-permute-done.7.refs_5_) | copy-start | bytes 1474564
  55.8 1.3 %copy-start.10 = (bf16[5,96,640]{2,1,0:T(8,128)(2,1)}, bf16[5,96,640]{2,1,0:T(8,128)(2,1)S(1)}, u32[]{:S(2)}) copy-start(bf16[5,96,640]{2,1,0:T(8,128)(2,1)S(1)} %collective-permute-done.6.refs_4_) | copy-start | bytes 1843204
  55.8 8.5 %collective-permute-start.8 = (bf16[5,96,640]{2,1,0:T(8,128)(2,1)S(1)}, bf16[5,96,640]{2,1,0:T(8,128)(2,1)S(1)}, u32[]{:S(2)}, u32[]{:S(2)}) collective-permute-start(bf16[5,96,640]{2,1,0:T(8,128)(2,1)S(1)} %collective-permute-done.6.refs_4_), channel_id=1, source_target_pairs={{0,1},{2,3},{4,5},{6,7},{8,9},{10,11},{12,13},{14,15},{16,17},{18,... | collective-permute-start | bytes 1843208 | tf_op jit(solution)/shard_map/ppermute | solution.py:573
  64.2 0.8 copy-start.11
  69.2 4.9 %collective-permute-start.9 = (s16[144,128]{1,0:T(8,128)(2,1)}, s16[144,128]{1,0:T(8,128)(2,1)S(1)}, u32[]{:S(2)}, u32[]{:S(2)}) collective-permute-start(s16[144,128]{1,0:T(8,128)(2,1)} %get-tuple-element.56), channel_id=1, source_target_pairs={{32,0},{64,32},{96,64},{128,96},{160,128},{192,160},{224,192},{33,... | collective-permute-start | bytes 110600 | tf_op jit(solution)/shard_map/ppermute | solution.py:577
  75.0 9.1 %collective-permute-start.12 = (s16[272,128]{1,0:T(8,128)(2,1)S(1)}, s16[272,128]{1,0:T(8,128)(2,1)S(1)}, u32[]{:S(2)}, u32[]{:S(2)}) collective-permute-start(s16[272,128]{1,0:T(8,128)(2,1)S(1)} %get-tuple-element.58), channel_id=1, source_target_pairs={{6,0},{7,1},{0,2},{1,3},{2,4},{3,5},{4,6},{5,7},{14,8},{15,9},{8,1... | collective-permute-start | bytes 208904 | tf_op jit(solution)/shard_map/ppermute | solution.py:588
  78.5 11.2 %collective-permute-start.11 = (s16[272,128]{1,0:T(8,128)(2,1)S(1)}, s16[272,128]{1,0:T(8,128)(2,1)S(1)}, u32[]{:S(2)}, u32[]{:S(2)}) collective-permute-start(s16[272,128]{1,0:T(8,128)(2,1)S(1)} %get-tuple-element.58), channel_id=1, source_target_pairs={{4,0},{5,1},{6,2},{7,3},{0,4},{1,5},{2,6},{3,7},{12,8},{13,9},{14,... | collective-permute-start | bytes 208904 | tf_op jit(solution)/shard_map/ppermute | solution.py:588
  83.6 8.5 %collective-permute-start.10 = (s16[272,128]{1,0:T(8,128)(2,1)S(1)}, s16[272,128]{1,0:T(8,128)(2,1)S(1)}, u32[]{:S(2)}, u32[]{:S(2)}) collective-permute-start(s16[272,128]{1,0:T(8,128)(2,1)S(1)} %get-tuple-element.58), channel_id=1, source_target_pairs={{2,0},{3,1},{4,2},{5,3},{6,4},{7,5},{0,6},{1,7},{10,8},{11,9},{12,... | collective-permute-start | bytes 208904 | tf_op jit(solution)/shard_map/ppermute | solution.py:588
  92.1 15.8 %collective-permute-start.15 = (s16[4,272,128]{2,1,0:T(8,128)(2,1)S(1)}, s16[4,272,128]{2,1,0:T(8,128)(2,1)S(1)}, u32[]{:S(2)}, u32[]{:S(2)}) collective-permute-start(s16[4,272,128]{2,1,0:T(8,128)(2,1)S(1)} %pad_add_fusion), channel_id=1, source_target_pairs={{24,0},{25,1},{26,2},{27,3},{28,4},{29,5},{30,6},{31,7},{0,8},{1,9... | collective-permute-start | bytes 835592 | tf_op jit(solution)/shard_map/ppermute | solution.py:588
  93.4 14.4 %collective-permute-start.14 = (s16[4,272,128]{2,1,0:T(8,128)(2,1)S(1)}, s16[4,272,128]{2,1,0:T(8,128)(2,1)S(1)}, u32[]{:S(2)}, u32[]{:S(2)}) collective-permute-start(s16[4,272,128]{2,1,0:T(8,128)(2,1)S(1)} %pad_add_fusion), channel_id=1, source_target_pairs={{16,0},{17,1},{18,2},{19,3},{20,4},{21,5},{22,6},{23,7},{24,8},{25... | collective-permute-start | bytes 835592 | tf_op jit(solution)/shard_map/ppermute | solution.py:588
  94.1 13.7 %collective-permute-start.13 = (s16[4,272,128]{2,1,0:T(8,128)(2,1)S(1)}, s16[4,272,128]{2,1,0:T(8,128)(2,1)S(1)}, u32[]{:S(2)}, u32[]{:S(2)}) collective-permute-start(s16[4,272,128]{2,1,0:T(8,128)(2,1)S(1)} %pad_add_fusion), channel_id=1, source_target_pairs={{8,0},{9,1},{10,2},{11,3},{12,4},{13,5},{14,6},{15,7},{16,8},{17,9... | collective-permute-start | bytes 835592 | tf_op jit(solution)/shard_map/ppermute | solution.py:588
  107.9 3.9 %collective-permute-start.16 = (s16[16,272,128]{2,1,0:T(8,128)(2,1)S(1)}, s16[16,272,128]{2,1,0:T(8,128)(2,1)S(1)}, u32[]{:S(2)}, u32[]{:S(2)}) collective-permute-start(s16[16,272,128]{2,1,0:T(8,128)(2,1)S(1)} %constant_dynamic-update-slice_fusion.here), channel_id=1, source_target_pairs={{1,0},{0,1},{3,2},{2,3},{5,4},{4,5},{7,6},{6,7},{9,8},{8,9},{11,10... | collective-permute-start | bytes 3342344 | tf_op jit(solution)/shard_map/ppermute | solution.py:592

commit v3 on v2

--- a/solution.py
+++ b/solution.py
@@ -445,7 +445,8 @@
     )(meta, applied01, applied2b, partner_x, *coded)
 
 
-def decode_kernel(meta, here, there, out, blocks, sems, columns):
+def decode_kernel(meta, *refs, columns):
+    here, there, (out, blocks, sems) = refs[:4], refs[4:8], refs[8:]
     mirrored = meta[0] == 1
     my_y, my_z, my_core = meta[1], meta[2], meta[3]
     i_y = jnp.where(mirrored, 3, 5)
@@ -456,11 +457,11 @@
     i_cn = jnp.where(mirrored, 6, 8)
     step = jnp.where(mirrored, -1, 1)
 
-    def spread(ref, c):
-        slot = ((c // 8 - my_y) & 3) * 4 + (((c % 8) // 2 - my_z) & 3)
+    def spread(ref, c, slot):
         to_own = (c + step + columns) & (columns - 1)
         to_next = (c - step + columns) & (columns - 1)
         level = jnp.exp2(ref[slot, 4 * VEC : 4 * VEC + 16].astype(jnp.float32)) * (1.0 / (CODE_MAX * CODE_MAX))
+
         def value(part):
             code = ref[slot, part * VEC : (part + 1) * VEC].astype(jnp.float32)
             return code * jnp.abs(code) * level[part : part + 1]
@@ -480,21 +481,27 @@
         blocks[c, i_c] = tile[:, :NZ]
         blocks[to_next, i_cn] = tile[:, NZ:]
 
+    def move(first, count, sem):
+        return pltpu.make_async_copy(blocks.at[pl.ds(first, count)], out.at[0, pl.ds(first, count)], sems.at[sem])
+
+    def inner(n):
+        return move(((my_y + n) & 3) * 8 + 1, 6, n)
+
+    edges = [move(0, 1, 4), move(columns - 1, 1, 5)] + [move(8 * y - 1, 2, 5 + y) for y in (1, 2, 3)]
+
     def both(even, odd):
-        @pl.loop(0, columns // 2)
-        def _(j):
-            spread(even, 2 * j)
-            spread(odd, 2 * j + 1)
-
-            @pl.when(j >= 2)
-            def _():
-                copy(j - 1).start()
-
-        copy(0).start()
-        copy(columns // 2 - 1).start()
-
-    def copy(j):
-        return pltpu.make_async_copy(blocks.at[pl.ds(2 * j, 2)], out.at[0, pl.ds(2 * j, 2)], sems.at[j])
+        for n in range(4):
+            first = ((my_y + n) & 3) * 8
+
+            @pl.loop(0, 2)
+            def _(half):
+                for z in range(2):
+                    z = 2 * half + z
+                    slot = (z - my_z) & 3
+                    spread(even[n], first + 2 * z, slot)
+                    spread(odd[n], first + 2 * z + 1, slot)
+
+            inner(n).start()
 
     @pl.when(my_core == 0)
     def _():
@@ -504,25 +511,23 @@
     def _():
         both(there, here)
 
-    @pl.loop(0, columns // 2)
-    def _(j):
-        copy(j).wait()
+    for copy in edges:
+        copy.start()
+    for copy in [inner(n) for n in range(4)] + edges:
+        copy.wait()
 
 
 def decode(meta, here, there, columns):
     return pl.pallas_call(
         functools.partial(decode_kernel, columns=columns),
-        in_specs=[pl.BlockSpec(memory_space=pltpu.SMEM)] + [pl.BlockSpec(memory_space=pltpu.VMEM)] * 2,
+        in_specs=[pl.BlockSpec(memory_space=pltpu.SMEM)] + [pl.BlockSpec(memory_space=pltpu.VMEM)] * 8,
         out_specs=pl.BlockSpec(memory_space=pl.ANY),
         out_shape=jax.ShapeDtypeStruct((1, columns, 9, VEC, VEC), jnp.float32),
-        scratch_shapes=[
-            pltpu.VMEM((columns, 9, VEC, VEC), jnp.float32),
-            pltpu.SemaphoreType.DMA((columns // 2,)),
-        ],
+        scratch_shapes=[pltpu.VMEM((columns, 9, VEC, VEC), jnp.float32), pltpu.SemaphoreType.DMA((9,))],
         compiler_params=pltpu.CompilerParams(vmem_limit_bytes=20 * MIB),
         cost_estimate=pl.CostEstimate(flops=10000000, bytes_accessed=12000000, transcendentals=0),
         name="decode",
-    )(meta, here, there)
+    )(meta, *here, *there)
 
 
 def body(coarse_vectors, stiffness, vector_counts):
@@ -588,8 +593,8 @@
         return [x] + [lax.ppermute(x, "sy", ring(n * d_y, n * d_z, 0)) for n in (1, 2, 3)]
 
     line = jnp.stack(everyone(pay, 0, 1))
-    here = jnp.concatenate(everyone(line, 1, 0), axis=0)
-    there = lax.ppermute(here, "sy", ring(0, 0, 1))
+    here = everyone(line, 1, 0)
+    there = [lax.ppermute(part, "sy", ring(0, 0, 1)) for part in here]
     place = jnp.stack([mirrored, col // 8, col % 8 // 2, col % 2]).astype(jnp.int32)
     return decode(place, here, there, columns)
 

time: 118 us -> 116 us (0.983)
  waiting for transfers between devices: 36.5 us -> 28.9 us
  starting transfers between devices: 43 us -> 49.3 us
    ppermute x6, waiting for transfers between devices: 20.9 us -> 14.5 us  [everyone(): lax.ppermute(x, 'sy', ring(n * d_y, n * d_z, 0))]
    ppermute x1 -> x4, starting transfers between devices: 1.47 us -> 7.8 us  [body(): there = [lax.ppermute(part, 'sy', ring(0, 0, 1)) for part in here]]
    ppermute x1 -> x4, waiting for transfers between devices: 2.3 us -> 1.1 us  [body(): there = [lax.ppermute(part, 'sy', ring(0, 0, 1)) for part in here]]
    unnamed x31 -> x26, local copies, waits for them, and re-layouts: 8.87 us -> 8.74 us
  transfers between devices with their start and end apart: 17 -> 20, of which waited for: 10 -> 12; matrix products, arithmetic and copies ran while one was open for 0% -> 0% of each run, Pallas kernels for 11% -> 12%
where the time goes in v3:
time: 116 us
  starting transfers between devices  49.3 us (42%)
  waiting for transfers between devices  28.9 us (25%)
  Pallas kernels  26.6 us (23%)
  local copies, waits for them, and re-layouts  8.78 us (8%)
    ppermute x6, waiting for transfers between devices, everyone(): lax.ppermute(x, 'sy', ring(n * d_y, n * d_z, 0))  14.5 us
    ppermute x6, starting transfers between devices, everyone(): lax.ppermute(x, 'sy', ring(n * d_y, n * d_z, 0))  11.8 us
    pallas_call x1, Pallas kernels, own(): pl.pallas_call(own_kernel, out_shape=[jax.ShapeDtypeStruct(half(width), j...  9.29 us
    unnamed x26, local copies, waits for them, and re-layouts  8.74 us
    ppermute x2, starting transfers between devices, halo(): lax.ppermute(lax.slice_in_dim(x, length - width, length, axis=dim), axis,...  8.17 us
    ppermute x4, starting transfers between devices, body(): there = [lax.ppermute(part, 'sy', ring(0, 0, 1)) for part in here]  7.8 us
    ppermute x2, waiting for transfers between devices, halo(): after = lax.ppermute(lax.slice_in_dim(x, 0, width, axis=dim), axis, down)  6.96 us
    ppermute x2, starting transfers between devices, halo(): after = lax.ppermute(lax.slice_in_dim(x, 0, width, axis=dim), axis, down)  5.83 us
  transfers between devices with their start and end apart: 20, of which 12 were waited for; matrix products, arithmetic and copies ran while one was open for 0% of the time, Pallas kernels for 12%

profile of v3, /device:TPU:11, one launch (start us, length us, event | category | flops | bytes accessed | tf_op | source)
XLA Modules:
  0.0 115.8 jit_solution(8059185868596723030)
XLA Ops:
  0.7 3.6 %pack.1 = (bf16[9,96,1152]{2,1,0:T(8,128)(2,1)}, bf16[9,96,640]{2,1,0:T(8,128)(2,1)}, bf16[5,96,640]{2,1,0:T(8,128)(2,1)}, bf16[5,96,512]{2,1,0:T(8,128)(2,1)}) custom-call(s32[1,1]{1,0:T(1,128)S(6)} %copy.4.counts, bf16[3,9,9,64,64]{4,3,2,1,0:T(8,128)(2,1)} %bitcast.14), custom_call_target="tpu_custom_call" | custom-call | flops 4000000000 | bytes 9000000 | tf_op jit(solution)/shard_map/pack/pallas_call | solution.py:123
  4.3 5.5 %collective-permute-start.2 = (bf16[9,96,640]{2,1,0:T(8,128)(2,1)}, bf16[9,96,640]{2,1,0:T(8,128)(2,1)S(1)}, u32[]{:S(2)}, u32[]{:S(2)}) collective-permute-start(bf16[9,96,640]{2,1,0:T(8,128)(2,1)} %get-tuple-element.33), channel_id=1, source_target_pairs={{0,1},{1,2},{2,3},{3,4},{4,5},{5,6},{6,7},{7,8},{8,9},{9,10},{10,1... | collective-permute-start | bytes 3317768 | tf_op jit(solution)/shard_map/ppermute | solution.py:563
  9.8 1.9 %collective-permute-start.1 = (f32[3,5,64]{2,1,0:T(8,128)S(1)}, f32[3,5,64]{2,1,0:T(8,128)S(1)}, u32[]{:S(2)}, u32[]{:S(2)}) collective-permute-start(f32[3,5,64]{2,1,0:T(8,128)S(1)} %get-tuple-element.59), channel_id=1, source_target_pairs={{32,0},{64,32},{96,64},{128,96},{160,128},{192,160},{224,192},{33,... | collective-permute-start | bytes 11528 | tf_op jit(solution)/shard_map/ppermute | solution.py:544
  11.7 3.4 %collective-permute-start = (f32[3,5,64]{2,1,0:T(8,128)S(1)}, f32[3,5,64]{2,1,0:T(8,128)S(1)}, u32[]{:S(2)}, u32[]{:S(2)}) collective-permute-start(f32[3,5,64]{2,1,0:T(8,128)S(1)} %get-tuple-element.60), channel_id=1, source_target_pairs={{0,32},{32,64},{64,96},{96,128},{128,160},{160,192},{192,224},{1,3... | collective-permute-start | bytes 11528 | tf_op jit(solution)/shard_map/ppermute | solution.py:543
  15.8 7.0 %collective-permute-done.1 = f32[3,5,64]{2,1,0:T(8,128)S(1)} collective-permute-done((f32[3,5,64]{2,1,0:T(8,128)S(1)}, f32[3,5,64]{2,1,0:T(8,128)S(1)}, u32[]{:S(2)}, u32[]{:S(2)}) %collective-permute-start.1) | collective-permute-done | bytes 3872 | tf_op jit(solution)/shard_map/ppermute | solution.py:544
  22.9 4.8 %collective-permute-start.4 = (f32[11,3,64]{2,1,0:T(4,128)S(1)}, f32[11,3,64]{2,1,0:T(4,128)S(1)}, u32[]{:S(2)}, u32[]{:S(2)}) collective-permute-start(f32[11,3,64]{2,1,0:T(4,128)S(1)} %get-tuple-element.57), channel_id=1, source_target_pairs={{0,1},{1,2},{2,3},{3,4},{4,5},{5,6},{6,7},{7,8},{8,9},{9,10},{10,1... | collective-permute-start | bytes 25352 | tf_op jit(solution)/shard_map/ppermute | solution.py:543
  27.7 3.9 %collective-permute-start.5 = (f32[11,3,64]{2,1,0:T(4,128)S(1)}, f32[11,3,64]{2,1,0:T(4,128)S(1)}, u32[]{:S(2)}, u32[]{:S(2)}) collective-permute-start(f32[11,3,64]{2,1,0:T(4,128)S(1)} %get-tuple-element.58), channel_id=1, source_target_pairs={{1,0},{2,1},{3,2},{4,3},{5,4},{6,5},{7,6},{8,7},{9,8},{10,9},{11,1... | collective-permute-start | bytes 25352 | tf_op jit(solution)/shard_map/ppermute | solution.py:544
  31.6 1.9 %collective-permute-start.7 = (bf16[5,96,512]{2,1,0:T(8,128)(2,1)}, bf16[5,96,512]{2,1,0:T(8,128)(2,1)S(1)}, u32[]{:S(2)}, u32[]{:S(2)}) collective-permute-start(bf16[5,96,512]{2,1,0:T(8,128)(2,1)} %get-tuple-element.42), channel_id=1, source_target_pairs={{0,32},{32,64},{64,96},{96,128},{128,160},{160,192},{192,224},{1,3... | collective-permute-start | bytes 1474568 | tf_op jit(solution)/shard_map/ppermute | solution.py:571
  33.6 4.2 %collective-permute-start.6 = (bf16[5,96,640]{2,1,0:T(8,128)(2,1)}, bf16[5,96,640]{2,1,0:T(8,128)(2,1)S(1)}, u32[]{:S(2)}, u32[]{:S(2)}) collective-permute-start(bf16[5,96,640]{2,1,0:T(8,128)(2,1)} %get-tuple-element.41), channel_id=1, source_target_pairs={{0,32},{32,64},{64,96},{96,128},{128,160},{160,192},{192,224},{1,3... | collective-permute-start | bytes 1843208 | tf_op jit(solution)/shard_map/ppermute | solution.py:570
  38.0 1.5 %copy-done.5 = bf16[9,96,1152]{2,1,0:T(8,128)(2,1)S(1)} copy-done((bf16[9,96,1152]{2,1,0:T(8,128)(2,1)S(1)}, bf16[9,96,1152]{2,1,0:T(8,128)(2,1)}, u32[]{:S(2)}) %copy-start.5) | copy-done | bytes 1990680
  39.6 9.3 %own.1 = (bf16[5,128,1280]{2,1,0:T(8,128)(2,1)S(1)}, bf16[5,128,640]{2,1,0:T(8,128)(2,1)S(1)}, bf16[5,128,384]{2,1,0:T(8,128)(2,1)S(1)}, bf16[5,128,640]{2,1,0:T...) custom-call(bf16[9,96,1152]{2,1,0:T(8,128)(2,1)S(1)} %copy-done.5, ...), custom_call_target="tpu_custom_call" | custom-call | flops 14000000000 | bytes 30000000 | tf_op jit(solution)/shard_map/own/pallas_call | solution.py:281
  48.9 1.2 copy-done
  55.8 1.3 %collective-permute-start.8 = (bf16[5,96,640]{2,1,0:T(8,128)(2,1)S(1)}, bf16[5,96,640]{2,1,0:T(8,128)(2,1)S(1)}, u32[]{:S(2)}, u32[]{:S(2)}) collective-permute-start(bf16[5,96,640]{2,1,0:T(8,128)(2,1)S(1)} %collective-permute-done.6.refs_4_), channel_id=1, source_target_pairs={{0,1},{2,3},{4,5},{6,7},{8,9},{10,11},{12,13},{14,15},{16,17},{18,... | collective-permute-start | bytes 1843208 | tf_op jit(solution)/shard_map/ppermute | solution.py:578
  57.1 4.1 %below.1 = (s16[64,128]{1,0:T(8,128)(2,1)}, s16[64,128]{1,0:T(8,128)(2,1)}, f32[8,128]{1,0:T(8,128)}) custom-call(bf16[5,128,1280]{2,1,0:T(8,128)(2,1)} %copy-done, bf16[5,128,640]{2,1,0:T(8,128)(2,1)} %copy-done.1, bf16[5,128,640]{2,1,0:T(8,128)(2,1)} %copy-done.2, bf16[5,128,384]{2,1,0:T(8,128)(2,1)} %copy-done.3, bf16[5,96,640]{2,1,0:T(8,128)(2,1)} %copy-done.10, ...), custom_call_target="tpu_custom_call" | custom-call | flops 2000000000 | bytes 6000000 | tf_op jit(solution)/shard_map/below/pallas_call | solution.py:377
  61.3 3.0 %collective-permute-done.8.refs_2_ = bf16[5,96,640]{2,1,0:T(8,128)(2,1)S(1)} collective-permute-done((bf16[5,96,640]{2,1,0:T(8,128)(2,1)S(1)}, bf16[5,96,640]{2,1,0:T(8,128)(2,1)S(1)}, u32[]{:S(2)}, u32[]{:S(2)}) %collective-permute-start.8) | collective-permute-done | bytes 614432 | tf_op jit(solution)/shard_map/ppermute | solution.py:578
  65.1 4.1 %corner.1 = (s16[272,128]{1,0:T(8,128)(2,1)}, s16[144,128]{1,0:T(8,128)(2,1)}) custom-call(s32[1]{0:T(128)} %bitcast.4.meta, bf16[5,128,1280]{2,1,0:T(8,128)(2,1)} %copy-done, bf16[5,128,384]{2,1,0:T(8,128)(2,1)} %copy-done.4, bf16[5,96,640]{2,1,0:T(8,128)(2,1)} %copy-done.11, f32[64,64]{1,0:T(8,128)} %copy-done.6, s16[64,128]{1,0:T(8,128)(2,1)} %copy-done.7, ...), custom_call_target="tpu_custom_call" | custom-call | flops 1500000000 | bytes 5000000 | tf_op jit(solution)/shard_map/corner/pallas_call | solution.py:433
  69.2 2.2 %collective-permute-start.9 = (s16[144,128]{1,0:T(8,128)(2,1)}, s16[144,128]{1,0:T(8,128)(2,1)S(1)}, u32[]{:S(2)}, u32[]{:S(2)}) collective-permute-start(s16[144,128]{1,0:T(8,128)(2,1)} %get-tuple-element.56), channel_id=1, source_target_pairs={{32,0},{64,32},{96,64},{128,96},{160,128},{192,160},{224,192},{33,... | collective-permute-start | bytes 110600 | tf_op jit(solution)/shard_map/ppermute | solution.py:582
  71.4 2.7 %collective-permute-done.9 = s16[144,128]{1,0:T(8,128)(2,1)S(1)} collective-permute-done((s16[144,128]{1,0:T(8,128)(2,1)}, s16[144,128]{1,0:T(8,128)(2,1)S(1)}, u32[]{:S(2)}, u32[]{:S(2)}) %collective-permute-start.9) | collective-permute-done | bytes 36896 | tf_op jit(solution)/shard_map/ppermute | solution.py:582
  75.0 3.5 %collective-permute-start.12 = (s16[272,128]{1,0:T(8,128)(2,1)S(1)}, s16[272,128]{1,0:T(8,128)(2,1)S(1)}, u32[]{:S(2)}, u32[]{:S(2)}) collective-permute-start(s16[272,128]{1,0:T(8,128)(2,1)S(1)} %pad_add_fusion.1), channel_id=1, source_target_pairs={{6,0},{7,1},{0,2},{1,3},{2,4},{3,5},{4,6},{5,7},{14,8},{15,9},{8,1... | collective-permute-start | bytes 208904 | tf_op jit(solution)/shard_map/ppermute | solution.py:593
  78.5 5.0 %collective-permute-start.11 = (s16[272,128]{1,0:T(8,128)(2,1)S(1)}, s16[272,128]{1,0:T(8,128)(2,1)S(1)}, u32[]{:S(2)}, u32[]{:S(2)}) collective-permute-start(s16[272,128]{1,0:T(8,128)(2,1)S(1)} %pad_add_fusion.1), channel_id=1, source_target_pairs={{4,0},{5,1},{6,2},{7,3},{0,4},{1,5},{2,6},{3,7},{12,8},{13,9},{14,... | collective-permute-start | bytes 208904 | tf_op jit(solution)/shard_map/ppermute | solution.py:593
  84.1 5.6 %collective-permute-done.11 = s16[272,128]{1,0:T(8,128)(2,1)S(1)} collective-permute-done((s16[272,128]{1,0:T(8,128)(2,1)S(1)}, s16[272,128]{1,0:T(8,128)(2,1)S(1)}, u32[]{:S(2)}, u32[]{:S(2)}) %collective-permute-start.11) | collective-permute-done | bytes 69664 | tf_op jit(solution)/shard_map/ppermute | solution.py:593
  89.8 2.3 %collective-permute-done.10 = s16[272,128]{1,0:T(8,128)(2,1)S(1)} collective-permute-done((s16[272,128]{1,0:T(8,128)(2,1)S(1)}, s16[272,128]{1,0:T(8,128)(2,1)S(1)}, u32[]{:S(2)}, u32[]{:S(2)}) %collective-permute-start.10) | collective-permute-done | bytes 69664 | tf_op jit(solution)/shard_map/ppermute | solution.py:593
  92.0 1.4 %collective-permute-start.15 = (s16[4,272,128]{2,1,0:T(8,128)(2,1)S(1)}, s16[4,272,128]{2,1,0:T(8,128)(2,1)S(1)}, u32[]{:S(2)}, u32[]{:S(2)}) collective-permute-start(s16[4,272,128]{2,1,0:T(8,128)(2,1)S(1)} %pad_add_fusion.refs_0_), channel_id=1, source_target_pairs={{24,0},{25,1},{26,2},{27,3},{28,4},{29,5},{30,6},{31,7},{0,8},{1,9... | collective-permute-start | bytes 835592 | tf_op jit(solution)/shard_map/ppermute | solution.py:593
  94.1 1.2 %collective-permute-start.13 = (s16[4,272,128]{2,1,0:T(8,128)(2,1)S(1)}, s16[4,272,128]{2,1,0:T(8,128)(2,1)S(1)}, u32[]{:S(2)}, u32[]{:S(2)}) collective-permute-start(s16[4,272,128]{2,1,0:T(8,128)(2,1)S(1)} %pad_add_fusion.refs_0_), channel_id=1, source_target_pairs={{8,0},{9,1},{10,2},{11,3},{12,4},{13,5},{14,6},{15,7},{16,8},{17,9... | collective-permute-start | bytes 835592 | tf_op jit(solution)/shard_map/ppermute | solution.py:593
  95.3 1.1 collective-permute-start.16
  96.4 3.4 %collective-permute-done.15.refs_3_ = s16[4,272,128]{2,1,0:T(8,128)(2,1)S(1)} collective-permute-done((s16[4,272,128]{2,1,0:T(8,128)(2,1)S(1)}, s16[4,272,128]{2,1,0:T(8,128)(2,1)S(1)}, u32[]{:S(2)}, u32[]{:S(2)}) %collective-permute-start.15) | collective-permute-done | bytes 278560 | tf_op jit(solution)/shard_map/ppermute | solution.py:593
  99.8 2.4 %collective-permute-start.19 = (s16[4,272,128]{2,1,0:T(8,128)(2,1)S(1)}, s16[4,272,128]{2,1,0:T(8,128)(2,1)S(1)}, u32[]{:S(2)}, u32[]{:S(2)}) collective-permute-start(s16[4,272,128]{2,1,0:T(8,128)(2,1)S(1)} %collective-permute-done.15.refs_3_), channel_id=1, source_target_pairs={{1,0},{0,1},{3,2},{2,3},{5,4},{4,5},{7,6},{6,7},{9,8},{8,9},{11,10... | collective-permute-start | bytes 835592 | tf_op jit(solution)/shard_map/ppermute | solution.py:597
  102.4 2.9 %collective-permute-start.18 = (s16[4,272,128]{2,1,0:T(8,128)(2,1)S(1)}, s16[4,272,128]{2,1,0:T(8,128)(2,1)S(1)}, u32[]{:S(2)}, u32[]{:S(2)}) collective-permute-start(s16[4,272,128]{2,1,0:T(8,128)(2,1)S(1)} %collective-permute-done.14.refs_2_), channel_id=1, source_target_pairs={{1,0},{0,1},{3,2},{2,3},{5,4},{4,5},{7,6},{6,7},{9,8},{8,9},{11,10... | collective-permute-start | bytes 835592 | tf_op jit(solution)/shard_map/ppermute | solution.py:597
  105.3 2.4 %collective-permute-done.13.refs_1_ = s16[4,272,128]{2,1,0:T(8,128)(2,1)S(1)} collective-permute-done((s16[4,272,128]{2,1,0:T(8,128)(2,1)S(1)}, s16[4,272,128]{2,1,0:T(8,128)(2,1)S(1)}, u32[]{:S(2)}, u32[]{:S(2)}) %collective-permute-start.13) | collective-permute-done | bytes 278560 | tf_op jit(solution)/shard_map/ppermute | solution.py:593
  107.7 1.4 %collective-permute-start.17 = (s16[4,272,128]{2,1,0:T(8,128)(2,1)S(1)}, s16[4,272,128]{2,1,0:T(8,128)(2,1)S(1)}, u32[]{:S(2)}, u32[]{:S(2)}) collective-permute-start(s16[4,272,128]{2,1,0:T(8,128)(2,1)S(1)} %collective-permute-done.13.refs_1_), channel_id=1, source_target_pairs={{1,0},{0,1},{3,2},{2,3},{5,4},{4,5},{7,6},{6,7},{9,8},{8,9},{11,10... | collective-permute-start | bytes 835592 | tf_op jit(solution)/shard_map/ppermute | solution.py:597
  109.2 1.1 collective-permute-done.17.refs_5_
  110.3 5.4 %decode.1 = f32[1,32,9,64,64]{4,3,2,1,0:T(8,128)} custom-call(s32[4]{0:T(128)S(1)} %pad_add_fusion.2.meta, s16[4,272,128]{2,1,0:T(8,128)(2,1)S(1)} %pad_add_fusion.refs_0_, s16[4,272,128]{2,1,0:T(8,128)(2,1)S(1)} %collective-permute-done.13.refs_1_, s16[4,272,128]{2,1,0:T(8,128)(2,1)S(1)} %collective-permute-done.14.refs_2_, ...), custom_call_target="tpu_custom_call" | custom-call | flops 10000000 | bytes 12000000 | tf_op jit(solution)/shard_map/decode/pallas_call | solution.py:521
  (49 shorter events, 10.1 us)
Async XLA Ops:
  0.7 9.1 %copy-start.9 = (f32[5,5,64]{2,1,0:T(8,128)S(1)}, f32[5,5,64]{2,1,0:T(8,128)}, u32[]{:S(2)}) copy-start(f32[5,5,64]{2,1,0:T(8,128)} %param.4) | copy-start | bytes 19204
  4.3 33.7 %collective-permute-start.2 = (bf16[9,96,640]{2,1,0:T(8,128)(2,1)}, bf16[9,96,640]{2,1,0:T(8,128)(2,1)S(1)}, u32[]{:S(2)}, u32[]{:S(2)}) collective-permute-start(bf16[9,96,640]{2,1,0:T(8,128)(2,1)} %get-tuple-element.33), channel_id=1, source_target_pairs={{0,1},{1,2},{2,3},{3,4},{4,5},{5,6},{6,7},{7,8},{8,9},{9,10},{10,1... | collective-permute-start | bytes 3317768 | tf_op jit(solution)/shard_map/ppermute | solution.py:563
  9.8 13.0 %collective-permute-start.1 = (f32[3,5,64]{2,1,0:T(8,128)S(1)}, f32[3,5,64]{2,1,0:T(8,128)S(1)}, u32[]{:S(2)}, u32[]{:S(2)}) collective-permute-start(f32[3,5,64]{2,1,0:T(8,128)S(1)} %get-tuple-element.59), channel_id=1, source_target_pairs={{32,0},{64,32},{96,64},{128,96},{160,128},{192,160},{224,192},{33,... | collective-permute-start | bytes 11528 | tf_op jit(solution)/shard_map/ppermute | solution.py:544
  11.7 11.2 %collective-permute-start = (f32[3,5,64]{2,1,0:T(8,128)S(1)}, f32[3,5,64]{2,1,0:T(8,128)S(1)}, u32[]{:S(2)}, u32[]{:S(2)}) collective-permute-start(f32[3,5,64]{2,1,0:T(8,128)S(1)} %get-tuple-element.60), channel_id=1, source_target_pairs={{0,32},{32,64},{64,96},{96,128},{128,160},{160,192},{192,224},{1,3... | collective-permute-start | bytes 11528 | tf_op jit(solution)/shard_map/ppermute | solution.py:543
  15.1 22.9 %collective-permute-start.3 = (bf16[5,96,640]{2,1,0:T(8,128)(2,1)}, bf16[5,96,640]{2,1,0:T(8,128)(2,1)S(1)}, u32[]{:S(2)}, u32[]{:S(2)}) collective-permute-start(bf16[5,96,640]{2,1,0:T(8,128)(2,1)} %get-tuple-element.41), channel_id=1, source_target_pairs={{2,33},{4,35},{6,37},{8,39},{10,41},{12,43},{14,45},{16,47},{18,49... | collective-permute-start | bytes 1843208 | tf_op jit(solution)/shard_map/ppermute | solution.py:564
  22.9 10.7 %collective-permute-start.4 = (f32[11,3,64]{2,1,0:T(4,128)S(1)}, f32[11,3,64]{2,1,0:T(4,128)S(1)}, u32[]{:S(2)}, u32[]{:S(2)}) collective-permute-start(f32[11,3,64]{2,1,0:T(4,128)S(1)} %get-tuple-element.57), channel_id=1, source_target_pairs={{0,1},{1,2},{2,3},{3,4},{4,5},{5,6},{6,7},{7,8},{8,9},{9,10},{10,1... | collective-permute-start | bytes 25352 | tf_op jit(solution)/shard_map/ppermute | solution.py:543
  27.7 10.1 %collective-permute-start.5 = (f32[11,3,64]{2,1,0:T(4,128)S(1)}, f32[11,3,64]{2,1,0:T(4,128)S(1)}, u32[]{:S(2)}, u32[]{:S(2)}) collective-permute-start(f32[11,3,64]{2,1,0:T(4,128)S(1)} %get-tuple-element.58), channel_id=1, source_target_pairs={{1,0},{2,1},{3,2},{4,3},{5,4},{6,5},{7,6},{8,7},{9,8},{10,9},{11,1... | collective-permute-start | bytes 25352 | tf_op jit(solution)/shard_map/ppermute | solution.py:544
  31.6 23.6 %collective-permute-start.7 = (bf16[5,96,512]{2,1,0:T(8,128)(2,1)}, bf16[5,96,512]{2,1,0:T(8,128)(2,1)S(1)}, u32[]{:S(2)}, u32[]{:S(2)}) collective-permute-start(bf16[5,96,512]{2,1,0:T(8,128)(2,1)} %get-tuple-element.42), channel_id=1, source_target_pairs={{0,32},{32,64},{64,96},{96,128},{128,160},{160,192},{192,224},{1,3... | collective-permute-start | bytes 1474568 | tf_op jit(solution)/shard_map/ppermute | solution.py:571
  33.6 22.2 %collective-permute-start.6 = (bf16[5,96,640]{2,1,0:T(8,128)(2,1)}, bf16[5,96,640]{2,1,0:T(8,128)(2,1)S(1)}, u32[]{:S(2)}, u32[]{:S(2)}) collective-permute-start(bf16[5,96,640]{2,1,0:T(8,128)(2,1)} %get-tuple-element.41), channel_id=1, source_target_pairs={{0,32},{32,64},{64,96},{96,128},{128,160},{160,192},{192,224},{1,3... | collective-permute-start | bytes 1843208 | tf_op jit(solution)/shard_map/ppermute | solution.py:570
  38.0 1.6 %copy-start.5 = (bf16[9,96,1152]{2,1,0:T(8,128)(2,1)S(1)}, bf16[9,96,1152]{2,1,0:T(8,128)(2,1)}, u32[]{:S(2)}) copy-start(bf16[9,96,1152]{2,1,0:T(8,128)(2,1)} %get-tuple-element.32.u) | copy-start | bytes 5971972
  48.9 1.2 %copy-start = (bf16[5,128,1280]{2,1,0:T(8,128)(2,1)}, bf16[5,128,1280]{2,1,0:T(8,128)(2,1)S(1)}, u32[]{:S(2)}) copy-start(bf16[5,128,1280]{2,1,0:T(8,128)(2,1)S(1)} %get-tuple-element.39.refs_0_) | copy-start | bytes 4915204
  50.0 0.9 copy-start.1
  50.9 0.9 copy-start.2
  51.8 0.8 copy-start.3
  52.6 0.8 copy-start.4
  53.4 0.6 copy-start.6
  54.0 0.6 copy-start.7
  55.2 1.9 %copy-start.12 = (bf16[5,96,512]{2,1,0:T(8,128)(2,1)}, bf16[5,96,512]{2,1,0:T(8,128)(2,1)S(1)}, u32[]{:S(2)}) copy-start(bf16[5,96,512]{2,1,0:T(8,128)(2,1)S(1)} %collective-permute-done.7.refs_5_) | copy-start | bytes 1474564
  55.8 1.3 %copy-start.10 = (bf16[5,96,640]{2,1,0:T(8,128)(2,1)}, bf16[5,96,640]{2,1,0:T(8,128)(2,1)S(1)}, u32[]{:S(2)}) copy-start(bf16[5,96,640]{2,1,0:T(8,128)(2,1)S(1)} %collective-permute-done.6.refs_4_) | copy-start | bytes 1843204
  55.8 8.5 %collective-permute-start.8 = (bf16[5,96,640]{2,1,0:T(8,128)(2,1)S(1)}, bf16[5,96,640]{2,1,0:T(8,128)(2,1)S(1)}, u32[]{:S(2)}, u32[]{:S(2)}) collective-permute-start(bf16[5,96,640]{2,1,0:T(8,128)(2,1)S(1)} %collective-permute-done.6.refs_4_), channel_id=1, source_target_pairs={{0,1},{2,3},{4,5},{6,7},{8,9},{10,11},{12,13},{14,15},{16,17},{18,... | collective-permute-start | bytes 1843208 | tf_op jit(solution)/shard_map/ppermute | solution.py:578
  64.2 0.8 copy-start.11
  69.2 4.9 %collective-permute-start.9 = (s16[144,128]{1,0:T(8,128)(2,1)}, s16[144,128]{1,0:T(8,128)(2,1)S(1)}, u32[]{:S(2)}, u32[]{:S(2)}) collective-permute-start(s16[144,128]{1,0:T(8,128)(2,1)} %get-tuple-element.56), channel_id=1, source_target_pairs={{32,0},{64,32},{96,64},{128,96},{160,128},{192,160},{224,192},{33,... | collective-permute-start | bytes 110600 | tf_op jit(solution)/shard_map/ppermute | solution.py:582
  75.0 9.1 %collective-permute-start.12 = (s16[272,128]{1,0:T(8,128)(2,1)S(1)}, s16[272,128]{1,0:T(8,128)(2,1)S(1)}, u32[]{:S(2)}, u32[]{:S(2)}) collective-permute-start(s16[272,128]{1,0:T(8,128)(2,1)S(1)} %pad_add_fusion.1), channel_id=1, source_target_pairs={{6,0},{7,1},{0,2},{1,3},{2,4},{3,5},{4,6},{5,7},{14,8},{15,9},{8,1... | collective-permute-start | bytes 208904 | tf_op jit(solution)/shard_map/ppermute | solution.py:593
  78.5 11.2 %collective-permute-start.11 = (s16[272,128]{1,0:T(8,128)(2,1)S(1)}, s16[272,128]{1,0:T(8,128)(2,1)S(1)}, u32[]{:S(2)}, u32[]{:S(2)}) collective-permute-start(s16[272,128]{1,0:T(8,128)(2,1)S(1)} %pad_add_fusion.1), channel_id=1, source_target_pairs={{4,0},{5,1},{6,2},{7,3},{0,4},{1,5},{2,6},{3,7},{12,8},{13,9},{14,... | collective-permute-start | bytes 208904 | tf_op jit(solution)/shard_map/ppermute | solution.py:593
  83.6 8.5 %collective-permute-start.10 = (s16[272,128]{1,0:T(8,128)(2,1)S(1)}, s16[272,128]{1,0:T(8,128)(2,1)S(1)}, u32[]{:S(2)}, u32[]{:S(2)}) collective-permute-start(s16[272,128]{1,0:T(8,128)(2,1)S(1)} %pad_add_fusion.1), channel_id=1, source_target_pairs={{2,0},{3,1},{4,2},{5,3},{6,4},{7,5},{0,6},{1,7},{10,8},{11,9},{12,... | collective-permute-start | bytes 208904 | tf_op jit(solution)/shard_map/ppermute | solution.py:593
  92.0 7.8 %collective-permute-start.15 = (s16[4,272,128]{2,1,0:T(8,128)(2,1)S(1)}, s16[4,272,128]{2,1,0:T(8,128)(2,1)S(1)}, u32[]{:S(2)}, u32[]{:S(2)}) collective-permute-start(s16[4,272,128]{2,1,0:T(8,128)(2,1)S(1)} %pad_add_fusion.refs_0_), channel_id=1, source_target_pairs={{24,0},{25,1},{26,2},{27,3},{28,4},{29,5},{30,6},{31,7},{0,8},{1,9... | collective-permute-start | bytes 835592 | tf_op jit(solution)/shard_map/ppermute | solution.py:593
  93.4 9.0 %collective-permute-start.14 = (s16[4,272,128]{2,1,0:T(8,128)(2,1)S(1)}, s16[4,272,128]{2,1,0:T(8,128)(2,1)S(1)}, u32[]{:S(2)}, u32[]{:S(2)}) collective-permute-start(s16[4,272,128]{2,1,0:T(8,128)(2,1)S(1)} %pad_add_fusion.refs_0_), channel_id=1, source_target_pairs={{16,0},{17,1},{18,2},{19,3},{20,4},{21,5},{22,6},{23,7},{24,8},{25... | collective-permute-start | bytes 835592 | tf_op jit(solution)/shard_map/ppermute | solution.py:593
  94.1 13.6 %collective-permute-start.13 = (s16[4,272,128]{2,1,0:T(8,128)(2,1)S(1)}, s16[4,272,128]{2,1,0:T(8,128)(2,1)S(1)}, u32[]{:S(2)}, u32[]{:S(2)}) collective-permute-start(s16[4,272,128]{2,1,0:T(8,128)(2,1)S(1)} %pad_add_fusion.refs_0_), channel_id=1, source_target_pairs={{8,0},{9,1},{10,2},{11,3},{12,4},{13,5},{14,6},{15,7},{16,8},{17,9... | collective-permute-start | bytes 835592 | tf_op jit(solution)/shard_map/ppermute | solution.py:593
  95.3 13.9 %collective-permute-start.16 = (s16[4,272,128]{2,1,0:T(8,128)(2,1)S(1)}, s16[4,272,128]{2,1,0:T(8,128)(2,1)S(1)}, u32[]{:S(2)}, u32[]{:S(2)}) collective-permute-start(s16[4,272,128]{2,1,0:T(8,128)(2,1)S(1)} %pad_add_fusion.refs_0_), channel_id=1, source_target_pairs={{1,0},{0,1},{3,2},{2,3},{5,4},{4,5},{7,6},{6,7},{9,8},{8,9},{11,10... | collective-permute-start | bytes 835592 | tf_op jit(solution)/shard_map/ppermute | solution.py:597
  99.8 9.4 %collective-permute-start.19 = (s16[4,272,128]{2,1,0:T(8,128)(2,1)S(1)}, s16[4,272,128]{2,1,0:T(8,128)(2,1)S(1)}, u32[]{:S(2)}, u32[]{:S(2)}) collective-permute-start(s16[4,272,128]{2,1,0:T(8,128)(2,1)S(1)} %collective-permute-done.15.refs_3_), channel_id=1, source_target_pairs={{1,0},{0,1},{3,2},{2,3},{5,4},{4,5},{7,6},{6,7},{9,8},{8,9},{11,10... | collective-permute-start | bytes 835592 | tf_op jit(solution)/shard_map/ppermute | solution.py:597
  102.4 6.8 %collective-permute-start.18 = (s16[4,272,128]{2,1,0:T(8,128)(2,1)S(1)}, s16[4,272,128]{2,1,0:T(8,128)(2,1)S(1)}, u32[]{:S(2)}, u32[]{:S(2)}) collective-permute-start(s16[4,272,128]{2,1,0:T(8,128)(2,1)S(1)} %collective-permute-done.14.refs_2_), channel_id=1, source_target_pairs={{1,0},{0,1},{3,2},{2,3},{5,4},{4,5},{7,6},{6,7},{9,8},{8,9},{11,10... | collective-permute-start | bytes 835592 | tf_op jit(solution)/shard_map/ppermute | solution.py:597
  107.7 2.6 %collective-permute-start.17 = (s16[4,272,128]{2,1,0:T(8,128)(2,1)S(1)}, s16[4,272,128]{2,1,0:T(8,128)(2,1)S(1)}, u32[]{:S(2)}, u32[]{:S(2)}) collective-permute-start(s16[4,272,128]{2,1,0:T(8,128)(2,1)S(1)} %collective-permute-done.13.refs_1_), channel_id=1, source_target_pairs={{1,0},{0,1},{3,2},{2,3},{5,4},{4,5},{7,6},{6,7},{9,8},{8,9},{11,10... | collective-permute-start | bytes 835592 | tf_op jit(solution)/shard_map/ppermute | solution.py:597
  (1 other events, 0.6 us)

commit v4 on v3

--- a/solution.py
+++ b/solution.py
@@ -287,7 +287,7 @@
         + [pltpu.VMEM((FRAME + 1, ROWS, (FRAME + 1) * L), jnp.float32)]
         + [pltpu.VMEM(half(width, 2), jnp.bfloat16) for width in (FRAME - 1, 5, 3)]
         + [acc, acc, acc],
-        compiler_params=pltpu.CompilerParams(vmem_limit_bytes=26 * MIB),
+        compiler_params=pltpu.CompilerParams(vmem_limit_bytes=VMEM),
         cost_estimate=pl.CostEstimate(flops=14000000000, bytes_accessed=30000000, transcendentals=0),
         name="own",
     )(u, high_y, far, stiff)
@@ -530,6 +530,26 @@
     )(meta, *here, *there)
 
 
+def stack_lines_kernel(before, middle, after, lines, left, right):
+    width = MARGIN + 1
+    for first, part in ((0, before), (width, middle), (width + CX, after)):
+        rows = slice(first, first + part.shape[0])
+        lines[rows] = part[...]
+        left[rows] = part[:, :width]
+        right[rows] = part[:, CX - width :]
+
+
+def stack_lines(before, middle, after):
+    rows, width = CX + 2 * (MARGIN + 1), MARGIN + 1
+    return pl.pallas_call(
+        stack_lines_kernel,
+        out_shape=[jax.ShapeDtypeStruct((rows, columns, NZ), jnp.float32) for columns in (CX, width, width)],
+        compiler_params=pltpu.CompilerParams(vmem_limit_bytes=4 * MIB),
+        cost_estimate=pl.CostEstimate(flops=16000000000, bytes_accessed=1000000, transcendentals=0),
+        name="stack_lines",
+    )(before, middle, after)
+
+
 def body(coarse_vectors, stiffness, vector_counts):
     rows, columns = lax.axis_size("sx"), lax.axis_size("sy")
     row, col = lax.axis_index("sx"), lax.axis_index("sy")
@@ -562,10 +582,12 @@
                     diagonal.append((number(r - 1, c + toward), number(r, c)))
     high_y = lax.ppermute(strip, both, sides)
     far = lax.ppermute(down_a, both, diagonal)
-    lines, down_a, down_b = lax.optimization_barrier(
-        (jnp.concatenate([before, stiffness, after], axis=0), down_a, down_b)
-    )
-    before, after = halo(lines, "sy", 1)
+    before, after, down_b = lax.optimization_barrier((before, after, down_b))
+    lines, left, right = stack_lines(before, stiffness, after)
+    along = [(c, c + 1) for c in range(columns - 1)]
+    before = lax.ppermute(right, "sy", along)
+    after = lax.ppermute(left, "sy", [(target, source) for source, target in along])
+    before, after, down_a = lax.optimization_barrier((before, after, down_a))
     next_row = [(r, r + 1) for r in range(rows - 1)]
     low_a = lax.ppermute(down_a, "sx", next_row)
     low_b = lax.ppermute(down_b, "sx", next_row)

time: 116 us -> 116 us (level); the launches traced: 116 us -> 113 us
  local copies, waits for them, and re-layouts: 8.78 us -> 2.84 us
  waiting for transfers between devices: 28.9 us -> 23.4 us
  starting transfers between devices: 49.3 us -> 53.9 us
  Pallas kernels: 26.6 us -> 30.5 us
    ppermute x0 -> x2, waiting for transfers between devices: none -> 8.89 us  [the longest x1 5.77 us: body(): lax.ppermute(left, 'sy', [(target, source) for source, target in along])]
    ppermute x2 -> x1, waiting for transfers between devices: 6.96 us -> 0.01 us  [halo(): after = lax.ppermute(lax.slice_in_dim(x, 0, width, axis=dim), axis, down)]
    unnamed x26 -> x12, local copies, waits for them, and re-layouts: 8.74 us -> 2.02 us
    ppermute x0 -> x2, starting transfers between devices: none -> 6.61 us  [the longest x1 4.55 us: body(): lax.ppermute(left, 'sy', [(target, source) for source, target in along])]
    ppermute x2 -> x1, starting transfers between devices: 8.17 us -> 1.95 us  [halo(): lax.ppermute(lax.slice_in_dim(x, length - width, length, axis=dim), axis,...]
    ppermute x6, waiting for transfers between devices: 14.5 us -> 10.3 us  [everyone(): lax.ppermute(x, 'sy', ring(n * d_y, n * d_z, 0))]
    pallas_call x1, Pallas kernels: 9.29 us -> 13.2 us  [own(): pl.pallas_call(own_kernel, out_shape=[jax.ShapeDtypeStruct(half(width), j...]
    ppermute x1, starting transfers between devices: 2.21 us -> 4.87 us  [body(): got = lax.ppermute(theirs, 'sx', [(r + 1, r) for r in range(rows - 1)])]
  transfers between devices with their start and end apart: 20 -> 20, of which waited for: 12 -> 8; matrix products, arithmetic and copies ran while one was open for 0% -> 1% of each run, Pallas kernels for 12% -> 19%
where the time goes in v4:
time: 116 us; the launch traced here: 113 us
  starting transfers between devices  53.9 us (46%)
  Pallas kernels  30.5 us (26%)
  waiting for transfers between devices  23.4 us (20%)
  local copies, waits for them, and re-layouts  2.84 us (2%)
  other arithmetic  1.77 us (2%)
    pallas_call x1, Pallas kernels, own(): pl.pallas_call(own_kernel, out_shape=[jax.ShapeDtypeStruct(half(width), j...  13.2 us
    ppermute x6, starting transfers between devices, everyone(): lax.ppermute(x, 'sy', ring(n * d_y, n * d_z, 0))  12.2 us
    ppermute x6, waiting for transfers between devices, everyone(): lax.ppermute(x, 'sy', ring(n * d_y, n * d_z, 0))  10.3 us
    ppermute x4, starting transfers between devices, body(): there = [lax.ppermute(part, 'sy', ring(0, 0, 1)) for part in here]  8.49 us
    ppermute x1, starting transfers between devices, body(): high_y = lax.ppermute(strip, both, sides)  7.06 us
    ppermute x1, waiting for transfers between devices, body(): lax.ppermute(left, 'sy', [(target, source) for source, target in along])  5.77 us
    pallas_call x1, Pallas kernels, decode(): pl.pallas_call(functools.partial(decode_kernel, columns=columns), in_spec...  5.38 us
    ppermute x1, starting transfers between devices, body(): got = lax.ppermute(theirs, 'sx', [(r + 1, r) for r in range(rows - 1)])  4.87 us
  transfers between devices with their start and end apart: 20, of which 8 were waited for; matrix products, arithmetic and copies ran while one was open for 1% of the time, Pallas kernels for 19%

profile of v4, /device:TPU:11, one launch (start us, length us, event | category | flops | bytes accessed | tf_op | source)
XLA Modules:
  0.0 113.4 jit_solution(2855288468771118553)
XLA Ops:
  0.8 3.5 %collective-permute-start.1 = (f32[3,5,64]{2,1,0:T(8,128)S(1)}, f32[3,5,64]{2,1,0:T(8,128)S(1)}, u32[]{:S(2)}, u32[]{:S(2)}) collective-permute-start(f32[3,5,64]{2,1,0:T(8,128)S(1)} %get-tuple-element.69), channel_id=1, source_target_pairs={{32,0},{64,32},{96,64},{128,96},{160,128},{192,160},{224,192},{33,... | collective-permute-start | bytes 11528 | tf_op jit(solution)/shard_map/ppermute | solution.py:564
  4.3 1.9 %collective-permute-start = (f32[3,5,64]{2,1,0:T(8,128)S(1)}, f32[3,5,64]{2,1,0:T(8,128)S(1)}, u32[]{:S(2)}, u32[]{:S(2)}) collective-permute-start(f32[3,5,64]{2,1,0:T(8,128)S(1)} %get-tuple-element.70), channel_id=1, source_target_pairs={{0,32},{32,64},{64,96},{96,128},{128,160},{160,192},{192,224},{1,3... | collective-permute-start | bytes 11528 | tf_op jit(solution)/shard_map/ppermute | solution.py:563
  6.9 3.6 %pack.1 = (bf16[9,96,1152]{2,1,0:T(8,128)(2,1)}, bf16[9,96,640]{2,1,0:T(8,128)(2,1)}, bf16[5,96,640]{2,1,0:T(8,128)(2,1)}, bf16[5,96,512]{2,1,0:T(8,128)(2,1)}) custom-call(s32[1,1]{1,0:T(1,128)S(6)} %copy.4.counts, bf16[3,9,9,64,64]{4,3,2,1,0:T(8,128)(2,1)} %bitcast.14), custom_call_target="tpu_custom_call" | custom-call | flops 4000000000 | bytes 9000000 | tf_op jit(solution)/shard_map/pack/pallas_call | solution.py:123
  11.3 7.1 %collective-permute-start.2 = (bf16[9,96,640]{2,1,0:T(8,128)(2,1)}, bf16[9,96,640]{2,1,0:T(8,128)(2,1)S(1)}, u32[]{:S(2)}, u32[]{:S(2)}) collective-permute-start(bf16[9,96,640]{2,1,0:T(8,128)(2,1)} %get-tuple-element.39), channel_id=1, source_target_pairs={{0,1},{1,2},{2,3},{3,4},{4,5},{5,6},{6,7},{7,8},{8,9},{9,10},{10,1... | collective-permute-start | bytes 3317768 | tf_op jit(solution)/shard_map/ppermute | solution.py:583
  18.4 2.1 %collective-permute-start.4 = (f32[11,3,64]{2,1,0:T(4,128)S(1)}, f32[11,3,64]{2,1,0:T(4,128)S(1)}, u32[]{:S(2)}, u32[]{:S(2)}) collective-permute-start(f32[11,3,64]{2,1,0:T(4,128)S(1)} %get-tuple-element.46), channel_id=1, source_target_pairs={{0,1},{1,2},{2,3},{3,4},{4,5},{5,6},{6,7},{7,8},{8,9},{9,10},{10,1... | collective-permute-start | bytes 25352 | tf_op jit(solution)/shard_map/ppermute | solution.py:588
  20.4 4.6 %collective-permute-start.5 = (f32[11,3,64]{2,1,0:T(4,128)S(1)}, f32[11,3,64]{2,1,0:T(4,128)S(1)}, u32[]{:S(2)}, u32[]{:S(2)}) collective-permute-start(f32[11,3,64]{2,1,0:T(4,128)S(1)} %get-tuple-element.47), channel_id=1, source_target_pairs={{1,0},{2,1},{3,2},{4,3},{5,4},{6,5},{7,6},{8,7},{9,8},{10,9},{11,1... | collective-permute-start | bytes 25352 | tf_op jit(solution)/shard_map/ppermute | solution.py:589
  25.0 3.1 %collective-permute-start.7 = (bf16[5,96,512]{2,1,0:T(8,128)(2,1)}, bf16[5,96,512]{2,1,0:T(8,128)(2,1)}, u32[]{:S(2)}, u32[]{:S(2)}) collective-permute-start(bf16[5,96,512]{2,1,0:T(8,128)(2,1)} %get-tuple-element.54), channel_id=1, source_target_pairs={{0,32},{32,64},{64,96},{96,128},{128,160},{160,192},{192,224},{1,3... | collective-permute-start | bytes 1474568 | tf_op jit(solution)/shard_map/ppermute | solution.py:593
  28.1 3.1 %collective-permute-done.4 = f32[11,3,64]{2,1,0:T(4,128)S(1)} collective-permute-done((f32[11,3,64]{2,1,0:T(4,128)S(1)}, f32[11,3,64]{2,1,0:T(4,128)S(1)}, u32[]{:S(2)}, u32[]{:S(2)}) %collective-permute-start.4) | collective-permute-done | bytes 8480 | tf_op jit(solution)/shard_map/ppermute | solution.py:588
  31.3 5.8 %collective-permute-done.5 = f32[11,3,64]{2,1,0:T(4,128)S(1)} collective-permute-done((f32[11,3,64]{2,1,0:T(4,128)S(1)}, f32[11,3,64]{2,1,0:T(4,128)S(1)}, u32[]{:S(2)}, u32[]{:S(2)}) %collective-permute-start.5) | collective-permute-done | bytes 8480 | tf_op jit(solution)/shard_map/ppermute | solution.py:589
  37.1 4.1 %collective-permute-start.6 = (bf16[5,96,640]{2,1,0:T(8,128)(2,1)S(1)}, bf16[5,96,640]{2,1,0:T(8,128)(2,1)S(1)}, u32[]{:S(2)}, u32[]{:S(2)}) collective-permute-start(bf16[5,96,640]{2,1,0:T(8,128)(2,1)S(1)} %copy-done.2), channel_id=1, source_target_pairs={{0,32},{32,64},{64,96},{96,128},{128,160},{160,192},{192,224},{1,3... | collective-permute-start | bytes 1843208 | tf_op jit(solution)/shard_map/ppermute | solution.py:592
  43.1 13.2 %own.1 = (bf16[5,128,1280]{2,1,0:T(8,128)(2,1)}, bf16[5,128,640]{2,1,0:T(8,128)(2,1)}, bf16[5,128,384]{2,1,0:T(8,128)(2,1)}, bf16[5,128,640]{2,1,0:T(8,128)(2,1)...) custom-call(bf16[9,96,1152]{2,1,0:T(8,128)(2,1)} %get-tuple-element.38.u, ...), custom_call_target="tpu_custom_call" | custom-call | flops 14000000000 | bytes 30000000 | tf_op jit(solution)/shard_map/own/pallas_call | solution.py:281
  56.4 1.3 %collective-permute-start.8 = (bf16[5,96,640]{2,1,0:T(8,128)(2,1)S(1)}, bf16[5,96,640]{2,1,0:T(8,128)(2,1)S(1)}, u32[]{:S(2)}, u32[]{:S(2)}) collective-permute-start(bf16[5,96,640]{2,1,0:T(8,128)(2,1)S(1)} %collective-permute-done.6.refs_4_), channel_id=1, source_target_pairs={{0,1},{2,3},{4,5},{6,7},{8,9},{10,11},{12,13},{14,15},{16,17},{18,... | collective-permute-start | bytes 1843208 | tf_op jit(solution)/shard_map/ppermute | solution.py:600
  57.7 4.2 %below.1 = (s16[64,128]{1,0:T(8,128)(2,1)}, s16[64,128]{1,0:T(8,128)(2,1)}, f32[8,128]{1,0:T(8,128)}) custom-call(bf16[5,128,1280]{2,1,0:T(8,128)(2,1)} %get-tuple-element.51.refs_0_, bf16[5,128,640]{2,1,0:T(8,128)(2,1)} %get-tuple-element.60.refs_1_, bf16[5,128,640]{2,1,0:T(8,128)(2,1)} %get-tuple-element.61.refs_2_, ...), custom_call_target="tpu_custom_call" | custom-call | flops 2000000000 | bytes 6000000 | tf_op jit(solution)/shard_map/below/pallas_call | solution.py:377
  61.9 1.1 %collective-permute-done.8.refs_2_ = bf16[5,96,640]{2,1,0:T(8,128)(2,1)S(1)} collective-permute-done((bf16[5,96,640]{2,1,0:T(8,128)(2,1)S(1)}, bf16[5,96,640]{2,1,0:T(8,128)(2,1)S(1)}, u32[]{:S(2)}, u32[]{:S(2)}) %collective-permute-start.8) | collective-permute-done | bytes 614432 | tf_op jit(solution)/shard_map/ppermute | solution.py:600
  63.8 4.1 %corner.1 = (s16[272,128]{1,0:T(8,128)(2,1)}, s16[144,128]{1,0:T(8,128)(2,1)}) custom-call(s32[1]{0:T(128)} %bitcast.4.meta, bf16[5,128,1280]{2,1,0:T(8,128)(2,1)} %get-tuple-element.51.refs_0_, bf16[5,128,384]{2,1,0:T(8,128)(2,1)} %get-tuple-element.52.refs_1_, bf16[5,96,640]{2,1,0:T(8,128)(2,1)} %copy-done.5, f32[64,64]{1,0:T(8,128)} %get-tuple-element.57.refs_3_, ...), custom_call_target="tpu_custom_call" | custom-call | flops 1500000000 | bytes 5000000 | tf_op jit(solution)/shard_map/corner/pallas_call | solution.py:433
  68.0 4.9 %collective-permute-start.9 = (s16[144,128]{1,0:T(8,128)(2,1)}, s16[144,128]{1,0:T(8,128)(2,1)S(1)}, u32[]{:S(2)}, u32[]{:S(2)}) collective-permute-start(s16[144,128]{1,0:T(8,128)(2,1)} %get-tuple-element.68), channel_id=1, source_target_pairs={{32,0},{64,32},{96,64},{128,96},{160,128},{192,160},{224,192},{33,... | collective-permute-start | bytes 110600 | tf_op jit(solution)/shard_map/ppermute | solution.py:604
  72.8 1.9 %collective-permute-done.9 = s16[144,128]{1,0:T(8,128)(2,1)S(1)} collective-permute-done((s16[144,128]{1,0:T(8,128)(2,1)}, s16[144,128]{1,0:T(8,128)(2,1)S(1)}, u32[]{:S(2)}, u32[]{:S(2)}) %collective-permute-start.9) | collective-permute-done | bytes 36896 | tf_op jit(solution)/shard_map/ppermute | solution.py:604
  75.6 4.6 %collective-permute-start.12 = (s16[272,128]{1,0:T(8,128)(2,1)S(1)}, s16[272,128]{1,0:T(8,128)(2,1)S(1)}, u32[]{:S(2)}, u32[]{:S(2)}) collective-permute-start(s16[272,128]{1,0:T(8,128)(2,1)S(1)} %pad_add_fusion.1), channel_id=1, source_target_pairs={{6,0},{7,1},{0,2},{1,3},{2,4},{3,5},{4,6},{5,7},{14,8},{15,9},{8,1... | collective-permute-start | bytes 208904 | tf_op jit(solution)/shard_map/ppermute | solution.py:615
  80.2 0.9 collective-permute-start.11
  81.1 2.5 %collective-permute-start.10 = (s16[272,128]{1,0:T(8,128)(2,1)S(1)}, s16[272,128]{1,0:T(8,128)(2,1)S(1)}, u32[]{:S(2)}, u32[]{:S(2)}) collective-permute-start(s16[272,128]{1,0:T(8,128)(2,1)S(1)} %pad_add_fusion.1), channel_id=1, source_target_pairs={{2,0},{3,1},{4,2},{5,3},{6,4},{7,5},{0,6},{1,7},{10,8},{11,9},{12,... | collective-permute-start | bytes 208904 | tf_op jit(solution)/shard_map/ppermute | solution.py:615
  83.6 5.7 %collective-permute-done.11 = s16[272,128]{1,0:T(8,128)(2,1)S(1)} collective-permute-done((s16[272,128]{1,0:T(8,128)(2,1)S(1)}, s16[272,128]{1,0:T(8,128)(2,1)S(1)}, u32[]{:S(2)}, u32[]{:S(2)}) %collective-permute-start.11) | collective-permute-done | bytes 69664 | tf_op jit(solution)/shard_map/ppermute | solution.py:615
  89.3 1.4 %collective-permute-start.15 = (s16[4,272,128]{2,1,0:T(8,128)(2,1)S(1)}, s16[4,272,128]{2,1,0:T(8,128)(2,1)S(1)}, u32[]{:S(2)}, u32[]{:S(2)}) collective-permute-start(s16[4,272,128]{2,1,0:T(8,128)(2,1)S(1)} %pad_add_fusion.refs_0_), channel_id=1, source_target_pairs={{24,0},{25,1},{26,2},{27,3},{28,4},{29,5},{30,6},{31,7},{0,8},{1,9... | collective-permute-start | bytes 835592 | tf_op jit(solution)/shard_map/ppermute | solution.py:615
  90.7 0.9 collective-permute-start.14
  91.7 1.9 %collective-permute-start.13 = (s16[4,272,128]{2,1,0:T(8,128)(2,1)S(1)}, s16[4,272,128]{2,1,0:T(8,128)(2,1)S(1)}, u32[]{:S(2)}, u32[]{:S(2)}) collective-permute-start(s16[4,272,128]{2,1,0:T(8,128)(2,1)S(1)} %pad_add_fusion.refs_0_), channel_id=1, source_target_pairs={{8,0},{9,1},{10,2},{11,3},{12,4},{13,5},{14,6},{15,7},{16,8},{17,9... | collective-permute-start | bytes 835592 | tf_op jit(solution)/shard_map/ppermute | solution.py:615
  93.6 1.5 %collective-permute-start.16 = (s16[4,272,128]{2,1,0:T(8,128)(2,1)S(1)}, s16[4,272,128]{2,1,0:T(8,128)(2,1)S(1)}, u32[]{:S(2)}, u32[]{:S(2)}) collective-permute-start(s16[4,272,128]{2,1,0:T(8,128)(2,1)S(1)} %pad_add_fusion.refs_0_), channel_id=1, source_target_pairs={{1,0},{0,1},{3,2},{2,3},{5,4},{4,5},{7,6},{6,7},{9,8},{8,9},{11,10... | collective-permute-start | bytes 835592 | tf_op jit(solution)/shard_map/ppermute | solution.py:619
  95.1 1.8 %collective-permute-done.15.refs_3_ = s16[4,272,128]{2,1,0:T(8,128)(2,1)S(1)} collective-permute-done((s16[4,272,128]{2,1,0:T(8,128)(2,1)S(1)}, s16[4,272,128]{2,1,0:T(8,128)(2,1)S(1)}, u32[]{:S(2)}, u32[]{:S(2)}) %collective-permute-start.15) | collective-permute-done | bytes 278560 | tf_op jit(solution)/shard_map/ppermute | solution.py:615
  96.9 2.7 %collective-permute-start.19 = (s16[4,272,128]{2,1,0:T(8,128)(2,1)S(1)}, s16[4,272,128]{2,1,0:T(8,128)(2,1)S(1)}, u32[]{:S(2)}, u32[]{:S(2)}) collective-permute-start(s16[4,272,128]{2,1,0:T(8,128)(2,1)S(1)} %collective-permute-done.15.refs_3_), channel_id=1, source_target_pairs={{1,0},{0,1},{3,2},{2,3},{5,4},{4,5},{7,6},{6,7},{9,8},{8,9},{11,10... | collective-permute-start | bytes 835592 | tf_op jit(solution)/shard_map/ppermute | solution.py:619
  99.7 3.1 %collective-permute-start.18 = (s16[4,272,128]{2,1,0:T(8,128)(2,1)S(1)}, s16[4,272,128]{2,1,0:T(8,128)(2,1)S(1)}, u32[]{:S(2)}, u32[]{:S(2)}) collective-permute-start(s16[4,272,128]{2,1,0:T(8,128)(2,1)S(1)} %collective-permute-done.14.refs_2_), channel_id=1, source_target_pairs={{1,0},{0,1},{3,2},{2,3},{5,4},{4,5},{7,6},{6,7},{9,8},{8,9},{11,10... | collective-permute-start | bytes 835592 | tf_op jit(solution)/shard_map/ppermute | solution.py:619
  102.8 2.8 %collective-permute-done.13.refs_1_ = s16[4,272,128]{2,1,0:T(8,128)(2,1)S(1)} collective-permute-done((s16[4,272,128]{2,1,0:T(8,128)(2,1)S(1)}, s16[4,272,128]{2,1,0:T(8,128)(2,1)S(1)}, u32[]{:S(2)}, u32[]{:S(2)}) %collective-permute-start.13) | collective-permute-done | bytes 278560 | tf_op jit(solution)/shard_map/ppermute | solution.py:615
  105.6 1.1 collective-permute-start.17
  106.8 1.1 collective-permute-done.17.refs_5_
  107.9 5.4 %decode.1 = f32[1,32,9,64,64]{4,3,2,1,0:T(8,128)} custom-call(s32[4]{0:T(128)S(1)} %pad_add_fusion.2.meta, s16[4,272,128]{2,1,0:T(8,128)(2,1)S(1)} %pad_add_fusion.refs_0_, s16[4,272,128]{2,1,0:T(8,128)(2,1)S(1)} %collective-permute-done.13.refs_1_, s16[4,272,128]{2,1,0:T(8,128)(2,1)S(1)} %collective-permute-done.14.refs_2_, ...), custom_call_target="tpu_custom_call" | custom-call | flops 10000000 | bytes 12000000 | tf_op jit(solution)/shard_map/decode/pallas_call | solution.py:521
  (34 shorter events, 5.4 us)
Async XLA Ops:
  0.8 17.5 %collective-permute-start.1 = (f32[3,5,64]{2,1,0:T(8,128)S(1)}, f32[3,5,64]{2,1,0:T(8,128)S(1)}, u32[]{:S(2)}, u32[]{:S(2)}) collective-permute-start(f32[3,5,64]{2,1,0:T(8,128)S(1)} %get-tuple-element.69), channel_id=1, source_target_pairs={{32,0},{64,32},{96,64},{128,96},{160,128},{192,160},{224,192},{33,... | collective-permute-start | bytes 11528 | tf_op jit(solution)/shard_map/ppermute | solution.py:564
  4.3 14.0 %collective-permute-start = (f32[3,5,64]{2,1,0:T(8,128)S(1)}, f32[3,5,64]{2,1,0:T(8,128)S(1)}, u32[]{:S(2)}, u32[]{:S(2)}) collective-permute-start(f32[3,5,64]{2,1,0:T(8,128)S(1)} %get-tuple-element.70), channel_id=1, source_target_pairs={{0,32},{32,64},{64,96},{96,128},{128,160},{160,192},{192,224},{1,3... | collective-permute-start | bytes 11528 | tf_op jit(solution)/shard_map/ppermute | solution.py:563
  6.9 11.4 %copy-start = (f32[5,5,64]{2,1,0:T(8,128)S(1)}, f32[5,5,64]{2,1,0:T(8,128)}, u32[]{:S(2)}) copy-start(f32[5,5,64]{2,1,0:T(8,128)} %middle.1) | copy-start | bytes 19204
  10.6 31.4 %collective-permute-start.3 = (bf16[5,96,640]{2,1,0:T(8,128)(2,1)}, bf16[5,96,640]{2,1,0:T(8,128)(2,1)S(1)}, u32[]{:S(2)}, u32[]{:S(2)}) collective-permute-start(bf16[5,96,640]{2,1,0:T(8,128)(2,1)} %get-tuple-element.53), channel_id=1, source_target_pairs={{2,33},{4,35},{6,37},{8,39},{10,41},{12,43},{14,45},{16,47},{18,49... | collective-permute-start | bytes 1843208 | tf_op jit(solution)/shard_map/ppermute | solution.py:584
  11.3 30.7 %collective-permute-start.2 = (bf16[9,96,640]{2,1,0:T(8,128)(2,1)}, bf16[9,96,640]{2,1,0:T(8,128)(2,1)S(1)}, u32[]{:S(2)}, u32[]{:S(2)}) collective-permute-start(bf16[9,96,640]{2,1,0:T(8,128)(2,1)} %get-tuple-element.39), channel_id=1, source_target_pairs={{0,1},{1,2},{2,3},{3,4},{4,5},{5,6},{6,7},{7,8},{8,9},{9,10},{10,1... | collective-permute-start | bytes 3317768 | tf_op jit(solution)/shard_map/ppermute | solution.py:583
  18.4 18.7 %copy-start.2 = (bf16[5,96,640]{2,1,0:T(8,128)(2,1)S(1)}, bf16[5,96,640]{2,1,0:T(8,128)(2,1)}, u32[]{:S(2)}) copy-start(bf16[5,96,640]{2,1,0:T(8,128)(2,1)} %get-tuple-element.53) | copy-start | bytes 1843204
  18.4 12.9 %collective-permute-start.4 = (f32[11,3,64]{2,1,0:T(4,128)S(1)}, f32[11,3,64]{2,1,0:T(4,128)S(1)}, u32[]{:S(2)}, u32[]{:S(2)}) collective-permute-start(f32[11,3,64]{2,1,0:T(4,128)S(1)} %get-tuple-element.46), channel_id=1, source_target_pairs={{0,1},{1,2},{2,3},{3,4},{4,5},{5,6},{6,7},{7,8},{8,9},{9,10},{10,1... | collective-permute-start | bytes 25352 | tf_op jit(solution)/shard_map/ppermute | solution.py:588
  20.4 16.6 %collective-permute-start.5 = (f32[11,3,64]{2,1,0:T(4,128)S(1)}, f32[11,3,64]{2,1,0:T(4,128)S(1)}, u32[]{:S(2)}, u32[]{:S(2)}) collective-permute-start(f32[11,3,64]{2,1,0:T(4,128)S(1)} %get-tuple-element.47), channel_id=1, source_target_pairs={{1,0},{2,1},{3,2},{4,3},{5,4},{6,5},{7,6},{8,7},{9,8},{10,9},{11,1... | collective-permute-start | bytes 25352 | tf_op jit(solution)/shard_map/ppermute | solution.py:589
  25.0 31.3 %collective-permute-start.7 = (bf16[5,96,512]{2,1,0:T(8,128)(2,1)}, bf16[5,96,512]{2,1,0:T(8,128)(2,1)}, u32[]{:S(2)}, u32[]{:S(2)}) collective-permute-start(bf16[5,96,512]{2,1,0:T(8,128)(2,1)} %get-tuple-element.54), channel_id=1, source_target_pairs={{0,32},{32,64},{64,96},{96,128},{128,160},{160,192},{192,224},{1,3... | collective-permute-start | bytes 1474568 | tf_op jit(solution)/shard_map/ppermute | solution.py:593
  37.1 19.3 %collective-permute-start.6 = (bf16[5,96,640]{2,1,0:T(8,128)(2,1)S(1)}, bf16[5,96,640]{2,1,0:T(8,128)(2,1)S(1)}, u32[]{:S(2)}, u32[]{:S(2)}) collective-permute-start(bf16[5,96,640]{2,1,0:T(8,128)(2,1)S(1)} %copy-done.2), channel_id=1, source_target_pairs={{0,32},{32,64},{64,96},{96,128},{128,160},{160,192},{192,224},{1,3... | collective-permute-start | bytes 1843208 | tf_op jit(solution)/shard_map/ppermute | solution.py:592
  41.9 0.8 copy-start.3
  41.9 1.2 %copy-start.1 = (bf16[9,96,640]{2,1,0:T(8,128)(2,1)}, bf16[9,96,640]{2,1,0:T(8,128)(2,1)S(1)}, u32[]{:S(2)}) copy-start(bf16[9,96,640]{2,1,0:T(8,128)(2,1)S(1)} %collective-permute-done.2.high_y) | copy-start | bytes 3317764
  56.4 1.3 %copy-start.4 = (bf16[5,96,640]{2,1,0:T(8,128)(2,1)}, bf16[5,96,640]{2,1,0:T(8,128)(2,1)S(1)}, u32[]{:S(2)}) copy-start(bf16[5,96,640]{2,1,0:T(8,128)(2,1)S(1)} %collective-permute-done.6.refs_4_) | copy-start | bytes 1843204
  56.4 6.6 %collective-permute-start.8 = (bf16[5,96,640]{2,1,0:T(8,128)(2,1)S(1)}, bf16[5,96,640]{2,1,0:T(8,128)(2,1)S(1)}, u32[]{:S(2)}, u32[]{:S(2)}) collective-permute-start(bf16[5,96,640]{2,1,0:T(8,128)(2,1)S(1)} %collective-permute-done.6.refs_4_), channel_id=1, source_target_pairs={{0,1},{2,3},{4,5},{6,7},{8,9},{10,11},{12,13},{14,15},{16,17},{18,... | collective-permute-start | bytes 1843208 | tf_op jit(solution)/shard_map/ppermute | solution.py:600
  63.0 0.8 copy-start.5
  68.0 6.7 %collective-permute-start.9 = (s16[144,128]{1,0:T(8,128)(2,1)}, s16[144,128]{1,0:T(8,128)(2,1)S(1)}, u32[]{:S(2)}, u32[]{:S(2)}) collective-permute-start(s16[144,128]{1,0:T(8,128)(2,1)} %get-tuple-element.68), channel_id=1, source_target_pairs={{32,0},{64,32},{96,64},{128,96},{160,128},{192,160},{224,192},{33,... | collective-permute-start | bytes 110600 | tf_op jit(solution)/shard_map/ppermute | solution.py:604
  75.6 8.0 %collective-permute-start.12 = (s16[272,128]{1,0:T(8,128)(2,1)S(1)}, s16[272,128]{1,0:T(8,128)(2,1)S(1)}, u32[]{:S(2)}, u32[]{:S(2)}) collective-permute-start(s16[272,128]{1,0:T(8,128)(2,1)S(1)} %pad_add_fusion.1), channel_id=1, source_target_pairs={{6,0},{7,1},{0,2},{1,3},{2,4},{3,5},{4,6},{5,7},{14,8},{15,9},{8,1... | collective-permute-start | bytes 208904 | tf_op jit(solution)/shard_map/ppermute | solution.py:615
  80.2 9.1 %collective-permute-start.11 = (s16[272,128]{1,0:T(8,128)(2,1)S(1)}, s16[272,128]{1,0:T(8,128)(2,1)S(1)}, u32[]{:S(2)}, u32[]{:S(2)}) collective-permute-start(s16[272,128]{1,0:T(8,128)(2,1)S(1)} %pad_add_fusion.1), channel_id=1, source_target_pairs={{4,0},{5,1},{6,2},{7,3},{0,4},{1,5},{2,6},{3,7},{12,8},{13,9},{14,... | collective-permute-start | bytes 208904 | tf_op jit(solution)/shard_map/ppermute | solution.py:615
  81.1 8.2 %collective-permute-start.10 = (s16[272,128]{1,0:T(8,128)(2,1)S(1)}, s16[272,128]{1,0:T(8,128)(2,1)S(1)}, u32[]{:S(2)}, u32[]{:S(2)}) collective-permute-start(s16[272,128]{1,0:T(8,128)(2,1)S(1)} %pad_add_fusion.1), channel_id=1, source_target_pairs={{2,0},{3,1},{4,2},{5,3},{6,4},{7,5},{0,6},{1,7},{10,8},{11,9},{12,... | collective-permute-start | bytes 208904 | tf_op jit(solution)/shard_map/ppermute | solution.py:615
  89.3 7.6 %collective-permute-start.15 = (s16[4,272,128]{2,1,0:T(8,128)(2,1)S(1)}, s16[4,272,128]{2,1,0:T(8,128)(2,1)S(1)}, u32[]{:S(2)}, u32[]{:S(2)}) collective-permute-start(s16[4,272,128]{2,1,0:T(8,128)(2,1)S(1)} %pad_add_fusion.refs_0_), channel_id=1, source_target_pairs={{24,0},{25,1},{26,2},{27,3},{28,4},{29,5},{30,6},{31,7},{0,8},{1,9... | collective-permute-start | bytes 835592 | tf_op jit(solution)/shard_map/ppermute | solution.py:615
  90.7 8.9 %collective-permute-start.14 = (s16[4,272,128]{2,1,0:T(8,128)(2,1)S(1)}, s16[4,272,128]{2,1,0:T(8,128)(2,1)S(1)}, u32[]{:S(2)}, u32[]{:S(2)}) collective-permute-start(s16[4,272,128]{2,1,0:T(8,128)(2,1)S(1)} %pad_add_fusion.refs_0_), channel_id=1, source_target_pairs={{16,0},{17,1},{18,2},{19,3},{20,4},{21,5},{22,6},{23,7},{24,8},{25... | collective-permute-start | bytes 835592 | tf_op jit(solution)/shard_map/ppermute | solution.py:615
  91.7 13.9 %collective-permute-start.13 = (s16[4,272,128]{2,1,0:T(8,128)(2,1)S(1)}, s16[4,272,128]{2,1,0:T(8,128)(2,1)S(1)}, u32[]{:S(2)}, u32[]{:S(2)}) collective-permute-start(s16[4,272,128]{2,1,0:T(8,128)(2,1)S(1)} %pad_add_fusion.refs_0_), channel_id=1, source_target_pairs={{8,0},{9,1},{10,2},{11,3},{12,4},{13,5},{14,6},{15,7},{16,8},{17,9... | collective-permute-start | bytes 835592 | tf_op jit(solution)/shard_map/ppermute | solution.py:615
  93.6 13.2 %collective-permute-start.16 = (s16[4,272,128]{2,1,0:T(8,128)(2,1)S(1)}, s16[4,272,128]{2,1,0:T(8,128)(2,1)S(1)}, u32[]{:S(2)}, u32[]{:S(2)}) collective-permute-start(s16[4,272,128]{2,1,0:T(8,128)(2,1)S(1)} %pad_add_fusion.refs_0_), channel_id=1, source_target_pairs={{1,0},{0,1},{3,2},{2,3},{5,4},{4,5},{7,6},{6,7},{9,8},{8,9},{11,10... | collective-permute-start | bytes 835592 | tf_op jit(solution)/shard_map/ppermute | solution.py:619
  96.9 9.9 %collective-permute-start.19 = (s16[4,272,128]{2,1,0:T(8,128)(2,1)S(1)}, s16[4,272,128]{2,1,0:T(8,128)(2,1)S(1)}, u32[]{:S(2)}, u32[]{:S(2)}) collective-permute-start(s16[4,272,128]{2,1,0:T(8,128)(2,1)S(1)} %collective-permute-done.15.refs_3_), channel_id=1, source_target_pairs={{1,0},{0,1},{3,2},{2,3},{5,4},{4,5},{7,6},{6,7},{9,8},{8,9},{11,10... | collective-permute-start | bytes 835592 | tf_op jit(solution)/shard_map/ppermute | solution.py:619
  99.7 7.1 %collective-permute-start.18 = (s16[4,272,128]{2,1,0:T(8,128)(2,1)S(1)}, s16[4,272,128]{2,1,0:T(8,128)(2,1)S(1)}, u32[]{:S(2)}, u32[]{:S(2)}) collective-permute-start(s16[4,272,128]{2,1,0:T(8,128)(2,1)S(1)} %collective-permute-done.14.refs_2_), channel_id=1, source_target_pairs={{1,0},{0,1},{3,2},{2,3},{5,4},{4,5},{7,6},{6,7},{9,8},{8,9},{11,10... | collective-permute-start | bytes 835592 | tf_op jit(solution)/shard_map/ppermute | solution.py:619
  105.6 2.3 %collective-permute-start.17 = (s16[4,272,128]{2,1,0:T(8,128)(2,1)S(1)}, s16[4,272,128]{2,1,0:T(8,128)(2,1)S(1)}, u32[]{:S(2)}, u32[]{:S(2)}) collective-permute-start(s16[4,272,128]{2,1,0:T(8,128)(2,1)S(1)} %collective-permute-done.13.refs_1_), channel_id=1, source_target_pairs={{1,0},{0,1},{3,2},{2,3},{5,4},{4,5},{7,6},{6,7},{9,8},{8,9},{11,10... | collective-permute-start | bytes 835592 | tf_op jit(solution)/shard_map/ppermute | solution.py:619

commit v5 on v4

--- a/solution.py
+++ b/solution.py
@@ -319,9 +319,10 @@
     return jnp.concatenate(third, axis=1).astype(jnp.bfloat16)
 
 
-def bring(sources, slots, sems):
+def bring(sources, slots, sems, begin=(0,) * 6):
     def copy(n, a):
-        return pltpu.make_async_copy(sources[n].at[a], slots[n].at[a], sems.at[n, a])
+        source = sources[n].at[a, :, pl.ds(begin[n], slots[n].shape[2])]
+        return pltpu.make_async_copy(source, slots[n].at[a], sems.at[n, a])
 
     def start(which=None):
         for a in range(STRIP):
@@ -385,13 +386,13 @@
     )(applied01, applied2a, side01, side2, low_a, low_b)
 
 
-CORNER = ((2 * VEC, FRAME - 1), (2 * VEC, 3), (ROWS, STRIP))
+CORNER = ((2 * VEC, STRIP), (2 * VEC, 3), (ROWS, STRIP))
 
 
 def corner_kernel(meta, *refs):
     sources, coded, (mine, theirs), slots, (sems, block) = refs[:3], refs[3:9], refs[9:11], refs[11:14], refs[14:]
     far_block, first_tile, first_level, second_tile, second_turned, second_level = coded
-    start, wait = bring(sources, slots, sems)
+    start, wait = bring(sources, slots, sems, (FIRST * L, 0, 0))
     applied01, applied2b, partner = slots
 
     @pl.when(meta[0] == 1)
@@ -400,7 +401,7 @@
         parts = []
         for a in range(STRIP):
             wait(a)
-            parts.append(dot(applied01[a, :, FIRST * L :], partner[a, :VEC]))
+            parts.append(dot(applied01[a], partner[a, :VEC]))
             parts.append(dot(applied2b[a], thirds_of(partner, a, STRIP)))
         block[...] = total(sum(parts))
 

time: 116 us -> 116 us (level)
  no operation moved by 1% of the time
where the time goes in v5:
time: 116 us; the launch traced here: 113 us
  starting transfers between devices  53.9 us (46%)
  Pallas kernels  30.5 us (26%)
  waiting for transfers between devices  23.3 us (20%)
  local copies, waits for them, and re-layouts  2.84 us (2%)
  other arithmetic  1.77 us (2%)
    pallas_call x1, Pallas kernels, own(): pl.pallas_call(own_kernel, out_shape=[jax.ShapeDtypeStruct(half(width), j...  13.2 us
    ppermute x6, starting transfers between devices, everyone(): lax.ppermute(x, 'sy', ring(n * d_y, n * d_z, 0))  12.2 us
    ppermute x6, waiting for transfers between devices, everyone(): lax.ppermute(x, 'sy', ring(n * d_y, n * d_z, 0))  10.3 us
    ppermute x4, starting transfers between devices, body(): there = [lax.ppermute(part, 'sy', ring(0, 0, 1)) for part in here]  8.54 us
    ppermute x1, starting transfers between devices, body(): high_y = lax.ppermute(strip, both, sides)  7.06 us
    ppermute x1, waiting for transfers between devices, body(): lax.ppermute(left, 'sy', [(target, source) for source, target in along])  5.77 us
    pallas_call x1, Pallas kernels, decode(): pl.pallas_call(functools.partial(decode_kernel, columns=columns), in_spec...  5.38 us
    ppermute x1, starting transfers between devices, body(): got = lax.ppermute(theirs, 'sx', [(r + 1, r) for r in range(rows - 1)])  4.88 us
  transfers between devices with their start and end apart: 20, of which 8 were waited for; matrix products, arithmetic and copies ran while one was open for 1% of the time, Pallas kernels for 19%

profile of v5, /device:TPU:11, one launch (start us, length us, event | category | flops | bytes accessed | tf_op | source)
XLA Modules:
  0.0 113.4 jit_solution(15443705103814968823)
XLA Ops:
  0.8 3.5 %collective-permute-start.1 = (f32[3,5,64]{2,1,0:T(8,128)S(1)}, f32[3,5,64]{2,1,0:T(8,128)S(1)}, u32[]{:S(2)}, u32[]{:S(2)}) collective-permute-start(f32[3,5,64]{2,1,0:T(8,128)S(1)} %get-tuple-element.69), channel_id=1, source_target_pairs={{32,0},{64,32},{96,64},{128,96},{160,128},{192,160},{224,192},{33,... | collective-permute-start | bytes 11528 | tf_op jit(solution)/shard_map/ppermute | solution.py:565
  4.3 1.9 %collective-permute-start = (f32[3,5,64]{2,1,0:T(8,128)S(1)}, f32[3,5,64]{2,1,0:T(8,128)S(1)}, u32[]{:S(2)}, u32[]{:S(2)}) collective-permute-start(f32[3,5,64]{2,1,0:T(8,128)S(1)} %get-tuple-element.70), channel_id=1, source_target_pairs={{0,32},{32,64},{64,96},{96,128},{128,160},{160,192},{192,224},{1,3... | collective-permute-start | bytes 11528 | tf_op jit(solution)/shard_map/ppermute | solution.py:564
  6.9 3.6 %pack.1 = (bf16[9,96,1152]{2,1,0:T(8,128)(2,1)}, bf16[9,96,640]{2,1,0:T(8,128)(2,1)}, bf16[5,96,640]{2,1,0:T(8,128)(2,1)}, bf16[5,96,512]{2,1,0:T(8,128)(2,1)}) custom-call(s32[1,1]{1,0:T(1,128)S(6)} %copy.4.counts, bf16[3,9,9,64,64]{4,3,2,1,0:T(8,128)(2,1)} %bitcast.14), custom_call_target="tpu_custom_call" | custom-call | flops 4000000000 | bytes 9000000 | tf_op jit(solution)/shard_map/pack/pallas_call | solution.py:123
  11.3 7.1 %collective-permute-start.2 = (bf16[9,96,640]{2,1,0:T(8,128)(2,1)}, bf16[9,96,640]{2,1,0:T(8,128)(2,1)S(1)}, u32[]{:S(2)}, u32[]{:S(2)}) collective-permute-start(bf16[9,96,640]{2,1,0:T(8,128)(2,1)} %get-tuple-element.39), channel_id=1, source_target_pairs={{0,1},{1,2},{2,3},{3,4},{4,5},{5,6},{6,7},{7,8},{8,9},{9,10},{10,1... | collective-permute-start | bytes 3317768 | tf_op jit(solution)/shard_map/ppermute | solution.py:584
  18.4 2.1 %collective-permute-start.4 = (f32[11,3,64]{2,1,0:T(4,128)S(1)}, f32[11,3,64]{2,1,0:T(4,128)S(1)}, u32[]{:S(2)}, u32[]{:S(2)}) collective-permute-start(f32[11,3,64]{2,1,0:T(4,128)S(1)} %get-tuple-element.46), channel_id=1, source_target_pairs={{0,1},{1,2},{2,3},{3,4},{4,5},{5,6},{6,7},{7,8},{8,9},{9,10},{10,1... | collective-permute-start | bytes 25352 | tf_op jit(solution)/shard_map/ppermute | solution.py:589
  20.4 4.6 %collective-permute-start.5 = (f32[11,3,64]{2,1,0:T(4,128)S(1)}, f32[11,3,64]{2,1,0:T(4,128)S(1)}, u32[]{:S(2)}, u32[]{:S(2)}) collective-permute-start(f32[11,3,64]{2,1,0:T(4,128)S(1)} %get-tuple-element.47), channel_id=1, source_target_pairs={{1,0},{2,1},{3,2},{4,3},{5,4},{6,5},{7,6},{8,7},{9,8},{10,9},{11,1... | collective-permute-start | bytes 25352 | tf_op jit(solution)/shard_map/ppermute | solution.py:590
  25.0 3.1 %collective-permute-start.7 = (bf16[5,96,512]{2,1,0:T(8,128)(2,1)}, bf16[5,96,512]{2,1,0:T(8,128)(2,1)}, u32[]{:S(2)}, u32[]{:S(2)}) collective-permute-start(bf16[5,96,512]{2,1,0:T(8,128)(2,1)} %get-tuple-element.54), channel_id=1, source_target_pairs={{0,32},{32,64},{64,96},{96,128},{128,160},{160,192},{192,224},{1,3... | collective-permute-start | bytes 1474568 | tf_op jit(solution)/shard_map/ppermute | solution.py:594
  28.1 3.1 %collective-permute-done.4 = f32[11,3,64]{2,1,0:T(4,128)S(1)} collective-permute-done((f32[11,3,64]{2,1,0:T(4,128)S(1)}, f32[11,3,64]{2,1,0:T(4,128)S(1)}, u32[]{:S(2)}, u32[]{:S(2)}) %collective-permute-start.4) | collective-permute-done | bytes 8480 | tf_op jit(solution)/shard_map/ppermute | solution.py:589
  31.3 5.8 %collective-permute-done.5 = f32[11,3,64]{2,1,0:T(4,128)S(1)} collective-permute-done((f32[11,3,64]{2,1,0:T(4,128)S(1)}, f32[11,3,64]{2,1,0:T(4,128)S(1)}, u32[]{:S(2)}, u32[]{:S(2)}) %collective-permute-start.5) | collective-permute-done | bytes 8480 | tf_op jit(solution)/shard_map/ppermute | solution.py:590
  37.1 4.1 %collective-permute-start.6 = (bf16[5,96,640]{2,1,0:T(8,128)(2,1)S(1)}, bf16[5,96,640]{2,1,0:T(8,128)(2,1)S(1)}, u32[]{:S(2)}, u32[]{:S(2)}) collective-permute-start(bf16[5,96,640]{2,1,0:T(8,128)(2,1)S(1)} %copy-done.2), channel_id=1, source_target_pairs={{0,32},{32,64},{64,96},{96,128},{128,160},{160,192},{192,224},{1,3... | collective-permute-start | bytes 1843208 | tf_op jit(solution)/shard_map/ppermute | solution.py:593
  43.1 13.2 %own.1 = (bf16[5,128,1280]{2,1,0:T(8,128)(2,1)}, bf16[5,128,640]{2,1,0:T(8,128)(2,1)}, bf16[5,128,384]{2,1,0:T(8,128)(2,1)}, bf16[5,128,640]{2,1,0:T(8,128)(2,1)...) custom-call(bf16[9,96,1152]{2,1,0:T(8,128)(2,1)} %get-tuple-element.38.u, ...), custom_call_target="tpu_custom_call" | custom-call | flops 14000000000 | bytes 30000000 | tf_op jit(solution)/shard_map/own/pallas_call | solution.py:281
  56.4 1.3 %collective-permute-start.8 = (bf16[5,96,640]{2,1,0:T(8,128)(2,1)S(1)}, bf16[5,96,640]{2,1,0:T(8,128)(2,1)S(1)}, u32[]{:S(2)}, u32[]{:S(2)}) collective-permute-start(bf16[5,96,640]{2,1,0:T(8,128)(2,1)S(1)} %collective-permute-done.6.refs_4_), channel_id=1, source_target_pairs={{0,1},{2,3},{4,5},{6,7},{8,9},{10,11},{12,13},{14,15},{16,17},{18,... | collective-permute-start | bytes 1843208 | tf_op jit(solution)/shard_map/ppermute | solution.py:601
  57.7 4.2 %below.1 = (s16[64,128]{1,0:T(8,128)(2,1)}, s16[64,128]{1,0:T(8,128)(2,1)}, f32[8,128]{1,0:T(8,128)}) custom-call(bf16[5,128,1280]{2,1,0:T(8,128)(2,1)} %get-tuple-element.51.refs_0_, bf16[5,128,640]{2,1,0:T(8,128)(2,1)} %get-tuple-element.60.refs_1_, bf16[5,128,640]{2,1,0:T(8,128)(2,1)} %get-tuple-element.61.refs_2_, ...), custom_call_target="tpu_custom_call" | custom-call | flops 2000000000 | bytes 6000000 | tf_op jit(solution)/shard_map/below/pallas_call | solution.py:378
  61.9 1.1 %collective-permute-done.8.refs_2_ = bf16[5,96,640]{2,1,0:T(8,128)(2,1)S(1)} collective-permute-done((bf16[5,96,640]{2,1,0:T(8,128)(2,1)S(1)}, bf16[5,96,640]{2,1,0:T(8,128)(2,1)S(1)}, u32[]{:S(2)}, u32[]{:S(2)}) %collective-permute-start.8) | collective-permute-done | bytes 614432 | tf_op jit(solution)/shard_map/ppermute | solution.py:601
  63.8 4.1 %corner.1 = (s16[272,128]{1,0:T(8,128)(2,1)}, s16[144,128]{1,0:T(8,128)(2,1)}) custom-call(s32[1]{0:T(128)} %bitcast.4.meta, bf16[5,128,1280]{2,1,0:T(8,128)(2,1)} %get-tuple-element.51.refs_0_, bf16[5,128,384]{2,1,0:T(8,128)(2,1)} %get-tuple-element.52.refs_1_, bf16[5,96,640]{2,1,0:T(8,128)(2,1)} %copy-done.5, f32[64,64]{1,0:T(8,128)} %get-tuple-element.57.refs_3_, ...), custom_call_target="tpu_custom_call" | custom-call | flops 1500000000 | bytes 5000000 | tf_op jit(solution)/shard_map/corner/pallas_call | solution.py:434
  68.0 4.9 %collective-permute-start.9 = (s16[144,128]{1,0:T(8,128)(2,1)}, s16[144,128]{1,0:T(8,128)(2,1)S(1)}, u32[]{:S(2)}, u32[]{:S(2)}) collective-permute-start(s16[144,128]{1,0:T(8,128)(2,1)} %get-tuple-element.68), channel_id=1, source_target_pairs={{32,0},{64,32},{96,64},{128,96},{160,128},{192,160},{224,192},{33,... | collective-permute-start | bytes 110600 | tf_op jit(solution)/shard_map/ppermute | solution.py:605
  72.8 1.9 %collective-permute-done.9 = s16[144,128]{1,0:T(8,128)(2,1)S(1)} collective-permute-done((s16[144,128]{1,0:T(8,128)(2,1)}, s16[144,128]{1,0:T(8,128)(2,1)S(1)}, u32[]{:S(2)}, u32[]{:S(2)}) %collective-permute-start.9) | collective-permute-done | bytes 36896 | tf_op jit(solution)/shard_map/ppermute | solution.py:605
  75.6 4.6 %collective-permute-start.12 = (s16[272,128]{1,0:T(8,128)(2,1)S(1)}, s16[272,128]{1,0:T(8,128)(2,1)S(1)}, u32[]{:S(2)}, u32[]{:S(2)}) collective-permute-start(s16[272,128]{1,0:T(8,128)(2,1)S(1)} %pad_add_fusion.1), channel_id=1, source_target_pairs={{6,0},{7,1},{0,2},{1,3},{2,4},{3,5},{4,6},{5,7},{14,8},{15,9},{8,1... | collective-permute-start | bytes 208904 | tf_op jit(solution)/shard_map/ppermute | solution.py:616
  80.2 0.9 collective-permute-start.11
  81.1 2.5 %collective-permute-start.10 = (s16[272,128]{1,0:T(8,128)(2,1)S(1)}, s16[272,128]{1,0:T(8,128)(2,1)S(1)}, u32[]{:S(2)}, u32[]{:S(2)}) collective-permute-start(s16[272,128]{1,0:T(8,128)(2,1)S(1)} %pad_add_fusion.1), channel_id=1, source_target_pairs={{2,0},{3,1},{4,2},{5,3},{6,4},{7,5},{0,6},{1,7},{10,8},{11,9},{12,... | collective-permute-start | bytes 208904 | tf_op jit(solution)/shard_map/ppermute | solution.py:616
  83.6 5.7 %collective-permute-done.11 = s16[272,128]{1,0:T(8,128)(2,1)S(1)} collective-permute-done((s16[272,128]{1,0:T(8,128)(2,1)S(1)}, s16[272,128]{1,0:T(8,128)(2,1)S(1)}, u32[]{:S(2)}, u32[]{:S(2)}) %collective-permute-start.11) | collective-permute-done | bytes 69664 | tf_op jit(solution)/shard_map/ppermute | solution.py:616
  89.3 1.4 %collective-permute-start.15 = (s16[4,272,128]{2,1,0:T(8,128)(2,1)S(1)}, s16[4,272,128]{2,1,0:T(8,128)(2,1)S(1)}, u32[]{:S(2)}, u32[]{:S(2)}) collective-permute-start(s16[4,272,128]{2,1,0:T(8,128)(2,1)S(1)} %pad_add_fusion.refs_0_), channel_id=1, source_target_pairs={{24,0},{25,1},{26,2},{27,3},{28,4},{29,5},{30,6},{31,7},{0,8},{1,9... | collective-permute-start | bytes 835592 | tf_op jit(solution)/shard_map/ppermute | solution.py:616
  90.7 0.9 collective-permute-start.14
  91.6 1.9 %collective-permute-start.13 = (s16[4,272,128]{2,1,0:T(8,128)(2,1)S(1)}, s16[4,272,128]{2,1,0:T(8,128)(2,1)S(1)}, u32[]{:S(2)}, u32[]{:S(2)}) collective-permute-start(s16[4,272,128]{2,1,0:T(8,128)(2,1)S(1)} %pad_add_fusion.refs_0_), channel_id=1, source_target_pairs={{8,0},{9,1},{10,2},{11,3},{12,4},{13,5},{14,6},{15,7},{16,8},{17,9... | collective-permute-start | bytes 835592 | tf_op jit(solution)/shard_map/ppermute | solution.py:616
  93.6 1.5 %collective-permute-start.16 = (s16[4,272,128]{2,1,0:T(8,128)(2,1)S(1)}, s16[4,272,128]{2,1,0:T(8,128)(2,1)S(1)}, u32[]{:S(2)}, u32[]{:S(2)}) collective-permute-start(s16[4,272,128]{2,1,0:T(8,128)(2,1)S(1)} %pad_add_fusion.refs_0_), channel_id=1, source_target_pairs={{1,0},{0,1},{3,2},{2,3},{5,4},{4,5},{7,6},{6,7},{9,8},{8,9},{11,10... | collective-permute-start | bytes 835592 | tf_op jit(solution)/shard_map/ppermute | solution.py:620
  95.1 1.8 %collective-permute-done.15.refs_3_ = s16[4,272,128]{2,1,0:T(8,128)(2,1)S(1)} collective-permute-done((s16[4,272,128]{2,1,0:T(8,128)(2,1)S(1)}, s16[4,272,128]{2,1,0:T(8,128)(2,1)S(1)}, u32[]{:S(2)}, u32[]{:S(2)}) %collective-permute-start.15) | collective-permute-done | bytes 278560 | tf_op jit(solution)/shard_map/ppermute | solution.py:616
  96.9 2.7 %collective-permute-start.19 = (s16[4,272,128]{2,1,0:T(8,128)(2,1)S(1)}, s16[4,272,128]{2,1,0:T(8,128)(2,1)S(1)}, u32[]{:S(2)}, u32[]{:S(2)}) collective-permute-start(s16[4,272,128]{2,1,0:T(8,128)(2,1)S(1)} %collective-permute-done.15.refs_3_), channel_id=1, source_target_pairs={{1,0},{0,1},{3,2},{2,3},{5,4},{4,5},{7,6},{6,7},{9,8},{8,9},{11,10... | collective-permute-start | bytes 835592 | tf_op jit(solution)/shard_map/ppermute | solution.py:620
  99.6 3.1 %collective-permute-start.18 = (s16[4,272,128]{2,1,0:T(8,128)(2,1)S(1)}, s16[4,272,128]{2,1,0:T(8,128)(2,1)S(1)}, u32[]{:S(2)}, u32[]{:S(2)}) collective-permute-start(s16[4,272,128]{2,1,0:T(8,128)(2,1)S(1)} %collective-permute-done.14.refs_2_), channel_id=1, source_target_pairs={{1,0},{0,1},{3,2},{2,3},{5,4},{4,5},{7,6},{6,7},{9,8},{8,9},{11,10... | collective-permute-start | bytes 835592 | tf_op jit(solution)/shard_map/ppermute | solution.py:620
  102.8 2.7 %collective-permute-done.13.refs_1_ = s16[4,272,128]{2,1,0:T(8,128)(2,1)S(1)} collective-permute-done((s16[4,272,128]{2,1,0:T(8,128)(2,1)S(1)}, s16[4,272,128]{2,1,0:T(8,128)(2,1)S(1)}, u32[]{:S(2)}, u32[]{:S(2)}) %collective-permute-start.13) | collective-permute-done | bytes 278560 | tf_op jit(solution)/shard_map/ppermute | solution.py:616
  105.5 1.2 %collective-permute-start.17 = (s16[4,272,128]{2,1,0:T(8,128)(2,1)S(1)}, s16[4,272,128]{2,1,0:T(8,128)(2,1)S(1)}, u32[]{:S(2)}, u32[]{:S(2)}) collective-permute-start(s16[4,272,128]{2,1,0:T(8,128)(2,1)S(1)} %collective-permute-done.13.refs_1_), channel_id=1, source_target_pairs={{1,0},{0,1},{3,2},{2,3},{5,4},{4,5},{7,6},{6,7},{9,8},{8,9},{11,10... | collective-permute-start | bytes 835592 | tf_op jit(solution)/shard_map/ppermute | solution.py:620
  106.8 1.1 collective-permute-done.17.refs_5_
  107.9 5.4 %decode.1 = f32[1,32,9,64,64]{4,3,2,1,0:T(8,128)} custom-call(s32[4]{0:T(128)S(1)} %pad_add_fusion.2.meta, s16[4,272,128]{2,1,0:T(8,128)(2,1)S(1)} %pad_add_fusion.refs_0_, s16[4,272,128]{2,1,0:T(8,128)(2,1)S(1)} %collective-permute-done.13.refs_1_, s16[4,272,128]{2,1,0:T(8,128)(2,1)S(1)} %collective-permute-done.14.refs_2_, ...), custom_call_target="tpu_custom_call" | custom-call | flops 10000000 | bytes 12000000 | tf_op jit(solution)/shard_map/decode/pallas_call | solution.py:522
  (34 shorter events, 5.4 us)
Async XLA Ops:
  0.8 17.5 %collective-permute-start.1 = (f32[3,5,64]{2,1,0:T(8,128)S(1)}, f32[3,5,64]{2,1,0:T(8,128)S(1)}, u32[]{:S(2)}, u32[]{:S(2)}) collective-permute-start(f32[3,5,64]{2,1,0:T(8,128)S(1)} %get-tuple-element.69), channel_id=1, source_target_pairs={{32,0},{64,32},{96,64},{128,96},{160,128},{192,160},{224,192},{33,... | collective-permute-start | bytes 11528 | tf_op jit(solution)/shard_map/ppermute | solution.py:565
  4.3 14.0 %collective-permute-start = (f32[3,5,64]{2,1,0:T(8,128)S(1)}, f32[3,5,64]{2,1,0:T(8,128)S(1)}, u32[]{:S(2)}, u32[]{:S(2)}) collective-permute-start(f32[3,5,64]{2,1,0:T(8,128)S(1)} %get-tuple-element.70), channel_id=1, source_target_pairs={{0,32},{32,64},{64,96},{96,128},{128,160},{160,192},{192,224},{1,3... | collective-permute-start | bytes 11528 | tf_op jit(solution)/shard_map/ppermute | solution.py:564
  6.9 11.4 %copy-start = (f32[5,5,64]{2,1,0:T(8,128)S(1)}, f32[5,5,64]{2,1,0:T(8,128)}, u32[]{:S(2)}) copy-start(f32[5,5,64]{2,1,0:T(8,128)} %middle.1) | copy-start | bytes 19204
  10.6 31.4 %collective-permute-start.3 = (bf16[5,96,640]{2,1,0:T(8,128)(2,1)}, bf16[5,96,640]{2,1,0:T(8,128)(2,1)S(1)}, u32[]{:S(2)}, u32[]{:S(2)}) collective-permute-start(bf16[5,96,640]{2,1,0:T(8,128)(2,1)} %get-tuple-element.53), channel_id=1, source_target_pairs={{2,33},{4,35},{6,37},{8,39},{10,41},{12,43},{14,45},{16,47},{18,49... | collective-permute-start | bytes 1843208 | tf_op jit(solution)/shard_map/ppermute | solution.py:585
  11.3 30.7 %collective-permute-start.2 = (bf16[9,96,640]{2,1,0:T(8,128)(2,1)}, bf16[9,96,640]{2,1,0:T(8,128)(2,1)S(1)}, u32[]{:S(2)}, u32[]{:S(2)}) collective-permute-start(bf16[9,96,640]{2,1,0:T(8,128)(2,1)} %get-tuple-element.39), channel_id=1, source_target_pairs={{0,1},{1,2},{2,3},{3,4},{4,5},{5,6},{6,7},{7,8},{8,9},{9,10},{10,1... | collective-permute-start | bytes 3317768 | tf_op jit(solution)/shard_map/ppermute | solution.py:584
  18.4 18.7 %copy-start.2 = (bf16[5,96,640]{2,1,0:T(8,128)(2,1)S(1)}, bf16[5,96,640]{2,1,0:T(8,128)(2,1)}, u32[]{:S(2)}) copy-start(bf16[5,96,640]{2,1,0:T(8,128)(2,1)} %get-tuple-element.53) | copy-start | bytes 1843204
  18.4 12.9 %collective-permute-start.4 = (f32[11,3,64]{2,1,0:T(4,128)S(1)}, f32[11,3,64]{2,1,0:T(4,128)S(1)}, u32[]{:S(2)}, u32[]{:S(2)}) collective-permute-start(f32[11,3,64]{2,1,0:T(4,128)S(1)} %get-tuple-element.46), channel_id=1, source_target_pairs={{0,1},{1,2},{2,3},{3,4},{4,5},{5,6},{6,7},{7,8},{8,9},{9,10},{10,1... | collective-permute-start | bytes 25352 | tf_op jit(solution)/shard_map/ppermute | solution.py:589
  20.4 16.6 %collective-permute-start.5 = (f32[11,3,64]{2,1,0:T(4,128)S(1)}, f32[11,3,64]{2,1,0:T(4,128)S(1)}, u32[]{:S(2)}, u32[]{:S(2)}) collective-permute-start(f32[11,3,64]{2,1,0:T(4,128)S(1)} %get-tuple-element.47), channel_id=1, source_target_pairs={{1,0},{2,1},{3,2},{4,3},{5,4},{6,5},{7,6},{8,7},{9,8},{10,9},{11,1... | collective-permute-start | bytes 25352 | tf_op jit(solution)/shard_map/ppermute | solution.py:590
  25.0 31.3 %collective-permute-start.7 = (bf16[5,96,512]{2,1,0:T(8,128)(2,1)}, bf16[5,96,512]{2,1,0:T(8,128)(2,1)}, u32[]{:S(2)}, u32[]{:S(2)}) collective-permute-start(bf16[5,96,512]{2,1,0:T(8,128)(2,1)} %get-tuple-element.54), channel_id=1, source_target_pairs={{0,32},{32,64},{64,96},{96,128},{128,160},{160,192},{192,224},{1,3... | collective-permute-start | bytes 1474568 | tf_op jit(solution)/shard_map/ppermute | solution.py:594
  37.1 19.3 %collective-permute-start.6 = (bf16[5,96,640]{2,1,0:T(8,128)(2,1)S(1)}, bf16[5,96,640]{2,1,0:T(8,128)(2,1)S(1)}, u32[]{:S(2)}, u32[]{:S(2)}) collective-permute-start(bf16[5,96,640]{2,1,0:T(8,128)(2,1)S(1)} %copy-done.2), channel_id=1, source_target_pairs={{0,32},{32,64},{64,96},{96,128},{128,160},{160,192},{192,224},{1,3... | collective-permute-start | bytes 1843208 | tf_op jit(solution)/shard_map/ppermute | solution.py:593
  41.9 0.8 copy-start.3
  41.9 1.2 %copy-start.1 = (bf16[9,96,640]{2,1,0:T(8,128)(2,1)}, bf16[9,96,640]{2,1,0:T(8,128)(2,1)S(1)}, u32[]{:S(2)}) copy-start(bf16[9,96,640]{2,1,0:T(8,128)(2,1)S(1)} %collective-permute-done.2.high_y) | copy-start | bytes 3317764
  56.4 1.3 %copy-start.4 = (bf16[5,96,640]{2,1,0:T(8,128)(2,1)}, bf16[5,96,640]{2,1,0:T(8,128)(2,1)S(1)}, u32[]{:S(2)}) copy-start(bf16[5,96,640]{2,1,0:T(8,128)(2,1)S(1)} %collective-permute-done.6.refs_4_) | copy-start | bytes 1843204
  56.4 6.6 %collective-permute-start.8 = (bf16[5,96,640]{2,1,0:T(8,128)(2,1)S(1)}, bf16[5,96,640]{2,1,0:T(8,128)(2,1)S(1)}, u32[]{:S(2)}, u32[]{:S(2)}) collective-permute-start(bf16[5,96,640]{2,1,0:T(8,128)(2,1)S(1)} %collective-permute-done.6.refs_4_), channel_id=1, source_target_pairs={{0,1},{2,3},{4,5},{6,7},{8,9},{10,11},{12,13},{14,15},{16,17},{18,... | collective-permute-start | bytes 1843208 | tf_op jit(solution)/shard_map/ppermute | solution.py:601
  63.0 0.8 copy-start.5
  68.0 6.8 %collective-permute-start.9 = (s16[144,128]{1,0:T(8,128)(2,1)}, s16[144,128]{1,0:T(8,128)(2,1)S(1)}, u32[]{:S(2)}, u32[]{:S(2)}) collective-permute-start(s16[144,128]{1,0:T(8,128)(2,1)} %get-tuple-element.68), channel_id=1, source_target_pairs={{32,0},{64,32},{96,64},{128,96},{160,128},{192,160},{224,192},{33,... | collective-permute-start | bytes 110600 | tf_op jit(solution)/shard_map/ppermute | solution.py:605
  75.6 7.9 %collective-permute-start.12 = (s16[272,128]{1,0:T(8,128)(2,1)S(1)}, s16[272,128]{1,0:T(8,128)(2,1)S(1)}, u32[]{:S(2)}, u32[]{:S(2)}) collective-permute-start(s16[272,128]{1,0:T(8,128)(2,1)S(1)} %pad_add_fusion.1), channel_id=1, source_target_pairs={{6,0},{7,1},{0,2},{1,3},{2,4},{3,5},{4,6},{5,7},{14,8},{15,9},{8,1... | collective-permute-start | bytes 208904 | tf_op jit(solution)/shard_map/ppermute | solution.py:616
  80.2 9.1 %collective-permute-start.11 = (s16[272,128]{1,0:T(8,128)(2,1)S(1)}, s16[272,128]{1,0:T(8,128)(2,1)S(1)}, u32[]{:S(2)}, u32[]{:S(2)}) collective-permute-start(s16[272,128]{1,0:T(8,128)(2,1)S(1)} %pad_add_fusion.1), channel_id=1, source_target_pairs={{4,0},{5,1},{6,2},{7,3},{0,4},{1,5},{2,6},{3,7},{12,8},{13,9},{14,... | collective-permute-start | bytes 208904 | tf_op jit(solution)/shard_map/ppermute | solution.py:616
  81.1 8.2 %collective-permute-start.10 = (s16[272,128]{1,0:T(8,128)(2,1)S(1)}, s16[272,128]{1,0:T(8,128)(2,1)S(1)}, u32[]{:S(2)}, u32[]{:S(2)}) collective-permute-start(s16[272,128]{1,0:T(8,128)(2,1)S(1)} %pad_add_fusion.1), channel_id=1, source_target_pairs={{2,0},{3,1},{4,2},{5,3},{6,4},{7,5},{0,6},{1,7},{10,8},{11,9},{12,... | collective-permute-start | bytes 208904 | tf_op jit(solution)/shard_map/ppermute | solution.py:616
  89.3 7.6 %collective-permute-start.15 = (s16[4,272,128]{2,1,0:T(8,128)(2,1)S(1)}, s16[4,272,128]{2,1,0:T(8,128)(2,1)S(1)}, u32[]{:S(2)}, u32[]{:S(2)}) collective-permute-start(s16[4,272,128]{2,1,0:T(8,128)(2,1)S(1)} %pad_add_fusion.refs_0_), channel_id=1, source_target_pairs={{24,0},{25,1},{26,2},{27,3},{28,4},{29,5},{30,6},{31,7},{0,8},{1,9... | collective-permute-start | bytes 835592 | tf_op jit(solution)/shard_map/ppermute | solution.py:616
  90.7 8.9 %collective-permute-start.14 = (s16[4,272,128]{2,1,0:T(8,128)(2,1)S(1)}, s16[4,272,128]{2,1,0:T(8,128)(2,1)S(1)}, u32[]{:S(2)}, u32[]{:S(2)}) collective-permute-start(s16[4,272,128]{2,1,0:T(8,128)(2,1)S(1)} %pad_add_fusion.refs_0_), channel_id=1, source_target_pairs={{16,0},{17,1},{18,2},{19,3},{20,4},{21,5},{22,6},{23,7},{24,8},{25... | collective-permute-start | bytes 835592 | tf_op jit(solution)/shard_map/ppermute | solution.py:616
  91.6 13.9 %collective-permute-start.13 = (s16[4,272,128]{2,1,0:T(8,128)(2,1)S(1)}, s16[4,272,128]{2,1,0:T(8,128)(2,1)S(1)}, u32[]{:S(2)}, u32[]{:S(2)}) collective-permute-start(s16[4,272,128]{2,1,0:T(8,128)(2,1)S(1)} %pad_add_fusion.refs_0_), channel_id=1, source_target_pairs={{8,0},{9,1},{10,2},{11,3},{12,4},{13,5},{14,6},{15,7},{16,8},{17,9... | collective-permute-start | bytes 835592 | tf_op jit(solution)/shard_map/ppermute | solution.py:616
  93.6 13.2 %collective-permute-start.16 = (s16[4,272,128]{2,1,0:T(8,128)(2,1)S(1)}, s16[4,272,128]{2,1,0:T(8,128)(2,1)S(1)}, u32[]{:S(2)}, u32[]{:S(2)}) collective-permute-start(s16[4,272,128]{2,1,0:T(8,128)(2,1)S(1)} %pad_add_fusion.refs_0_), channel_id=1, source_target_pairs={{1,0},{0,1},{3,2},{2,3},{5,4},{4,5},{7,6},{6,7},{9,8},{8,9},{11,10... | collective-permute-start | bytes 835592 | tf_op jit(solution)/shard_map/ppermute | solution.py:620
  96.9 9.8 %collective-permute-start.19 = (s16[4,272,128]{2,1,0:T(8,128)(2,1)S(1)}, s16[4,272,128]{2,1,0:T(8,128)(2,1)S(1)}, u32[]{:S(2)}, u32[]{:S(2)}) collective-permute-start(s16[4,272,128]{2,1,0:T(8,128)(2,1)S(1)} %collective-permute-done.15.refs_3_), channel_id=1, source_target_pairs={{1,0},{0,1},{3,2},{2,3},{5,4},{4,5},{7,6},{6,7},{9,8},{8,9},{11,10... | collective-permute-start | bytes 835592 | tf_op jit(solution)/shard_map/ppermute | solution.py:620
  99.6 7.1 %collective-permute-start.18 = (s16[4,272,128]{2,1,0:T(8,128)(2,1)S(1)}, s16[4,272,128]{2,1,0:T(8,128)(2,1)S(1)}, u32[]{:S(2)}, u32[]{:S(2)}) collective-permute-start(s16[4,272,128]{2,1,0:T(8,128)(2,1)S(1)} %collective-permute-done.14.refs_2_), channel_id=1, source_target_pairs={{1,0},{0,1},{3,2},{2,3},{5,4},{4,5},{7,6},{6,7},{9,8},{8,9},{11,10... | collective-permute-start | bytes 835592 | tf_op jit(solution)/shard_map/ppermute | solution.py:620
  105.5 2.3 %collective-permute-start.17 = (s16[4,272,128]{2,1,0:T(8,128)(2,1)S(1)}, s16[4,272,128]{2,1,0:T(8,128)(2,1)S(1)}, u32[]{:S(2)}, u32[]{:S(2)}) collective-permute-start(s16[4,272,128]{2,1,0:T(8,128)(2,1)S(1)} %collective-permute-done.13.refs_1_), channel_id=1, source_target_pairs={{1,0},{0,1},{3,2},{2,3},{5,4},{4,5},{7,6},{6,7},{9,8},{8,9},{11,10... | collective-permute-start | bytes 835592 | tf_op jit(solution)/shard_map/ppermute | solution.py:620
